TPU v7x, 32 devices: a whole 2x2x4 slice. The times are simulated.
32 devices in a mesh: wide: 8 (over y, x, core), narrow: 4 (over z).
Axes of the slice: x: 2, y: 2, z: 4, core: 2. Of those that a mesh axis runs over, the one named last changes fastest.
Arguments:
- piece_table: bfloat16 [32768, 512], P(('wide', 'narrow')), may hold values from -6 to 6
- piece_ids: int32 [4096, 7], P(('wide', 'narrow')), may hold values from 0 to 32767, as said below
- slot_mask: int32 [4096, 7], P(('wide', 'narrow')), may hold values from 0 to 1, as said below
- text_ids: int32 [8, 1024], replicated, may hold values from 0 to 4095
- text_mask: int32 [8, 1024], replicated, may hold values 0 or 1
- text_cot: bfloat16 [4096, 8192], P(('wide', 'narrow'))
- mat_master: float32 [4, 2560, 512], P('narrow')
- mat_momentum: float32 [4, 2560, 512], P('narrow')
- mat_ema: float32 [4, 2560, 512], P('narrow')
- vec_master: float32 [14336], replicated
- vec_moment1: float32 [14336], replicated
- vec_moment2: float32 [14336], replicated, as said below
- vec_ema: float32 [14336], replicated
Outputs:
- text_embeds: float32 [4096, 8192], P(('wide', 'narrow'))
- piece_grad: float32 [32768, 512], P(('wide', 'narrow'))
- mat_grad: float32 [4, 2560, 512], P('narrow')
- mat_momentum_new: float32 [4, 2560, 512], P('narrow')
- mat_weight: float32 [4, 2560, 512], P('narrow')
- mat_ema_new: float32 [4, 2560, 512], P('narrow')
- vec_grad: float32 [14336], replicated
- vec_moment1_new: float32 [14336], replicated
- vec_moment2_new: float32 [14336], replicated
- vec_weight: float32 [14336], replicated
- vec_ema_new: float32 [14336], replicated
Inputs may be any that keep to these rules, and one draw needn't show every extreme that they name: `slot_mask`: the live piece slots of an entry are its first n slots, n from 1 to 7; the first entry of every block of 128 entries has all 7. `piece_ids`: call pieces j * 1024 to (j + 1) * 1024 - 1 group j. Of the 896 piece slots of each aligned block of 128 entries, at most 58 name pieces of any one group, and exactly 58 name pieces of some group. `vec_moment2`: every entry is positive.
All inputs are finite; a program needn't handle non-finite values.
Results may differ from a plain program's by a relative error of at most 0.0095.
Values may be sent and summed in bfloat16 or wider, within the bound.
A program may use at most 256 MiB of HBM per device.

v0:
```python
from functools import partial
import math

import jax
import jax.numpy as jnp
from jax import lax
from jax.sharding import PartitionSpec as P

D = 512
HEADS = 8
HDIM = 64
FF = 2048
OUTW = 4096
SLOTS = 8
PSLOTS = 7
STEP = 10


HIGHEST = lax.Precision.HIGHEST
MUON_RATE = 0.5
MUON_DECAY = 0.01
MUON_BETA = 0.95
ADAM_RATE = 0.5
ADAM_BETA1 = 0.9
ADAM_BETA2 = 0.95
ADAM_EPSILON = 1e-08
EMA_DECAY = 0.8
NEWTON_A = 3.4445
NEWTON_B = -4.775
NEWTON_C = 2.0315


def matrix_rows():
    return (3 * D, D, FF, FF, OUTW)


def unpack(packed, narrow_count):
    matrices = []
    offset = 0
    for row_total in matrix_rows():
        height = row_total // narrow_count
        matrices.append(packed[:, offset : offset + height, :].reshape(row_total, packed.shape[2]))
        offset = offset + height
    return matrices


def pack(matrices, narrow_count):
    return jnp.concatenate(
        [
            matrix.reshape(narrow_count, matrix.shape[0] // narrow_count, matrix.shape[1])
            for matrix in matrices
        ],
        axis=1,
    )


def block_slices(block, narrow_count):
    segments = []
    offset = 0
    for row_total in matrix_rows():
        height = row_total // narrow_count
        segments.append(block[offset : offset + height])
        offset = offset + height
    return segments


def split_vectors(vector):
    lengths = (D, SLOTS * D, D, D, D, D, D, D, FF, D, OUTW)
    chosen = []
    offset = 0
    for length in lengths:
        chosen.append(vector[offset : offset + length])
        offset = offset + length
    chosen[1] = chosen[1].reshape(SLOTS, D)
    return chosen


def layer_norm(values, gain, shift):
    center = values - jnp.mean(values, axis=-1, keepdims=True)
    spread = jnp.mean(center * center, axis=-1, keepdims=True)
    return center * lax.rsqrt(spread + 1e-05) * gain + shift


def gelu_tanh(values):
    return jax.nn.gelu(values, approximate=True)


def attend(query_rows, key_rows, value_rows, live_slots):
    entry_count = query_rows.shape[0]
    query_heads = query_rows.reshape(entry_count, HEADS, HDIM)
    key_heads = key_rows.reshape(entry_count, SLOTS, HEADS, HDIM)
    value_heads = value_rows.reshape(entry_count, SLOTS, HEADS, HDIM)
    scores = jnp.einsum("ehd,eshd->ehs", query_heads, key_heads, precision=HIGHEST) / math.sqrt(
        HDIM
    )
    scores = jnp.where(live_slots[:, None, :], scores, -1e30)
    scores = scores - jnp.max(scores, axis=-1, keepdims=True)
    expped = jnp.exp(scores)
    probabilities = expped / jnp.sum(expped, axis=-1, keepdims=True)
    mixed_heads = jnp.einsum("ehs,eshd->ehd", probabilities, value_heads, precision=HIGHEST)
    return mixed_heads.reshape(entry_count, D)


def contract_rows(left, right):
    return lax.dot_general(
        left, right, (((0,), (0,)), ((), ())), preferred_element_type=jnp.float32
    )


def gram_of(block):
    return lax.dot_general(block, block, (((0,), (0,)), ((), ())), precision=HIGHEST)


def newton_step(ortho_block, gram):
    poly = NEWTON_B * gram + NEWTON_C * jnp.dot(gram, gram, precision=HIGHEST)
    return NEWTON_A * ortho_block + jnp.dot(ortho_block, poly, precision=HIGHEST)


def on_device(
    piece_table,
    piece_ids,
    slot_mask,
    text_ids,
    text_mask,
    text_cot,
    mat_master,
    mat_momentum,
    mat_ema,
    vec_master,
    vec_moment1,
    vec_moment2,
    vec_ema,
):
    narrow_count = lax.axis_size("narrow")
    packed_bf = lax.all_gather(mat_master.astype(jnp.bfloat16), "narrow", axis=0, tiled=True)
    w_qkv, w_out, w_up, w_down, w_proj = unpack(packed_bf, narrow_count)
    (
        cls_vec,
        positions,
        ln1_gain,
        ln1_shift,
        ln2_gain,
        ln2_shift,
        final_gain,
        final_shift,
        bias_up,
        bias_down,
        bias_out,
    ) = split_vectors(vec_master)
    entries = piece_ids.shape[0]
    slot_ids = piece_ids.reshape(-1)
    group_rows = piece_table.shape[0]
    shard_rows = lax.all_gather(piece_table, ("wide", "narrow"), axis=0, tiled=True)
    targets = lax.iota(jnp.int32, shard_rows.shape[0])
    onehot = (slot_ids[:, None] == targets[None, :]).astype(jnp.bfloat16)
    looked = jnp.dot(onehot, shard_rows, preferred_element_type=jnp.float32)
    pieces = looked.reshape(entries, PSLOTS, D)
    first_slot = jnp.broadcast_to(cls_vec + positions[0], (entries, 1, D))
    slots_x = jnp.concatenate([first_slot, pieces + positions[1:]], axis=1)
    live_slots = jnp.concatenate([jnp.ones((entries, 1), jnp.int32), slot_mask], axis=1) > 0
    normed, norm1_pull = jax.vjp(layer_norm, slots_x, ln1_gain, ln1_shift)
    normed_bf = normed.astype(jnp.bfloat16)
    query_rows = jnp.einsum(
        "ed,fd->ef", normed_bf[:, 0], w_qkv[:D], preferred_element_type=jnp.float32
    )
    key_value = jnp.einsum("esd,fd->esf", normed_bf, w_qkv[D:], preferred_element_type=jnp.float32)
    attended, attend_pull = jax.vjp(
        partial(attend, live_slots=live_slots), query_rows, key_value[:, :, :D], key_value[:, :, D:]
    )
    attended_bf = attended.astype(jnp.bfloat16)
    residual = slots_x[:, 0] + jnp.einsum(
        "ed,fd->ef", attended_bf, w_out, preferred_element_type=jnp.float32
    )
    normed_two, norm2_pull = jax.vjp(layer_norm, residual, ln2_gain, ln2_shift)
    normed_two_bf = normed_two.astype(jnp.bfloat16)
    gate_in = (
        jnp.einsum("ed,fd->ef", normed_two_bf, w_up, preferred_element_type=jnp.float32) + bias_up
    )
    active, gelu_pull = jax.vjp(gelu_tanh, gate_in)
    active_bf = active.astype(jnp.bfloat16)
    second_residual = residual + (
        jnp.dot(active_bf, w_down, preferred_element_type=jnp.float32) + bias_down
    )
    normed_three, norm3_pull = jax.vjp(layer_norm, second_residual, final_gain, final_shift)
    normed_three_bf = normed_three.astype(jnp.bfloat16)
    table_local = (
        jnp.einsum("fd,ed->fe", w_proj, normed_three_bf, preferred_element_type=jnp.float32)
        + bias_out[:, None]
    )
    table_cols = lax.all_to_all(
        table_local, ("wide", "narrow"), split_axis=0, concat_axis=1, tiled=True
    )
    feature_rows = table_cols.shape[0]
    all_entries = table_cols.shape[1]
    flat_ids = text_ids.reshape(-1)
    flat_mask = text_mask.reshape(-1)
    token_count = flat_ids.shape[0]
    block_len = min(512, token_count)
    entry_index = lax.iota(jnp.int32, all_entries)
    text_embeds = jnp.take(table_cols, flat_ids, axis=1) * flat_mask[None, :].astype(jnp.float32)

    def text_block(step_index, grad_cols):
        begin_at = step_index * block_len
        ids_now = lax.dynamic_slice_in_dim(flat_ids, begin_at, block_len)
        keep_mask = lax.dynamic_slice_in_dim(flat_mask, begin_at, block_len)
        onehot = (entry_index[:, None] == ids_now[None, :]).astype(jnp.bfloat16)
        cot_now = lax.dynamic_slice_in_dim(text_cot, begin_at, block_len, 1)
        masked_cot = jnp.where(keep_mask[None, :] > 0, cot_now, jnp.zeros_like(cot_now))
        return grad_cols + lax.dot_general(
            masked_cot, onehot, (((1,), (1,)), ((), ())), preferred_element_type=jnp.float32
        )

    grad_cols = lax.fori_loop(
        0, token_count // block_len, text_block, jnp.zeros((feature_rows, all_entries), jnp.float32)
    )
    grad_table_cols = grad_cols.astype(jnp.bfloat16)
    grad_table = lax.all_to_all(
        grad_table_cols, ("wide", "narrow"), split_axis=1, concat_axis=0, tiled=True
    )
    grad_bias_out = jnp.sum(grad_table.astype(jnp.float32), axis=1)
    grad_proj = jnp.dot(grad_table, normed_three_bf, preferred_element_type=jnp.float32)
    grad_normed_three = contract_rows(grad_table, w_proj)
    grad_second, grad_final_gain, grad_final_shift = norm3_pull(grad_normed_three)
    grad_branch_two = grad_second.astype(jnp.bfloat16)
    grad_bias_down = jnp.sum(grad_branch_two.astype(jnp.float32), axis=0)
    grad_down = contract_rows(active_bf, grad_branch_two)
    grad_active = jnp.einsum(
        "ed,fd->ef", grad_branch_two, w_down, preferred_element_type=jnp.float32
    )
    (grad_gate,) = gelu_pull(grad_active)
    grad_gate_bf = grad_gate.astype(jnp.bfloat16)
    grad_bias_up = jnp.sum(grad_gate_bf.astype(jnp.float32), axis=0)
    grad_up = contract_rows(grad_gate_bf, normed_two_bf)
    grad_normed_two = jnp.dot(grad_gate_bf, w_up, preferred_element_type=jnp.float32)
    grad_residual_norm, grad_ln2_gain, grad_ln2_shift = norm2_pull(grad_normed_two)
    grad_residual = grad_second + grad_residual_norm
    grad_branch_one = grad_residual.astype(jnp.bfloat16)
    grad_out_w = contract_rows(grad_branch_one, attended_bf)
    grad_attended = jnp.dot(grad_branch_one, w_out, preferred_element_type=jnp.float32)
    grad_query, grad_keys, grad_values = attend_pull(grad_attended)
    grad_query_bf = grad_query.astype(jnp.bfloat16)
    grad_kv = jnp.concatenate(
        [grad_keys.astype(jnp.bfloat16), grad_values.astype(jnp.bfloat16)], axis=2
    )
    grad_q_w = contract_rows(grad_query_bf, normed_bf[:, 0])
    grad_kv_w = jnp.einsum("esf,esd->fd", grad_kv, normed_bf, preferred_element_type=jnp.float32)
    grad_normed = jnp.einsum("esf,fd->esd", grad_kv, w_qkv[D:], preferred_element_type=jnp.float32)
    grad_normed = grad_normed.at[:, 0].add(
        jnp.dot(grad_query_bf, w_qkv[:D], preferred_element_type=jnp.float32)
    )
    grad_slots, grad_ln1_gain, grad_ln1_shift = norm1_pull(grad_normed)
    grad_first = grad_slots[:, 0] + grad_residual
    grad_cls = jnp.sum(grad_first, axis=0)
    grad_pos = jnp.concatenate([grad_cls[None], jnp.sum(grad_slots[:, 1:], axis=0)], axis=0)
    grad_pieces = grad_slots[:, 1:].astype(jnp.bfloat16).reshape(-1, D)
    targets = lax.iota(jnp.int32, group_rows * lax.axis_size(("wide", "narrow")))
    onehot = (slot_ids[:, None] == targets[None, :]).astype(jnp.bfloat16)
    piece_grad = lax.psum_scatter(
        contract_rows(onehot, grad_pieces), ("wide", "narrow"), scatter_dimension=0, tiled=True
    )
    vec_local = jnp.concatenate(
        [
            grad_cls,
            grad_pos.reshape(-1),
            grad_ln1_gain,
            grad_ln1_shift,
            grad_ln2_gain,
            grad_ln2_shift,
            grad_final_gain,
            grad_final_shift,
            grad_bias_up,
            grad_bias_down,
            grad_bias_out,
        ]
    )
    grad_qkv = jnp.concatenate([grad_q_w, grad_kv_w], axis=0)
    packed_term = pack([grad_qkv, grad_out_w, grad_up, grad_down, grad_proj], narrow_count)
    block_grad = lax.psum_scatter(packed_term, "narrow", scatter_dimension=0, tiled=True)
    block_grad, vec_partial = lax.psum((block_grad, vec_local), "wide")
    grad_block = block_grad[0]
    momentum_block = MUON_BETA * mat_momentum[0] + grad_block
    update_block = grad_block + MUON_BETA * momentum_block
    segments = block_slices(update_block, narrow_count)
    local_squares = jnp.stack([jnp.sum(segment * segment) for segment in segments])
    squares, vec_grad = lax.psum((local_squares, vec_partial), "narrow")
    orthos = [
        segment / (jnp.sqrt(squares[position]) + 1e-07) for position, segment in enumerate(segments)
    ]
    for sweep_index in range(5):
        gram_sums = lax.psum(jnp.stack([gram_of(ortho_block) for ortho_block in orthos]), "narrow")
        orthos = [
            newton_step(ortho_block, gram_sums[position])
            for position, ortho_block in enumerate(orthos)
        ]
    new_segments = []
    for row_total, master_seg, ortho_block in zip(
        matrix_rows(), block_slices(mat_master[0], narrow_count), orthos
    ):
        new_segments.append(
            master_seg * (1.0 - MUON_RATE * MUON_DECAY)
            - MUON_RATE * math.sqrt(row_total / D) * ortho_block
        )
    weight_block = jnp.concatenate(new_segments, axis=0)[None]
    ema_block = EMA_DECAY * mat_ema + (1.0 - EMA_DECAY) * weight_block
    moment_one = ADAM_BETA1 * vec_moment1 + (1.0 - ADAM_BETA1) * vec_grad
    moment_two = ADAM_BETA2 * vec_moment2 + (1.0 - ADAM_BETA2) * vec_grad * vec_grad
    corrected_one = moment_one / (1.0 - ADAM_BETA1**STEP)
    corrected_two = moment_two / (1.0 - ADAM_BETA2**STEP)
    vec_weight = vec_master - ADAM_RATE * corrected_one / (jnp.sqrt(corrected_two) + ADAM_EPSILON)
    vec_ema_new = EMA_DECAY * vec_ema + (1.0 - EMA_DECAY) * vec_weight
    return (
        text_embeds,
        piece_grad,
        block_grad,
        momentum_block[None],
        weight_block,
        ema_block,
        vec_grad,
        moment_one,
        moment_two,
        vec_weight,
        vec_ema_new,
    )


def solution(mesh):
    in_specs = (
        P(("wide", "narrow"), None),
        P(("wide", "narrow"), None),
        P(("wide", "narrow"), None),
        P(),
        P(),
        P(("wide", "narrow"), None),
        P("narrow", None, None),
        P("narrow", None, None),
        P("narrow", None, None),
        P(),
        P(),
        P(),
        P(),
    )
    out_specs = (
        P(("wide", "narrow"), None),
        P(("wide", "narrow"), None),
        P("narrow", None, None),
        P("narrow", None, None),
        P("narrow", None, None),
        P("narrow", None, None),
        P(),
        P(),
        P(),
        P(),
        P(),
    )
    return jax.shard_map(
        on_device, mesh=mesh, in_specs=in_specs, out_specs=out_specs, check_vma=False
    )
```

profile of v0, /device:TPU:31, one launch (start us, length us, event | category | flops | bytes accessed | tf_op | source)
XLA Modules:
  0.0 3590.9 jit_solution(11161500927895284943)
XLA Ops:
  13.0 49.7 %while.15 = (s32[]{:T(128)}, f32[128,4096]{1,0:T(8,128)S(1)}, s32[8192]{0:T(1024)S(1)}, bf16[128,8192]{1,0:T(8,128)(2,1)}, s32[8192]{0:T(1024)S(1)}, /*index=5*/s32[]{:T(128)}, s32[]{:T(128)}, s32[]{:T(128)}, s32[]{:T(128)}) while((s32[]{:T(128)}, f32[128,4096]{1,0:T(8,128)S(1)}, s32[8192]{0:T(1024)S(1)}, ...), condition=%wide.region_9.10_spmd.clone, body=%wide.region_8.9_spmd.clone.sunk | while | flops 540082688 | bytes 4334761 | solution.py:213
  64.1 6.1 all-to-all-start.1
  71.2 145.1 %all-gather.5.cloned.1.call-done = bf16[4,2560,512]{2,1,0:T(8,128)(2,1)} async-done(((bf16[1,2560,512]{2,1,0:T(8,128)(2,1)}), bf16[4,2560,512]{2,1,0:T(8,128)(2,1)}) %all-gather.5.cloned.1.call-update) | async-done | bytes 10485776 | tf_op jit(solution)/shard_map/all_gather | solution.py:135
  231.2 181.2 %all-gather.3.cloned.1.call-done = bf16[32768,512]{1,0:T(8,128)(2,1)} async-done(((bf16[1024,512]{1,0:T(8,128)(2,1)}), bf16[32768,512]{1,0:T(8,128)(2,1)}) %all-gather.3.cloned.1.call-update) | async-done | bytes 33554448 | tf_op jit(solution)/shard_map/all_gather | solution.py:153
  412.4 35.1 fusion.12
  525.0 341.4 %reduce-scatter.5.cloned.1.call-done = f32[1,2560,512]{2,1,0:T(8,128)} async-done(((f32[4,2560,512]{2,1,0:T(8,128)}), f32[1,2560,512]{2,1,0:T(8,128)}) %reduce-scatter.5.cloned.1.call-update) | async-done | bytes 5242896 | tf_op jit(solution)/shard_map/reduce_scatter | solution.py:278
  871.7 24.2 psum.70
  895.9 67.7 %all-reduce.9.cloned.1.call-done = f32[1,2560,512]{2,1,0:T(8,128)} async-done(((f32[1,2560,512]{2,1,0:T(8,128)}), f32[1,2560,512]{2,1,0:T(8,128)}) %all-reduce.9.cloned.1.call-update) | async-done | bytes 5242896 | tf_op jit(solution)/shard_map/psum | solution.py:279
  963.6 7.7 fusion.16
  983.4 13.2 all-reduce.1
  1016.7 6.8 fusion.64
  1024.1 192.0 %all-reduce.11.cloned.1.call-done = f32[5,512,512]{2,1,0:T(8,128)} async-done(((f32[5,512,512]{2,1,0:T(8,128)}), f32[5,512,512]{2,1,0:T(8,128)}) %all-reduce.11.cloned.1.call-update) | async-done | bytes 5242896 | tf_op jit(solution)/shard_map/psum | solution.py:290
  1260.7 188.0 %all-reduce.13.cloned.1.call-done = f32[5,512,512]{2,1,0:T(8,128)} async-done(((f32[5,512,512]{2,1,0:T(8,128)}), f32[5,512,512]{2,1,0:T(8,128)}) %all-reduce.13.cloned.1.call-update) | async-done | bytes 5242896 | tf_op jit(solution)/shard_map/psum | solution.py:290
  1485.6 188.0 %all-reduce.15.cloned.1.call-done = f32[5,512,512]{2,1,0:T(8,128)} async-done(((f32[5,512,512]{2,1,0:T(8,128)}), f32[5,512,512]{2,1,0:T(8,128)}) %all-reduce.15.cloned.1.call-update) | async-done | bytes 5242896 | tf_op jit(solution)/shard_map/psum | solution.py:290
  1712.2 188.0 %all-reduce.17.cloned.1.call-done = f32[5,512,512]{2,1,0:T(8,128)} async-done(((f32[5,512,512]{2,1,0:T(8,128)}), f32[5,512,512]{2,1,0:T(8,128)}) %all-reduce.17.cloned.1.call-update) | async-done | bytes 5242896 | tf_op jit(solution)/shard_map/psum | solution.py:290
  1939.8 41.0 %fusion.11 = f32[32768,512]{1,0:T(8,128)} fusion(bf16[896,512]{1,0:T(8,128)(2,1)S(1)} %reshape.412, s32[896]{0:T(1024)S(1)} %copy-done.89), kind=kOutput, calls=%fused_computation.14 | convolution fusion | flops 30094131200 | bytes 68029952 | tf_op jit(solution)/shard_map/dot_general | solution.py:105
  1987.1 6.0 all-to-all-start
  1993.3 79.5 %all-to-all-done = f32[32,128,128]{1,2,0:T(8,128)S(1)} async-done(((f32[32,128,128]{1,2,0:T(8,128)}), f32[32,128,128]{1,2,0:T(8,128)S(1)}, u32[]{:S(2)}, u32[]{:S(2)}) %all-to-all-start) | async-done | bytes 2097184 | tf_op jit(solution)/shard_map/all_to_all | solution.py:190
  2072.8 28.0 gather_fusion
  2100.7 9.7 multiply_bitcast_fusion
  2110.4 5.8 copy.60
  2117.0 7.8 multiply_add_fusion.1
  2124.8 40.0 %all-reduce.19.cloned.1.call-done = f32[5,512,512]{2,1,0:T(8,128)} async-done(((f32[5,512,512]{2,1,0:T(8,128)}), f32[5,512,512]{2,1,0:T(8,128)}) %all-reduce.19.cloned.1.call-update) | async-done | bytes 5242896 | tf_op jit(solution)/shard_map/psum | solution.py:290
  2197.8 1380.6 %reduce-scatter.3.cloned.1.call-done = f32[1024,512]{1,0:T(8,128)} async-done(((f32[32768,512]{1,0:T(8,128)}), f32[1024,512]{1,0:T(8,128)}) %reduce-scatter.3.cloned.1.call-update) | async-done | bytes 2097168 | tf_op jit(solution)/shard_map/reduce_scatter | solution.py:258
  (472 shorter events, 387.5 us)
Async XLA Ops:
  7.2 209.2 %all-gather.5.cloned.1.call-start = ((), (), s32[]{:S(2)}) async-start(), calls=%async_computation.5 | async-start | bytes 13107200 | tf_op jit(solution)/shard_map/all_gather | solution.py:135
  11.6 400.8 %all-gather.3.cloned.1.call-start = ((), (), s32[]{:S(2)}) async-start(), calls=%async_computation.4 | async-start | bytes 34603008 | tf_op jit(solution)/shard_map/all_gather | solution.py:153
  64.1 408.3 %all-to-all-start.1 = ((bf16[128,32,128]{2,0,1:T(8,128)(2,1)}), bf16[128,32,128]{2,0,1:T(8,128)(2,1)S(1)}, u32[]{:S(2)}, u32[]{:S(2)}) async-start(bf16[128,32,128]{2,0,1:T(8,128)(2,1)} %copy_bitcast_fusion.1), calls=%async_computation.1 | async-start | bytes 2097152 | tf_op jit(solution)/shard_map/all_to_all | solution.py:217
  70.2 796.1 %reduce-scatter.5.cloned.1.call-start = ((), (), s32[]{:S(2)}) async-start(), calls=%async_computation.7 | async-start | bytes 26214400 | tf_op jit(solution)/shard_map/reduce_scatter | solution.py:278
  70.6 341.8 %copy-start.88 = (s32[896]{0:T(1024)}, s32[896]{0:T(1024)S(1)}, u32[]{:S(2)}) copy-start(s32[896]{0:T(1024)S(1)} %eq.61) | copy-start | bytes 10756
  71.2 441.9 %copy-start.60 = (f32[512]{0:T(512)}, f32[512]{0:T(512)S(1)}, u32[]{:S(2)}) copy-start(f32[512]{0:T(512)S(1)} %get-tuple-element.232) | copy-start | bytes 6148
  471.6 14.1 copy-start.71
  472.3 13.4 copy-start.74
  517.9 445.7 %all-reduce.9.cloned.1.call-start = ((), (), s32[]{:S(2)}) async-start(), calls=%async_computation.8 | async-start | bytes 10485760 | tf_op jit(solution)/shard_map/psum | solution.py:279
  866.4 349.7 %all-reduce.11.cloned.1.call-start = ((), (), s32[]{:S(2)}) async-start(), calls=%async_computation.9 | async-start | bytes 10485760 | tf_op jit(solution)/shard_map/psum | solution.py:290
  1023.6 425.1 %all-reduce.13.cloned.1.call-start = ((), (), s32[]{:S(2)}) async-start(), calls=%async_computation.10 | async-start | bytes 10485760 | tf_op jit(solution)/shard_map/psum | solution.py:290
  1260.7 412.9 %all-reduce.15.cloned.1.call-start = ((), (), s32[]{:S(2)}) async-start(), calls=%async_computation.11 | async-start | bytes 10485760 | tf_op jit(solution)/shard_map/psum | solution.py:290
  1485.5 414.6 %all-reduce.17.cloned.1.call-start = ((), (), s32[]{:S(2)}) async-start(), calls=%async_computation.12 | async-start | bytes 10485760 | tf_op jit(solution)/shard_map/psum | solution.py:290
  1685.9 13.3 copy-start.43
  1689.7 11.5 copy-start.15
  1712.1 192.0 %copy-start.24 = (f32[384,512]{1,0:T(8,128)S(1)}, f32[384,512]{1,0:T(8,128)}, u32[]{:S(2)}) copy-start(f32[384,512]{1,0:T(8,128)} %copy-done.23) | copy-start | bytes 2359300
  1712.1 198.3 %copy-start.44 = (f32[128,512]{1,0:T(8,128)S(1)}, f32[128,512]{1,0:T(8,128)}, u32[]{:S(2)}) copy-start(f32[128,512]{1,0:T(8,128)} %copy-done.43) | copy-start | bytes 786436
  1712.1 452.7 %all-reduce.19.cloned.1.call-start = ((), (), s32[]{:S(2)}) async-start(), calls=%async_computation.13 | async-start | bytes 10485760 | tf_op jit(solution)/shard_map/psum | solution.py:290
  1915.0 11.5 copy-start.11
  1937.3 1641.1 %reduce-scatter.3.cloned.1.call-start = ((), (), s32[]{:S(2)}) async-start(), calls=%async_computation.6 | async-start | bytes 69206016 | tf_op jit(solution)/shard_map/reduce_scatter | solution.py:258
  1987.1 85.7 %all-to-all-start = ((f32[32,128,128]{1,2,0:T(8,128)}), f32[32,128,128]{1,2,0:T(8,128)S(1)}, u32[]{:S(2)}, u32[]{:S(2)}) async-start(f32[32,128,128]{1,2,0:T(8,128)} %bitcast.537), calls=%async_computation | async-start | bytes 4194304 | tf_op jit(solution)/shard_map/all_to_all | solution.py:190
  2072.8 28.0 copy-start.58
  2117.0 51.8 %copy-start.21 = (f32[384,512]{1,0:T(8,128)S(1)}, f32[384,512]{1,0:T(8,128)}, u32[]{:S(2)}) copy-start(f32[384,512]{1,0:T(8,128)} %copy-done.20) | copy-start | bytes 2359300
  2164.9 14.4 slice-start
  (89 other events, 419.9 us)
Sparse Core Ops, SparseCore 0:
  11.7 204.6 all-gather.4
  219.3 193.0 all-gather.2
  518.0 348.2 reduce-scatter.4
  869.8 93.7 all-reduce.8
  1023.7 192.2 all-reduce.10
  1260.8 187.8 all-reduce.12
  1485.7 187.8 all-reduce.14
  1712.2 187.8 all-reduce.16
  1937.4 227.4 all-reduce.18
  2167.6 1410.6 reduce-scatter.2
where the time goes:
time: 3600 us; the launch traced here: 3590 us
  waiting for transfers between devices  2990 us (83%)
  matrix products  365 us (10%)
  local copies, waits for them, and re-layouts  97 us (3%)
  other arithmetic  65.9 us (2%)
  blocking collectives  37.4 us (1%)
    reduce_scatter x1, waiting for transfers between devices, on_device(): lax.psum_scatter(contract_rows(onehot, grad_pieces), ('wide', 'narrow'),...  1380 us
    psum x5, waiting for transfers between devices, on_device(): lax.psum(jnp.stack([gram_of(ortho_block) for ortho_block in orthos]), 'na...  796 us
    reduce_scatter x1, waiting for transfers between devices, on_device(): lax.psum_scatter(packed_term, 'narrow', scatter_dimension=0, tiled=True)  341 us
    all_gather x1, waiting for transfers between devices, on_device(): lax.all_gather(piece_table, ('wide', 'narrow'), axis=0, tiled=True)  181 us
    all_gather x1, waiting for transfers between devices, on_device(): lax.all_gather(mat_master.astype(jnp.bfloat16), 'narrow', axis=0, tiled=T...  145 us
    dot_general x25, matrix products, gram_of(): lax.dot_general(block, block, (((0,), (0,)), ((), ())), precision=HIGHEST)  85.1 us
    all_to_all x1, waiting for transfers between devices, on_device(): lax.all_to_all(table_local, ('wide', 'narrow'), split_axis=0, concat_axis...  79.5 us
  transfers between devices with their start and end apart: 12, of which 11 were waited for; matrix products, arithmetic and copies ran while one was open for 7% of the time, Pallas kernels for 0%

commit v1 on v0

--- a/solution.py
+++ b/solution.py
@@ -17,6 +17,7 @@
 
 
 HIGHEST = lax.Precision.HIGHEST
+HIGH = lax.Precision.HIGH
 MUON_RATE = 0.5
 MUON_DECAY = 0.01
 MUON_BETA = 0.95
@@ -101,6 +102,15 @@
     return mixed_heads.reshape(entry_count, D)
 
 
+PIECE_CAPS = {1024: 58, 256: 16}
+BOTH = ("wide", "narrow")
+
+
+def piece_cap(group_rows):
+    cap = PIECE_CAPS.get(group_rows, group_rows)
+    return -(-cap // 16) * 16
+
+
 def contract_rows(left, right):
     return lax.dot_general(
         left, right, (((0,), (0,)), ((), ())), preferred_element_type=jnp.float32
@@ -109,11 +119,6 @@
 
 def gram_of(block):
     return lax.dot_general(block, block, (((0,), (0,)), ((), ())), precision=HIGHEST)
-
-
-def newton_step(ortho_block, gram):
-    poly = NEWTON_B * gram + NEWTON_C * jnp.dot(gram, gram, precision=HIGHEST)
-    return NEWTON_A * ortho_block + jnp.dot(ortho_block, poly, precision=HIGHEST)
 
 
 def on_device(
@@ -132,7 +137,17 @@
     vec_ema,
 ):
     narrow_count = lax.axis_size("narrow")
-    packed_bf = lax.all_gather(mat_master.astype(jnp.bfloat16), "narrow", axis=0, tiled=True)
+    wide_count = lax.axis_size("wide")
+    device_count = narrow_count * wide_count
+    wide_at = lax.axis_index("wide")
+    narrow_at = lax.axis_index("narrow")
+    me = wide_at * narrow_count + narrow_at
+    block_rows = mat_master.shape[1]
+    own_rows = block_rows // wide_count
+    own_part = lax.dynamic_slice_in_dim(mat_master[0], wide_at * own_rows, own_rows, 0)
+    packed_bf = lax.all_gather(
+        own_part.astype(jnp.bfloat16), ("narrow", "wide"), axis=0, tiled=True
+    ).reshape(narrow_count, block_rows, D)
     w_qkv, w_out, w_up, w_down, w_proj = unpack(packed_bf, narrow_count)
     (
         cls_vec,
@@ -149,55 +164,46 @@
     ) = split_vectors(vec_master)
     entries = piece_ids.shape[0]
     slot_ids = piece_ids.reshape(-1)
+    slot_count = slot_ids.shape[0]
     group_rows = piece_table.shape[0]
-    shard_rows = lax.all_gather(piece_table, ("wide", "narrow"), axis=0, tiled=True)
-    targets = lax.iota(jnp.int32, shard_rows.shape[0])
-    onehot = (slot_ids[:, None] == targets[None, :]).astype(jnp.bfloat16)
-    looked = jnp.dot(onehot, shard_rows, preferred_element_type=jnp.float32)
+    cap = piece_cap(group_rows)
+    every_ids = lax.all_gather(slot_ids, BOTH, axis=0, tiled=False)
+    asked = every_ids // group_rows == me
+    before = (
+        lax.broadcasted_iota(jnp.int32, (slot_count, slot_count), 0)
+        < lax.broadcasted_iota(jnp.int32, (slot_count, slot_count), 1)
+    )
+    asked_rank = jnp.dot(
+        asked.astype(jnp.bfloat16), before.astype(jnp.bfloat16), preferred_element_type=jnp.float32
+    ).astype(jnp.int32)
+    asked_rank = jnp.where(asked, asked_rank, -1)
+    chosen = asked_rank[:, None, :] == lax.iota(jnp.int32, cap)[None, :, None]
+    local_ids = every_ids - me * group_rows + 1
+    asked_rows = jnp.sum(jnp.where(chosen, local_ids[:, None, :], 0), axis=2).reshape(-1) - 1
+    asked_onehot = (
+        asked_rows[:, None] == lax.iota(jnp.int32, group_rows)[None, :]
+    ).astype(jnp.bfloat16)
+    outgoing = jnp.dot(asked_onehot, piece_table, preferred_element_type=jnp.float32)
+    incoming = lax.all_to_all(
+        outgoing.astype(jnp.bfloat16).reshape(device_count, cap, D), BOTH, 0, 0, tiled=True
+    ).reshape(device_count * cap, D)
+    own_group = slot_ids // group_rows
+    same = (own_group[:, None] == own_group[None, :]) & before.T
+    own_rank = jnp.sum(same.astype(jnp.int32), axis=1)
+    own_spot = own_group * cap + own_rank
+    own_onehot = (
+        own_spot[:, None] == lax.iota(jnp.int32, device_count * cap)[None, :]
+    ).astype(jnp.bfloat16)
+    looked = jnp.dot(own_onehot, incoming, preferred_element_type=jnp.float32)
     pieces = looked.reshape(entries, PSLOTS, D)
-    first_slot = jnp.broadcast_to(cls_vec + positions[0], (entries, 1, D))
-    slots_x = jnp.concatenate([first_slot, pieces + positions[1:]], axis=1)
-    live_slots = jnp.concatenate([jnp.ones((entries, 1), jnp.int32), slot_mask], axis=1) > 0
-    normed, norm1_pull = jax.vjp(layer_norm, slots_x, ln1_gain, ln1_shift)
-    normed_bf = normed.astype(jnp.bfloat16)
-    query_rows = jnp.einsum(
-        "ed,fd->ef", normed_bf[:, 0], w_qkv[:D], preferred_element_type=jnp.float32
-    )
-    key_value = jnp.einsum("esd,fd->esf", normed_bf, w_qkv[D:], preferred_element_type=jnp.float32)
-    attended, attend_pull = jax.vjp(
-        partial(attend, live_slots=live_slots), query_rows, key_value[:, :, :D], key_value[:, :, D:]
-    )
-    attended_bf = attended.astype(jnp.bfloat16)
-    residual = slots_x[:, 0] + jnp.einsum(
-        "ed,fd->ef", attended_bf, w_out, preferred_element_type=jnp.float32
-    )
-    normed_two, norm2_pull = jax.vjp(layer_norm, residual, ln2_gain, ln2_shift)
-    normed_two_bf = normed_two.astype(jnp.bfloat16)
-    gate_in = (
-        jnp.einsum("ed,fd->ef", normed_two_bf, w_up, preferred_element_type=jnp.float32) + bias_up
-    )
-    active, gelu_pull = jax.vjp(gelu_tanh, gate_in)
-    active_bf = active.astype(jnp.bfloat16)
-    second_residual = residual + (
-        jnp.dot(active_bf, w_down, preferred_element_type=jnp.float32) + bias_down
-    )
-    normed_three, norm3_pull = jax.vjp(layer_norm, second_residual, final_gain, final_shift)
-    normed_three_bf = normed_three.astype(jnp.bfloat16)
-    table_local = (
-        jnp.einsum("fd,ed->fe", w_proj, normed_three_bf, preferred_element_type=jnp.float32)
-        + bias_out[:, None]
-    )
-    table_cols = lax.all_to_all(
-        table_local, ("wide", "narrow"), split_axis=0, concat_axis=1, tiled=True
-    )
-    feature_rows = table_cols.shape[0]
-    all_entries = table_cols.shape[1]
+
     flat_ids = text_ids.reshape(-1)
     flat_mask = text_mask.reshape(-1)
     token_count = flat_ids.shape[0]
+    feature_rows = text_cot.shape[0]
+    all_entries = entries * device_count
     block_len = min(512, token_count)
     entry_index = lax.iota(jnp.int32, all_entries)
-    text_embeds = jnp.take(table_cols, flat_ids, axis=1) * flat_mask[None, :].astype(jnp.float32)
 
     def text_block(step_index, grad_cols):
         begin_at = step_index * block_len
@@ -214,12 +220,48 @@
         0, token_count // block_len, text_block, jnp.zeros((feature_rows, all_entries), jnp.float32)
     )
     grad_table_cols = grad_cols.astype(jnp.bfloat16)
-    grad_table = lax.all_to_all(
-        grad_table_cols, ("wide", "narrow"), split_axis=1, concat_axis=0, tiled=True
-    )
-    grad_bias_out = jnp.sum(grad_table.astype(jnp.float32), axis=1)
-    grad_proj = jnp.dot(grad_table, normed_three_bf, preferred_element_type=jnp.float32)
+    grad_table = lax.all_to_all(grad_table_cols, BOTH, split_axis=1, concat_axis=0, tiled=True)
+    grad_bias_own = jnp.sum(grad_table_cols.astype(jnp.float32), axis=1)
     grad_normed_three = contract_rows(grad_table, w_proj)
+
+    first_slot = jnp.broadcast_to(cls_vec + positions[0], (entries, 1, D))
+    slots_x = jnp.concatenate([first_slot, pieces + positions[1:]], axis=1)
+    live_slots = jnp.concatenate([jnp.ones((entries, 1), jnp.int32), slot_mask], axis=1) > 0
+    normed, norm1_pull = jax.vjp(layer_norm, slots_x, ln1_gain, ln1_shift)
+    normed_bf = normed.astype(jnp.bfloat16)
+    query_rows = jnp.einsum(
+        "ed,fd->ef", normed_bf[:, 0], w_qkv[:D], preferred_element_type=jnp.float32
+    )
+    key_value = jnp.einsum("esd,fd->esf", normed_bf, w_qkv[D:], preferred_element_type=jnp.float32)
+    attended, attend_pull = jax.vjp(
+        partial(attend, live_slots=live_slots), query_rows, key_value[:, :, :D], key_value[:, :, D:]
+    )
+    attended_bf = attended.astype(jnp.bfloat16)
+    residual = slots_x[:, 0] + jnp.einsum(
+        "ed,fd->ef", attended_bf, w_out, preferred_element_type=jnp.float32
+    )
+    normed_two, norm2_pull = jax.vjp(layer_norm, residual, ln2_gain, ln2_shift)
+    normed_two_bf = normed_two.astype(jnp.bfloat16)
+    gate_in = (
+        jnp.einsum("ed,fd->ef", normed_two_bf, w_up, preferred_element_type=jnp.float32) + bias_up
+    )
+    active, gelu_pull = jax.vjp(gelu_tanh, gate_in)
+    active_bf = active.astype(jnp.bfloat16)
+    second_residual = residual + (
+        jnp.dot(active_bf, w_down, preferred_element_type=jnp.float32) + bias_down
+    )
+    normed_three, norm3_pull = jax.vjp(layer_norm, second_residual, final_gain, final_shift)
+    normed_three_bf = normed_three.astype(jnp.bfloat16)
+    every_normed = lax.all_gather(normed_three_bf, BOTH, axis=0, tiled=True)
+    proj_own = lax.dynamic_slice_in_dim(w_proj, me * feature_rows, feature_rows, 0)
+    bias_own = lax.dynamic_slice_in_dim(bias_out, me * feature_rows, feature_rows, 0)
+    table_cols = (
+        jnp.einsum("fd,ed->fe", proj_own, every_normed, preferred_element_type=jnp.float32)
+        + bias_own[:, None]
+    )
+    text_embeds = jnp.take(table_cols, flat_ids, axis=1) * flat_mask[None, :].astype(jnp.float32)
+    grad_proj_own = jnp.dot(grad_table_cols, every_normed, preferred_element_type=jnp.float32)
+
     grad_second, grad_final_gain, grad_final_shift = norm3_pull(grad_normed_three)
     grad_branch_two = grad_second.astype(jnp.bfloat16)
     grad_bias_down = jnp.sum(grad_branch_two.astype(jnp.float32), axis=0)
@@ -253,11 +295,12 @@
     grad_cls = jnp.sum(grad_first, axis=0)
     grad_pos = jnp.concatenate([grad_cls[None], jnp.sum(grad_slots[:, 1:], axis=0)], axis=0)
     grad_pieces = grad_slots[:, 1:].astype(jnp.bfloat16).reshape(-1, D)
-    targets = lax.iota(jnp.int32, group_rows * lax.axis_size(("wide", "narrow")))
-    onehot = (slot_ids[:, None] == targets[None, :]).astype(jnp.bfloat16)
-    piece_grad = lax.psum_scatter(
-        contract_rows(onehot, grad_pieces), ("wide", "narrow"), scatter_dimension=0, tiled=True
-    )
+    grad_outgoing = contract_rows(own_onehot, grad_pieces).astype(jnp.bfloat16)
+    grad_incoming = lax.all_to_all(
+        grad_outgoing.reshape(device_count, cap, D), BOTH, 0, 0, tiled=True
+    ).reshape(device_count * cap, D)
+    piece_grad = contract_rows(asked_onehot, grad_incoming)
+
     vec_local = jnp.concatenate(
         [
             grad_cls,
@@ -270,35 +313,57 @@
             grad_final_shift,
             grad_bias_up,
             grad_bias_down,
-            grad_bias_out,
+            lax.dynamic_update_slice_in_dim(
+                jnp.zeros((OUTW,), jnp.float32), grad_bias_own, me * feature_rows, 0
+            ),
         ]
     )
+    vec_grad = lax.psum(vec_local, BOTH)
     grad_qkv = jnp.concatenate([grad_q_w, grad_kv_w], axis=0)
-    packed_term = pack([grad_qkv, grad_out_w, grad_up, grad_down, grad_proj], narrow_count)
-    block_grad = lax.psum_scatter(packed_term, "narrow", scatter_dimension=0, tiled=True)
-    block_grad, vec_partial = lax.psum((block_grad, vec_local), "wide")
-    grad_block = block_grad[0]
+    packed_term = jnp.concatenate(
+        [
+            matrix.reshape(narrow_count, matrix.shape[0] // narrow_count, D)
+            for matrix in (grad_qkv, grad_out_w, grad_up, grad_down)
+        ],
+        axis=1,
+    )
+    term_rows = packed_term.shape[1]
+    share = term_rows // wide_count
+    packed_term = (
+        packed_term.astype(jnp.bfloat16)
+        .reshape(narrow_count, wide_count, share, D)
+        .transpose(1, 0, 2, 3)
+        .reshape(device_count, share, D)
+    )
+    terms = lax.all_to_all(packed_term, BOTH, 0, 0, tiled=True)
+    share_sum = jnp.sum(terms.astype(jnp.float32), axis=0)
+    main_grad = lax.all_gather(share_sum.astype(jnp.bfloat16), "wide", axis=0, tiled=True)
+    proj_grad = lax.all_gather(grad_proj_own.astype(jnp.bfloat16), BOTH, axis=0, tiled=True)
+    proj_rows = OUTW // narrow_count
+    proj_grad = lax.dynamic_slice_in_dim(proj_grad, narrow_at * proj_rows, proj_rows, 0)
+    grad_block = jnp.concatenate([main_grad, proj_grad], axis=0).astype(jnp.float32)
     momentum_block = MUON_BETA * mat_momentum[0] + grad_block
     update_block = grad_block + MUON_BETA * momentum_block
     segments = block_slices(update_block, narrow_count)
-    local_squares = jnp.stack([jnp.sum(segment * segment) for segment in segments])
-    squares, vec_grad = lax.psum((local_squares, vec_partial), "narrow")
-    orthos = [
-        segment / (jnp.sqrt(squares[position]) + 1e-07) for position, segment in enumerate(segments)
-    ]
-    for sweep_index in range(5):
-        gram_sums = lax.psum(jnp.stack([gram_of(ortho_block) for ortho_block in orthos]), "narrow")
-        orthos = [
-            newton_step(ortho_block, gram_sums[position])
-            for position, ortho_block in enumerate(orthos)
-        ]
+    grams = lax.psum(jnp.stack([gram_of(segment) for segment in segments]), "narrow")
     new_segments = []
-    for row_total, master_seg, ortho_block in zip(
-        matrix_rows(), block_slices(mat_master[0], narrow_count), orthos
+    for position, (row_total, master_seg, segment) in enumerate(
+        zip(matrix_rows(), block_slices(mat_master[0], narrow_count), segments)
     ):
+        square = jnp.sum(jnp.diagonal(grams[position]))
+        norm = jnp.sqrt(square) + 1e-07
+        gram = grams[position] / (norm * norm)
+        chain = None
+        for sweep_index in range(5):
+            squared = jnp.dot(gram, gram, precision=HIGH)
+            poly = NEWTON_B * gram + NEWTON_C * squared + NEWTON_A * jnp.eye(D, dtype=jnp.float32)
+            chain = poly if chain is None else jnp.dot(chain, poly, precision=HIGH)
+            if sweep_index < 4:
+                gram = jnp.dot(jnp.dot(gram, poly, precision=HIGH), poly, precision=HIGH)
+        ortho = jnp.dot(segment / norm, chain, precision=HIGH)
         new_segments.append(
             master_seg * (1.0 - MUON_RATE * MUON_DECAY)
-            - MUON_RATE * math.sqrt(row_total / D) * ortho_block
+            - MUON_RATE * math.sqrt(row_total / D) * ortho
         )
     weight_block = jnp.concatenate(new_segments, axis=0)[None]
     ema_block = EMA_DECAY * mat_ema + (1.0 - EMA_DECAY) * weight_block
@@ -311,7 +376,7 @@
     return (
         text_embeds,
         piece_grad,
-        block_grad,
+        grad_block[None],
         momentum_block[None],
         weight_block,
         ema_block,

time: 3600 us -> 921 us (0.26)
  waiting for transfers between devices: 2990 us -> 293 us
  matrix products: 365 us -> 228 us
  blocking collectives: 37.4 us -> 146 us
    reduce_scatter x2 -> x0, waiting for transfers between devices: 1720 us -> none  [the longest x1 1380 us: on_device(): lax.psum_scatter(contract_rows(onehot, grad_pieces), ('wide', 'narrow'),...]
    psum x6 -> x1, waiting for transfers between devices: 864 us -> 77.9 us  [on_device(): lax.psum(jnp.stack([gram_of(segment) for segment in segments]), 'narrow')]
    all_gather x2 -> x4, waiting for transfers between devices: 326 us -> 70.1 us  [the longest x1 47.7 us: on_device(): every_normed = lax.all_gather(normed_three_bf, BOTH, axis=0, tiled=True)]
    all_gather x0 -> x1, blocking collectives: none -> 101 us  [on_device(): every_ids = lax.all_gather(slot_ids, BOTH, axis=0, tiled=False)]
    dot_general x25 -> x5, matrix products: 85.1 us -> 15 us  [gram_of(): lax.dot_general(block, block, (((0,), (0,)), ((), ())), precision=HIGHEST)]
    all_to_all x2 -> x4, waiting for transfers between devices: 79.5 us -> 145 us  [the longest x1 103 us: on_device(): terms = lax.all_to_all(packed_term, BOTH, 0, 0, tiled=True)]
    dot_general x6 -> x7, matrix products: 53.7 us -> 14.1 us  [contract_rows(): lax.dot_general(left, right, (((0,), (0,)), ((), ())), preferred_element_...]
    gather x0 -> x5, local copies, waits for them, and re-layouts: none -> 36.8 us  [on_device(): square = jnp.sum(jnp.diagonal(grams[position]))]
  transfers between devices with their start and end apart: 12 -> 9, of which waited for: 11 -> 5; matrix products, arithmetic and copies ran while one was open for 7% -> 22% of each run, Pallas kernels for 0% -> 0%
where the time goes in v1:
time: 921 us; the launch traced here: 909 us
  waiting for transfers between devices  293 us (32%)
  matrix products  228 us (25%)
  blocking collectives  146 us (16%)
  local copies, waits for them, and re-layouts  129 us (14%)
  other arithmetic  59.9 us (7%)
  starting transfers between devices  32.6 us (4%)
  between operations  19.6 us (2%)
    all_to_all x1, waiting for transfers between devices, on_device(): terms = lax.all_to_all(packed_term, BOTH, 0, 0, tiled=True)  103 us
    all_gather x1, blocking collectives, on_device(): every_ids = lax.all_gather(slot_ids, BOTH, axis=0, tiled=False)  101 us
    psum x1, waiting for transfers between devices, on_device(): lax.psum(jnp.stack([gram_of(segment) for segment in segments]), 'narrow')  77.9 us
    dot_general x40, matrix products, on_device(): gram = jnp.dot(jnp.dot(gram, poly, precision=HIGH), poly, precision=HIGH)  51.1 us
    all_gather x1, waiting for transfers between devices, on_device(): every_normed = lax.all_gather(normed_three_bf, BOTH, axis=0, tiled=True)  47.7 us
    dot_general x16, matrix products, text_block(): lax.dot_general(masked_cot, onehot, (((1,), (1,)), ((), ())), preferred_e...  46.7 us
    psum x1, blocking collectives, on_device(): vec_grad = lax.psum(vec_local, BOTH)  44.6 us
    all_to_all x1, waiting for transfers between devices, on_device(): lax.all_to_all(outgoing.astype(jnp.bfloat16).reshape(device_count, cap, D...  41.7 us
  transfers between devices with their start and end apart: 9, of which 5 were waited for; matrix products, arithmetic and copies ran while one was open for 22% of the time, Pallas kernels for 0%

profile of v1, /device:TPU:31, one launch (start us, length us, event | category | flops | bytes accessed | tf_op | source)
XLA Modules:
  0.0 909.1 jit_solution(11310662788399326676)
XLA Ops:
  10.6 49.7 %while.15 = (s32[]{:T(128)}, f32[128,4096]{1,0:T(8,128)S(1)}, s32[8192]{0:T(1024)S(1)}, bf16[128,8192]{1,0:T(8,128)(2,1)}, s32[8192]{0:T(1024)S(1)}, /*index=5*/s32[]{:T(128)}, s32[]{:T(128)}, s32[]{:T(128)}, s32[]{:T(128)}) while((s32[]{:T(128)}, f32[128,4096]{1,0:T(8,128)S(1)}, s32[8192]{0:T(1024)S(1)}, ...), condition=%wide.region_11.12_spmd.clone, body=%wide.region_10.11_spmd.clone.sunk | while | flops 540082688 | bytes 4334761 | solution.py:219
  61.7 6.1 all-to-all-start.1
  68.2 101.5 %all-gather.1 = s32[32,1,896]{2,1,0:T(1,128)S(1)} all-gather(s32[1,1,896]{2,1,0:T(1,128)S(1)} %reshape.614), channel_id=1, replica_groups=mesh['wide'=8,'narrow'=4] {'wide','narrow'}, dimensions={0}, use_global_device_ids=true | all-gather | bytes 118272 | tf_op jit(solution)/shard_map/all_gather | solution.py:170
  174.7 9.3 %all-to-all-start = ((bf16[32,64,512]{2,1,0:T(8,128)(2,1)}), bf16[32,64,512]{2,1,0:T(8,128)(2,1)}, u32[]{:S(2)}, u32[]{:S(2)}) async-start(bf16[32,64,512]{2,1,0:T(8,128)(2,1)} %bitcast.465), calls=%async_computation | async-start | bytes 4194304 | tf_op jit(solution)/shard_map/all_to_all | solution.py:187
  186.9 41.7 %all-to-all-done = bf16[32,64,512]{2,1,0:T(8,128)(2,1)} async-done(((bf16[32,64,512]{2,1,0:T(8,128)(2,1)}), bf16[32,64,512]{2,1,0:T(8,128)(2,1)}, u32[]{:S(2)}, u32[]{:S(2)}) %all-to-all-start) | async-done | bytes 2097184 | tf_op jit(solution)/shard_map/all_to_all | solution.py:187
  242.6 4.5 fusion.191
  302.7 7.2 all-to-all-start.3
  310.0 47.7 %all-gather.7.cloned.1.call-done = bf16[4096,512]{1,0:T(8,128)(2,1)} async-done(((bf16[128,512]{1,0:T(8,128)(2,1)}), bf16[4096,512]{1,0:T(8,128)(2,1)}) %all-gather.7.cloned.1.call-update) | async-done | bytes 4194320 | tf_op jit(solution)/shard_map/all_gather | solution.py:255
  370.4 103.1 %all-to-all-done.3 = bf16[32,192,512]{2,1,0:T(8,128)(2,1)} async-done(((bf16[32,192,512]{2,1,0:T(8,128)(2,1)}), bf16[32,192,512]{2,1,0:T(8,128)(2,1)}, u32[]{:S(2)}, u32[]{:S(2)}) %all-to-all-start.3) | async-done | bytes 6291488 | tf_op jit(solution)/shard_map/all_to_all | solution.py:338
  486.5 9.6 %all-to-all-start.2 = ((bf16[32,64,512]{2,1,0:T(8,128)(2,1)}), bf16[32,64,512]{2,1,0:T(8,128)(2,1)}, u32[]{:S(2)}, u32[]{:S(2)}) async-start(bf16[32,64,512]{2,1,0:T(8,128)(2,1)} %bitcast.43), calls=%async_computation.2 | async-start | bytes 4194304 | tf_op jit(solution)/shard_map/all_to_all | solution.py:299
  497.8 22.4 %all-gather.9.cloned.1.call-done = bf16[1536,512]{1,0:T(8,128)(2,1)} async-done(((bf16[192,512]{1,0:T(8,128)(2,1)}), bf16[1536,512]{1,0:T(8,128)(2,1)}) %all-gather.9.cloned.1.call-update) | async-done | bytes 1572880 | tf_op jit(solution)/shard_map/all_gather | solution.py:340
  539.9 44.6 %psum.15 = f32[14336]{0:T(1024)S(1)} all-reduce(f32[14336]{0:T(1024)S(1)} %constant_dynamic-update-slice_fusion.7), channel_id=1, replica_groups=mesh['wide'=8,'narrow'=4] {'wide','narrow'}, use_global_device_ids=true, to_apply=%region_39.40 | all-reduce | flops 14336 | bytes 114688 | tf_op jit(solution)/shard_map/psum | solution.py:321
  585.3 5.9 fusion.11
  596.8 28.0 %gather_fusion = f32[8192,128]{1,0:T(8,128)} fusion(f32[128,4096]{0,1:T(8,128)S(1)} %copy.103, s32[8192]{0:T(1024)S(1)} %broadcast_clamp_fusion), kind=kCustom, calls=%fused_computation | custom fusion | bytes 8421376 | tf_op jit(solution)/shard_map/jit(_take)/gather | solution.py:262
  624.8 9.7 %multiply_bitcast_fusion = f32[128,8192]{0,1:T(8,128)} fusion(f32[8192,128]{1,0:T(8,128)} %gather_fusion, f32[8192]{0:T(1024)S(1)} %copy-done.42, pred[8192]{0:T(1024)(128)(4,1)S(1)} %compare_and_fusion), kind=kLoop, calls=%fused_computation.60 | loop fusion | flops 2097152 | bytes 8429568 | tf_op jit(solution)/shard_map/mul | solution.py:262
  634.5 5.6 copy.114
  641.9 8.9 multiply_add_fusion.1
  650.8 77.9 %all-reduce.3.cloned.1.call-done = f32[5,512,512]{2,1,0:T(8,128)} async-done(((f32[5,512,512]{2,1,0:T(8,128)}), f32[5,512,512]{2,1,0:T(8,128)}) %all-reduce.3.cloned.1.call-update) | async-done | bytes 5242896 | tf_op jit(solution)/shard_map/psum | solution.py:348
  728.7 4.6 slice_bitcast_fusion.1
  733.2 9.1 gather_fusion.1
  755.3 9.1 gather_fusion.2
  777.2 4.7 gather_fusion.3
  794.5 4.7 gather_fusion.4
  812.1 9.2 %gather_fusion.5 = f32[512]{0:T(512)S(1)} fusion(f32[512,512]{1,0:T(8,128)} %get-tuple-element.248, s32[512]{0:T(512)S(1)} %bitcast.433), kind=kCustom, calls=%fused_computation.5 | custom fusion | bytes 8192 | tf_op jit(solution)/shard_map/jit(diagonal)/cond/branch_0_fun/gather | solution.py:353
  (473 shorter events, 314.1 us)
Async XLA Ops:
  7.2 163.9 %copy-start = (bf16[1024,512]{1,0:T(8,128)(2,1)S(1)}, bf16[1024,512]{1,0:T(8,128)(2,1)}, u32[]{:S(2)}) copy-start(bf16[1024,512]{1,0:T(8,128)(2,1)} %param.17) | copy-start | bytes 3145732
  7.2 227.1 %all-gather.13.cloned.1.call-start = ((), (), s32[]{:S(2)}) async-start(), calls=%async_computation.8 | async-start | bytes 10813440 | tf_op jit(solution)/shard_map/all_gather | solution.py:148
  61.7 112.9 %all-to-all-start.1 = ((bf16[128,32,128]{0,2,1:T(8,128)(2,1)}), bf16[128,32,128]{0,2,1:T(8,128)(2,1)S(1)}, u32[]{:S(2)}, u32[]{:S(2)}) async-start(bf16[128,32,128]{0,2,1:T(8,128)(2,1)} %bitcast.27), calls=%async_computation.1 | async-start | bytes 2097152 | tf_op jit(solution)/shard_map/all_to_all | solution.py:223
  174.6 10.7 %copy-start.72 = (s32[128,7]{0,1:T(8,128)S(1)}, s32[128,7]{0,1:T(8,128)}, u32[]{:S(2)}) copy-start(s32[128,7]{0,1:T(8,128)} %param.19) | copy-start | bytes 10756
  174.7 53.9 %all-to-all-start = ((bf16[32,64,512]{2,1,0:T(8,128)(2,1)}), bf16[32,64,512]{2,1,0:T(8,128)(2,1)}, u32[]{:S(2)}, u32[]{:S(2)}) async-start(bf16[32,64,512]{2,1,0:T(8,128)(2,1)} %bitcast.465), calls=%async_computation | async-start | bytes 4194304 | tf_op jit(solution)/shard_map/all_to_all | solution.py:187
  184.0 173.7 %all-gather.7.cloned.1.call-start = ((), (), s32[]{:S(2)}) async-start(), calls=%async_computation.4 | async-start | bytes 4325376 | tf_op jit(solution)/shard_map/all_gather | solution.py:255
  185.4 81.5 %copy-start.46 = (f32[512]{0:T(512)}, f32[512]{0:T(512)S(1)}, u32[]{:S(2)}) copy-start(f32[512]{0:T(512)S(1)} %get-tuple-element.260) | copy-start | bytes 6148
  266.6 12.2 %copy-start.48 = (f32[128]{0:T(128)}, f32[128]{0:T(128)S(1)}, u32[]{:S(2)}) copy-start(f32[128]{0:T(128)S(1)} %broadcast_multiply_fusion.2) | copy-start | bytes 1540
  266.9 12.0 %copy-start.53 = (f32[128]{0:T(128)}, f32[128]{0:T(128)S(1)}, u32[]{:S(2)}) copy-start(f32[128]{0:T(128)S(1)} %fusion.174) | copy-start | bytes 1540
  302.7 170.8 %all-to-all-start.3 = ((bf16[32,192,512]{2,1,0:T(8,128)(2,1)}), bf16[32,192,512]{2,1,0:T(8,128)(2,1)}, u32[]{:S(2)}, u32[]{:S(2)}) async-start(bf16[32,192,512]{2,1,0:T(8,128)(2,1)} %bitcast.434), calls=%async_computation.3 | async-start | bytes 12582912 | tf_op jit(solution)/shard_map/all_to_all | solution.py:338
  309.9 51.8 %copy-start.38 = (s32[8,1024]{1,0:T(8,128)S(1)}, s32[8,1024]{1,0:T(8,128)}, u32[]{:S(2)}) copy-start(s32[8,1024]{1,0:T(8,128)} %param.20) | copy-start | bytes 98308
  309.9 51.8 %slice-start.5 = ((f32[14336]{0:T(1024)}), f32[4096]{0:T(1024)S(1)}, s32[]{:S(2)}) async-start(f32[14336]{0:T(1024)} %param.26), calls=%async_computation.14 | async-start | bytes 32768 | tf_op jit(solution)/shard_map/slice | solution.py:73
  309.9 53.9 %copy-start.51 = (s32[896]{0:T(1024)S(1)}, s32[896]{0:T(1024)}, u32[]{:S(2)}) copy-start(s32[896]{0:T(1024)} %copy-done.50) | copy-start | bytes 10756
  310.0 186.5 %all-gather.11.cloned.1.call-start = ((), (), s32[]{:S(2)}) async-start(), calls=%async_computation.6 | async-start | bytes 4325376 | tf_op jit(solution)/shard_map/all_gather | solution.py:341
  361.6 158.6 %all-gather.9.cloned.1.call-start = ((), (), s32[]{:S(2)}) async-start(), calls=%async_computation.5 | async-start | bytes 1769472 | tf_op jit(solution)/shard_map/all_gather | solution.py:340
  486.5 98.8 %all-to-all-start.2 = ((bf16[32,64,512]{2,1,0:T(8,128)(2,1)}), bf16[32,64,512]{2,1,0:T(8,128)(2,1)}, u32[]{:S(2)}, u32[]{:S(2)}) async-start(bf16[32,64,512]{2,1,0:T(8,128)(2,1)} %bitcast.43), calls=%async_computation.2 | async-start | bytes 4194304 | tf_op jit(solution)/shard_map/all_to_all | solution.py:299
  496.1 232.6 %all-reduce.3.cloned.1.call-start = ((), (), s32[]{:S(2)}) async-start(), calls=%async_computation.7 | async-start | bytes 10485760 | tf_op jit(solution)/shard_map/psum | solution.py:348
  524.2 10.5 %copy-start.13 = (f32[2560,512]{1,0:T(8,128)}, f32[2560,512]{1,0:T(8,128)S(1)}, u32[]{:S(2)}) copy-start(f32[2560,512]{1,0:T(8,128)S(1)} %convert_add_fusion) | copy-start | bytes 15728644
  539.2 45.4 %copy-start.40 = (f32[14336]{0:T(1024)S(1)}, f32[14336]{0:T(1024)}, u32[]{:S(2)}) copy-start(f32[14336]{0:T(1024)} %param.26) | copy-start | bytes 172036
  539.2 45.4 %copy-start.43 = (f32[14336]{0:T(1024)S(1)}, f32[14336]{0:T(1024)}, u32[]{:S(2)}) copy-start(f32[14336]{0:T(1024)} %param.29) | copy-start | bytes 172036
  539.2 45.4 %copy-start.44 = (f32[14336]{0:T(1024)S(1)}, f32[14336]{0:T(1024)}, u32[]{:S(2)}) copy-start(f32[14336]{0:T(1024)} %param.28) | copy-start | bytes 172036
  539.2 45.4 %copy-start.45 = (f32[14336]{0:T(1024)S(1)}, f32[14336]{0:T(1024)}, u32[]{:S(2)}) copy-start(f32[14336]{0:T(1024)} %param.27) | copy-start | bytes 172036
  539.2 46.1 %copy-start.61 = (s32[2048]{0:T(1024)S(1)}, s32[2048]{0:T(1024)}, u32[]{:S(2)}) copy-start(s32[2048]{0:T(1024)} %copy-done.60) | copy-start | bytes 24580
  596.8 28.0 %copy-start.42 = (f32[8192]{0:T(1024)S(1)}, f32[8192]{0:T(1024)}, u32[]{:S(2)}) copy-start(f32[8192]{0:T(1024)} %get-tuple-element.270) | copy-start | bytes 98308
  (71 other events, 246.9 us)
Sparse Core Ops, SparseCore 0:
  11.4 106.4 all-gather.12
  273.4 84.1 all-gather.6
  361.7 101.0 all-gather.10
  478.1 42.0 all-gather.8
  539.4 189.2 all-reduce.2

commit v2 on v1

--- a/solution.py
+++ b/solution.py
@@ -4,6 +4,8 @@
 import jax
 import jax.numpy as jnp
 from jax import lax
+from jax.experimental import pallas as pl
+from jax.experimental.pallas import tpu as pltpu
 from jax.sharding import PartitionSpec as P
 
 D = 512
@@ -35,26 +37,6 @@
     return (3 * D, D, FF, FF, OUTW)
 
 
-def unpack(packed, narrow_count):
-    matrices = []
-    offset = 0
-    for row_total in matrix_rows():
-        height = row_total // narrow_count
-        matrices.append(packed[:, offset : offset + height, :].reshape(row_total, packed.shape[2]))
-        offset = offset + height
-    return matrices
-
-
-def pack(matrices, narrow_count):
-    return jnp.concatenate(
-        [
-            matrix.reshape(narrow_count, matrix.shape[0] // narrow_count, matrix.shape[1])
-            for matrix in matrices
-        ],
-        axis=1,
-    )
-
-
 def block_slices(block, narrow_count):
     segments = []
     offset = 0
@@ -119,6 +101,792 @@
 
 def gram_of(block):
     return lax.dot_general(block, block, (((0,), (0,)), ((), ())), precision=HIGHEST)
+
+
+MESH_ID = pl.DeviceIdType.MESH
+CORES = 2
+CHIPS = 4
+PLANES = 4
+MAIN = 192
+CHUNKS = 4
+CHUNK = MAIN // CHUNKS
+PROJ = 32
+PART = MAIN + PLANES * PROJ
+VROWS = 16
+
+
+def place():
+    wide_at = lax.axis_index("wide")
+    plane = lax.axis_index("narrow")
+    chip = wide_at // CORES
+    core = lax.rem(wide_at, CORES)
+    return wide_at, plane, chip, core
+
+
+def enter(targets):
+    barrier = pltpu.get_barrier_semaphore()
+    for target in targets:
+        pl.semaphore_signal(barrier, inc=1, device_id=target, device_id_type=MESH_ID)
+    pl.semaphore_wait(barrier, len(targets))
+
+
+def neighbours(wide_at, plane, chip, core):
+    sibling = (chip * CORES + 1 - core, plane)
+    chips = [(lax.rem(chip + k, CHIPS) * CORES + core, plane) for k in range(1, CHIPS)]
+    planes = [(wide_at, lax.rem(plane + k, PLANES)) for k in range(1, PLANES)]
+    return sibling, chips, planes
+
+
+def remote(src, dst, sems, index, target):
+    return pltpu.make_async_remote_copy(
+        src_ref=src,
+        dst_ref=dst,
+        send_sem=sems[0].at[index],
+        recv_sem=sems[1].at[index],
+        device_id=target,
+        device_id_type=MESH_ID,
+    )
+
+
+def reduce_kernel(
+    main_ref,
+    proj_ref,
+    vec_ref,
+    out_ref,
+    vec_out_ref,
+    near,
+    first,
+    far,
+    second,
+    deep,
+    proj_far,
+    part,
+    vec_near,
+    vec_far,
+    vec_deep,
+    load_sem,
+    main_send,
+    main_recv,
+    far_send,
+    far_recv,
+    deep_send,
+    deep_recv,
+    done_send,
+    done_recv,
+    pass_send,
+    pass_recv,
+    proj_send,
+    proj_recv,
+    vec_send,
+    vec_recv,
+):
+    wide_at, plane, chip, core = place()
+    sibling, chips, planes = neighbours(wide_at, plane, chip, core)
+    other = 1 - core
+    own_main = pltpu.make_async_copy(main_ref.at[core], first, load_sem.at[0])
+    own_main.start()
+    enter([sibling] + chips + planes)
+
+    vec_sems = (vec_send, vec_recv)
+    vec_copies = [remote(vec_ref.at[other], vec_near, vec_sems, 0, sibling)]
+    vec_copies[0].start()
+    main_sems = (main_send, main_recv)
+    near_copies = []
+    for chunk in range(CHUNKS):
+        copy = remote(main_ref.at[other, chunk], near.at[chunk], main_sems, chunk, sibling)
+        copy.start()
+        near_copies.append(copy)
+    proj_sems = (proj_send, proj_recv)
+    proj_copies = []
+    for k, target in enumerate(chips):
+        to_chip = lax.rem(chip + k + 1, CHIPS)
+        copy = remote(proj_ref.at[to_chip], proj_far.at[chip], proj_sems, k, target)
+        copy.start()
+        proj_copies.append(copy)
+    own_proj = pltpu.make_async_copy(proj_ref.at[chip], proj_far.at[chip], load_sem.at[1])
+    own_proj.start()
+    own_main.wait()
+
+    vec_copies[0].wait_recv()
+    vec_far[chip] = vec_ref[core] + vec_near[...]
+    for k, target in enumerate(chips):
+        copy = remote(vec_far.at[chip], vec_far.at[chip], vec_sems, 1 + k, target)
+        copy.start()
+        vec_copies.append(copy)
+
+    far_sems = (far_send, far_recv)
+    far_copies = []
+    for chunk in range(CHUNKS):
+        near_copies[chunk].wait_recv()
+
+        @pl.loop(0, CHIPS * PLANES)
+        def _(step, chunk=chunk):
+            q = step // PLANES
+            m = lax.rem(step, PLANES)
+            first[chunk, q, m] = (
+                first[chunk, q, m].astype(jnp.float32) + near[chunk, q, m].astype(jnp.float32)
+            ).astype(jnp.bfloat16)
+
+        copies = []
+        for k, target in enumerate(chips):
+            to_chip = lax.rem(chip + k + 1, CHIPS)
+            copy = remote(
+                first.at[chunk, to_chip],
+                far.at[chunk, k],
+                far_sems,
+                chunk * 3 + k,
+                target,
+            )
+            copy.start()
+            copies.append(copy)
+        far_copies.append(copies)
+
+    for copy in vec_copies[1:4]:
+        copy.wait()
+    vec_deep[plane] = (vec_far[0] + vec_far[1]) + (vec_far[2] + vec_far[3])
+    for k, target in enumerate(planes):
+        copy = remote(vec_deep.at[plane], vec_deep.at[plane], vec_sems, 4 + k, target)
+        copy.start()
+        vec_copies.append(copy)
+
+    deep_sems = (deep_send, deep_recv)
+    own_proj.wait()
+    for copy in proj_copies:
+        copy.wait()
+    proj_copies = []
+    for k, target in enumerate(planes):
+        to_plane = lax.rem(plane + k + 1, PLANES)
+        copy = remote(
+            proj_far.at[to_plane],
+            part.at[pl.ds(MAIN + plane * PROJ, PROJ)],
+            proj_sems,
+            3 + k,
+            target,
+        )
+        copy.start()
+        proj_copies.append(copy)
+    part[pl.ds(pl.multiple_of(MAIN + plane * PROJ, PROJ), PROJ), :] = proj_far[plane]
+
+    deep_copies = []
+    for chunk in range(CHUNKS):
+        for copy in far_copies[chunk]:
+            copy.wait_recv()
+
+        @pl.loop(0, PLANES)
+        def _(m, chunk=chunk):
+            total = first[chunk, chip, m].astype(jnp.float32)
+            for k in range(3):
+                total = total + far[chunk, k, m].astype(jnp.float32)
+            second[chunk, m] = total.astype(jnp.bfloat16)
+
+        copies = []
+        for k, target in enumerate(planes):
+            to_plane = lax.rem(plane + k + 1, PLANES)
+            copy = remote(
+                second.at[chunk, to_plane],
+                deep.at[chunk, k],
+                deep_sems,
+                chunk * 3 + k,
+                target,
+            )
+            copy.start()
+            copies.append(copy)
+        deep_copies.append(copies)
+
+    for copy in vec_copies[4:7]:
+        copy.wait()
+    vec_out_ref[core] = (vec_deep[0] + vec_deep[1]) + (vec_deep[2] + vec_deep[3])
+    copy = remote(vec_out_ref.at[core], vec_out_ref.at[core], vec_sems, 7, sibling)
+    copy.start()
+    vec_copies.append(copy)
+
+    done_sems = (done_send, done_recv)
+    done_copies = []
+    pieces = [(chunk * CHUNK, CHUNK) for chunk in range(CHUNKS)] + [(MAIN, PART - MAIN)]
+    for index, (offset, size) in enumerate(pieces):
+        rows = pl.ds(offset, size)
+        if index < CHUNKS:
+            for copy in deep_copies[index]:
+                copy.wait_recv()
+            total = second[index, plane].astype(jnp.float32)
+            for k in range(3):
+                total = total + deep[index, k].astype(jnp.float32)
+            part[rows, :] = total.astype(jnp.bfloat16)
+        else:
+            for copy in proj_copies:
+                copy.wait()
+        copies = []
+        for k, target in enumerate([sibling] + chips):
+            copy = remote(
+                part.at[rows], out_ref.at[wide_at, rows], done_sems, index * 4 + k, target
+            )
+            copy.start()
+            copies.append(copy)
+        done_copies.append(copies)
+    own_part = pltpu.make_async_copy(part, out_ref.at[wide_at], load_sem.at[2])
+    own_part.start()
+
+    pass_sems = (pass_send, pass_recv)
+    pass_copies = []
+    for index, (offset, size) in enumerate(pieces):
+        rows = pl.ds(offset, size)
+        for k in range(3):
+            done_copies[index][1 + k].wait_recv()
+            source = lax.rem(chip + CHIPS - 1 - k, CHIPS) * CORES + core
+            copy = remote(
+                out_ref.at[source, rows], out_ref.at[source, rows], pass_sems, index * 3 + k, sibling
+            )
+            copy.start()
+            pass_copies.append(copy)
+    own_part.wait()
+    for copies in done_copies:
+        copies[0].wait_recv()
+        for copy in copies:
+            copy.wait_send()
+    for copy in pass_copies:
+        copy.wait()
+    for copies in [near_copies] + far_copies + deep_copies:
+        for copy in copies:
+            copy.wait_send()
+    vec_copies[0].wait_send()
+    vec_copies[7].wait()
+
+
+def reduce_grads(main, proj, vec):
+    dma = pltpu.SemaphoreType.DMA
+    bf = jnp.bfloat16
+    return pl.pallas_call(
+        reduce_kernel,
+        out_shape=(
+            jax.ShapeDtypeStruct((CORES * CHIPS, PART, D), bf),
+            jax.ShapeDtypeStruct((CORES, VROWS, D), jnp.float32),
+        ),
+        in_specs=[
+            pl.BlockSpec(memory_space=pl.ANY),
+            pl.BlockSpec(memory_space=pl.ANY),
+            pl.BlockSpec(memory_space=pltpu.VMEM),
+        ],
+        out_specs=(
+            pl.BlockSpec(memory_space=pl.ANY),
+            pl.BlockSpec(memory_space=pltpu.VMEM),
+        ),
+        scratch_shapes=[
+            pltpu.VMEM((CHUNKS, CHIPS, PLANES, CHUNK, D), bf),
+            pltpu.VMEM((CHUNKS, CHIPS, PLANES, CHUNK, D), bf),
+            pltpu.VMEM((CHUNKS, 3, PLANES, CHUNK, D), bf),
+            pltpu.VMEM((CHUNKS, PLANES, CHUNK, D), bf),
+            pltpu.VMEM((CHUNKS, 3, CHUNK, D), bf),
+            pltpu.VMEM((CHIPS, PROJ, D), bf),
+            pltpu.VMEM((PART, D), bf),
+            pltpu.VMEM((VROWS, D), jnp.float32),
+            pltpu.VMEM((CHIPS, VROWS, D), jnp.float32),
+            pltpu.VMEM((PLANES, VROWS, D), jnp.float32),
+            dma((3,)),
+            dma((CHUNKS,)),
+            dma((CHUNKS,)),
+            dma((CHUNKS * 3,)),
+            dma((CHUNKS * 3,)),
+            dma((CHUNKS * 3,)),
+            dma((CHUNKS * 3,)),
+            dma(((CHUNKS + 1) * 4,)),
+            dma(((CHUNKS + 1) * 4,)),
+            dma(((CHUNKS + 1) * 3,)),
+            dma(((CHUNKS + 1) * 3,)),
+            dma((6,)),
+            dma((6,)),
+            dma((8,)),
+            dma((8,)),
+        ],
+        compiler_params=pltpu.CompilerParams(
+            collective_id=3, has_side_effects=True, vmem_limit_bytes=40 * 2**20
+        ),
+        name="reduce_grads",
+    )(main, proj, vec)
+
+
+TILE = 128
+STRIP = D // PLANES
+OWNERS = (6, 7, 2, 4, 0)
+BLOCK_TILES = (3, 1, 4, 4, 8)
+MOST_TILES = max(BLOCK_TILES)
+
+
+def halves(value):
+    high = value.astype(jnp.bfloat16)
+    return high, (value - high.astype(jnp.float32)).astype(jnp.bfloat16)
+
+
+def plain_dot(left, right):
+    return jnp.dot(left, right, preferred_element_type=jnp.float32)
+
+
+def split_dot(left, right):
+    return plain_dot(left[0], right[0]) + (
+        plain_dot(left[0], right[1]) + plain_dot(left[1], right[0])
+    )
+
+
+def newton_kernel(
+    grad_ref,
+    momentum_ref,
+    out_ref,
+    grad_tiles,
+    momentum_tiles,
+    update_high,
+    update_low,
+    gram,
+    poly,
+    chain,
+    pieces,
+    rows_out,
+    load_sem,
+    gram_send,
+    gram_recv,
+    sum_send,
+    sum_recv,
+    rows_send,
+    rows_recv,
+    pass_send,
+    pass_recv,
+    local_sem,
+):
+    wide_at, plane, chip, core = place()
+    sibling, chips, planes = neighbours(wide_at, plane, chip, core)
+    tile_count = jnp.int32(0)
+    tile_first = jnp.int32(0)
+    begin = 0
+    for owner, count in zip(OWNERS, BLOCK_TILES):
+        tile_count = tile_count + jnp.where(wide_at == owner, count, 0)
+        tile_first = tile_first + jnp.where(wide_at == owner, begin, 0)
+        begin = begin + count
+    owning = tile_count > 0
+
+    def tile_rows(tile):
+        return pl.ds(pl.multiple_of(tile * TILE, TILE), TILE)
+
+    def loads(tile):
+        source = tile_rows(tile_first + tile)
+        return (
+            pltpu.make_async_copy(grad_ref.at[source], grad_tiles.at[tile], load_sem.at[0, tile]),
+            pltpu.make_async_copy(
+                momentum_ref.at[source], momentum_tiles.at[tile], load_sem.at[1, tile]
+            ),
+        )
+
+    @pl.loop(0, tile_count)
+    def _(tile):
+        for copy in loads(tile):
+            copy.start()
+
+    enter([sibling] + chips + planes)
+
+    gram_sems = (gram_send, gram_recv)
+    sum_sems = (sum_send, sum_recv)
+
+    def transposed_dot(left, right):
+        return lax.dot_general(
+            left, right, (((0,), (0,)), ((), ())), preferred_element_type=jnp.float32
+        )
+
+    @pl.when(owning)
+    def _():
+        gram[...] = jnp.zeros_like(gram)
+        poly[...] = jnp.zeros_like(poly)
+
+        @pl.loop(0, tile_count)
+        def _(tile):
+            for copy in loads(tile):
+                copy.wait()
+            update = grad_tiles[tile] + MUON_BETA * momentum_tiles[tile]
+            high, low = halves(update)
+            update_high[tile] = high
+            update_low[tile] = low
+            gram[...] += transposed_dot(high, high)
+            poly[...] += transposed_dot(high, low)
+
+        gram[...] += poly[...] + poly[...].T
+        copies = []
+        for k, target in enumerate(planes):
+            to_plane = lax.rem(plane + k + 1, PLANES)
+            copy = remote(
+                gram.at[pl.ds(pl.multiple_of(to_plane * STRIP, STRIP), STRIP)],
+                pieces.at[plane],
+                gram_sems,
+                k,
+                target,
+            )
+            copy.start()
+            copies.append(copy)
+        own_strip = pl.ds(pl.multiple_of(plane * STRIP, STRIP), STRIP)
+        pieces[plane] = gram[own_strip, :]
+        for copy in copies:
+            copy.wait()
+        chain[own_strip, :] = (pieces[0] + pieces[1]) + (pieces[2] + pieces[3])
+        copies = []
+        for k, target in enumerate(planes):
+            copy = remote(chain.at[own_strip], chain.at[own_strip], sum_sems, k, target)
+            copy.start()
+            copies.append(copy)
+        for copy in copies:
+            copy.wait()
+
+        diagonal = lax.broadcasted_iota(jnp.int32, (D, D), 0) == lax.broadcasted_iota(
+            jnp.int32, (D, D), 1
+        )
+        square = jnp.sum(jnp.where(diagonal, chain[...], 0.0))
+        norm = jnp.sqrt(jnp.full((1, 1), square)) + 1e-07
+        inverse = 1.0 / norm
+        gram[...] = chain[...] * (inverse * inverse)
+
+        def make_poly():
+            value = gram[...]
+            parts = halves(value)
+            diagonal = lax.broadcasted_iota(jnp.int32, (D, D), 0) == lax.broadcasted_iota(
+                jnp.int32, (D, D), 1
+            )
+            poly[...] = (
+                NEWTON_B * value
+                + NEWTON_C * split_dot(parts, parts)
+                + jnp.where(diagonal, NEWTON_A, 0.0)
+            )
+
+        def next_gram():
+            parts = halves(poly[...])
+            half_way = split_dot(halves(gram[...]), parts)
+            gram[...] = split_dot(halves(half_way), parts)
+
+        def extend():
+            chain[...] = split_dot(halves(chain[...]), halves(poly[...]))
+
+        make_poly()
+        chain[...] = poly[...]
+        next_gram()
+
+        @pl.loop(0, 3)
+        def _(sweep):
+            make_poly()
+            extend()
+            next_gram()
+
+        make_poly()
+        extend()
+        chain_parts = halves(chain[...] * inverse)
+
+        @pl.loop(0, tile_count)
+        def _(tile):
+            rows_out[tile] = split_dot((update_high[tile], update_low[tile]), chain_parts).astype(
+                jnp.bfloat16
+            )
+
+    row_sems = (rows_send, rows_recv)
+    pass_sems = (pass_send, pass_recv)
+    begin = 0
+    for index, (owner, count) in enumerate(zip(OWNERS, BLOCK_TILES)):
+        owner_chip, owner_core = divmod(owner, CORES)
+        span = pl.ds(begin, count)
+        begin = begin + count
+
+        @pl.when(wide_at == owner)
+        def _(index=index, count=count, span=span):
+            for k, target in enumerate(chips + [sibling]):
+                remote(
+                    rows_out.at[pl.ds(0, count)], out_ref.at[span], row_sems, index * 4 + k, target
+                ).start()
+            pltpu.make_async_copy(
+                rows_out.at[pl.ds(0, count)], out_ref.at[span], local_sem.at[0]
+            ).start()
+
+    begin = 0
+    for index, (owner, count) in enumerate(zip(OWNERS, BLOCK_TILES)):
+        owner_chip, owner_core = divmod(owner, CORES)
+        span = pl.ds(begin, count)
+        begin = begin + count
+        for k in range(3):
+            receiver = (owner_chip + k + 1) % CHIPS * CORES + owner_core
+
+            @pl.when(wide_at == receiver)
+            def _(index=index, span=span, k=k):
+                remote(
+                    out_ref.at[span], out_ref.at[span], row_sems, index * 4 + k, sibling
+                ).wait_recv()
+                remote(out_ref.at[span], out_ref.at[span], pass_sems, index, sibling).start()
+
+    begin = 0
+    for index, (owner, count) in enumerate(zip(OWNERS, BLOCK_TILES)):
+        owner_chip, owner_core = divmod(owner, CORES)
+        span = pl.ds(begin, count)
+        begin = begin + count
+
+        @pl.when(wide_at == owner)
+        def _(index=index, count=count, span=span):
+            for k, target in enumerate(chips + [sibling]):
+                remote(
+                    rows_out.at[pl.ds(0, count)], out_ref.at[span], row_sems, index * 4 + k, target
+                ).wait_send()
+            pltpu.make_async_copy(
+                rows_out.at[pl.ds(0, count)], out_ref.at[span], local_sem.at[0]
+            ).wait()
+
+        @pl.when((core == owner_core) & (chip != owner_chip))
+        def _(index=index, span=span):
+            remote(out_ref.at[span], out_ref.at[span], pass_sems, index, sibling).wait_send()
+
+        @pl.when((core != owner_core) & (chip != owner_chip))
+        def _(index=index, span=span):
+            remote(out_ref.at[span], out_ref.at[span], pass_sems, index, sibling).wait_recv()
+
+        @pl.when((core != owner_core) & (chip == owner_chip))
+        def _(index=index, span=span):
+            remote(
+                out_ref.at[span], out_ref.at[span], row_sems, index * 4 + 3, sibling
+            ).wait_recv()
+
+
+def newton_rows(grad_block, momentum_block):
+    dma = pltpu.SemaphoreType.DMA
+    tiles = grad_block.shape[0] // TILE
+    scratch = [
+        pltpu.VMEM((MOST_TILES, TILE, D), jnp.float32),
+        pltpu.VMEM((MOST_TILES, TILE, D), jnp.float32),
+        pltpu.VMEM((MOST_TILES, TILE, D), jnp.bfloat16),
+        pltpu.VMEM((MOST_TILES, TILE, D), jnp.bfloat16),
+        pltpu.VMEM((D, D), jnp.float32),
+        pltpu.VMEM((D, D), jnp.float32),
+        pltpu.VMEM((D, D), jnp.float32),
+        pltpu.VMEM((PLANES, STRIP, D), jnp.float32),
+        pltpu.VMEM((MOST_TILES, TILE, D), jnp.bfloat16),
+        dma((2, MOST_TILES)),
+        dma((3,)),
+        dma((3,)),
+        dma((3,)),
+        dma((3,)),
+        dma((20,)),
+        dma((20,)),
+        dma((5,)),
+        dma((5,)),
+        dma((1,)),
+    ]
+    return pl.pallas_call(
+        newton_kernel,
+        out_shape=jax.ShapeDtypeStruct((tiles, TILE, D), jnp.bfloat16),
+        in_specs=[pl.BlockSpec(memory_space=pl.ANY)] * 2,
+        out_specs=pl.BlockSpec(memory_space=pl.ANY),
+        scratch_shapes=scratch,
+        compiler_params=pltpu.CompilerParams(
+            collective_id=4, has_side_effects=True, vmem_limit_bytes=48 * 2**20
+        ),
+        name="newton_rows",
+    )(grad_block, momentum_block).reshape(grad_block.shape)
+
+
+def spread_kernel(count, *refs):
+    own = refs[:count]
+    outs = refs[count : 2 * count]
+    local_sem, send_sem, recv_sem = refs[2 * count :]
+    wide_at, plane, chip, core = place()
+    sibling, chips, planes = neighbours(wide_at, plane, chip, core)
+    enter([sibling] + chips + planes)
+    sems = (send_sem, recv_sem)
+    pending = []
+    firsts = []
+
+    def send(src, dst, index, target):
+        copy = remote(src, dst, sems, index, target)
+        copy.start()
+        pending.append(copy)
+        return copy
+
+    for item in range(count):
+        base = item * 31
+        spot = outs[item].at[plane, wide_at]
+        local = pltpu.make_async_copy(own[item], spot, local_sem.at[item])
+        local.start()
+        pending.append(local)
+        from_planes = [send(own[item], spot, base + k, planes[k]) for k in range(3)]
+        from_chips = [send(own[item], spot, base + 3 + k, chips[k]) for k in range(3)]
+        send(own[item], spot, base + 6, sibling)
+        firsts.append((from_planes, [from_chips]))
+    for k in range(3):
+        for item in range(count):
+            base = item * 31 + 7 + k * 4
+            from_planes, from_chips = firsts[item]
+            from_planes[k].wait_recv()
+            spot = outs[item].at[lax.rem(plane + PLANES - 1 - k, PLANES), wide_at]
+            from_chips.append([send(spot, spot, base + j, chips[j]) for j in range(3)])
+            send(spot, spot, base + 3, sibling)
+    for step in range(PLANES):
+        for item in range(count):
+            base = item * 31 + 19 + step * 3
+            source_plane = plane if step == 0 else lax.rem(plane + PLANES - step, PLANES)
+            for j in range(3):
+                firsts[item][1][step][j].wait_recv()
+                source = lax.rem(chip + CHIPS - 1 - j, CHIPS) * CORES + core
+                spot = outs[item].at[source_plane, source]
+                send(spot, spot, base + j, sibling)
+    received = {id(copy) for from_planes, _ in firsts for copy in from_planes}
+    received |= {id(copy) for _, groups in firsts for group in groups for copy in group}
+    for copy in pending:
+        if id(copy) in received:
+            copy.wait_send()
+        else:
+            copy.wait()
+
+
+def spread(parts, collective_id, name):
+    dma = pltpu.SemaphoreType.DMA
+    count = len(parts)
+    return pl.pallas_call(
+        partial(spread_kernel, count),
+        out_shape=tuple(
+            jax.ShapeDtypeStruct((PLANES, CHIPS * CORES) + part.shape, part.dtype)
+            for part in parts
+        ),
+        in_specs=[pl.BlockSpec(memory_space=pl.ANY)] * count,
+        out_specs=tuple(pl.BlockSpec(memory_space=pl.ANY) for _ in parts),
+        scratch_shapes=[dma((count,)), dma((31 * count,)), dma((31 * count,))],
+        compiler_params=pltpu.CompilerParams(collective_id=collective_id, has_side_effects=True),
+        name=name,
+    )(*parts)
+
+
+def tell_kernel(own_ref, out_ref, send_sem, recv_sem):
+    wide_at, plane, chip, core = place()
+    wide_count = CHIPS * CORES
+    peers = [
+        (lax.rem(wide_at + k // PLANES, wide_count), lax.rem(plane + k % PLANES, PLANES))
+        for k in range(1, wide_count * PLANES)
+    ]
+    enter(peers)
+    spot = out_ref.at[wide_at * PLANES + plane]
+    copies = [
+        remote(own_ref, spot, (send_sem, recv_sem), k, target) for k, target in enumerate(peers)
+    ]
+    for copy in copies:
+        copy.start()
+    out_ref[wide_at * PLANES + plane] = own_ref[...]
+    for copy in copies:
+        copy.wait()
+
+
+def tell(values, collective_id):
+    dma = pltpu.SemaphoreType.DMA
+    every = PLANES * CHIPS * CORES
+    return pl.pallas_call(
+        tell_kernel,
+        out_shape=jax.ShapeDtypeStruct((every,) + values.shape, values.dtype),
+        in_specs=[pl.BlockSpec(memory_space=pltpu.VMEM)],
+        out_specs=pl.BlockSpec(memory_space=pltpu.VMEM),
+        scratch_shapes=[dma((every - 1,)), dma((every - 1,))],
+        compiler_params=pltpu.CompilerParams(collective_id=collective_id, has_side_effects=True),
+        name="tell_ids",
+    )(values)
+
+
+def meshed():
+    return lax.axis_size("wide") == CHIPS * CORES and lax.axis_size("narrow") == PLANES
+
+
+def gather_weights(mat_master):
+    narrow_count = lax.axis_size("narrow")
+    wide_count = lax.axis_size("wide")
+    wide_at = lax.axis_index("wide")
+    gathered = []
+    for segment in block_slices(mat_master[0], narrow_count):
+        rows = segment.shape[0] // wide_count
+        own_part = lax.dynamic_slice_in_dim(segment, wide_at * rows, rows, 0)
+        gathered.append(
+            lax.all_gather(own_part.astype(jnp.bfloat16), ("narrow", "wide"), axis=0, tiled=True)
+        )
+    return gathered
+
+
+def gather_ids(slot_ids):
+    if not meshed():
+        return lax.all_gather(slot_ids, BOTH, axis=0, tiled=False)
+    count = slot_ids.shape[0]
+    lanes = 128
+    rows = -(-count // (8 * lanes)) * 8
+    padded = jnp.pad(slot_ids, (0, rows * lanes - count)).reshape(rows, lanes)
+    every = tell(padded, 1)
+    return every.reshape(every.shape[0], rows * lanes)[:, :count]
+
+
+def gather_entries(rows):
+    if not meshed():
+        return lax.all_gather(rows, BOTH, axis=0, tiled=True)
+    (every,) = spread([rows], 2, "spread_entries")
+    return every.transpose(1, 0, 2, 3).reshape(-1, rows.shape[1])
+
+
+def total_grads(matrices, grad_proj_own, vec_local):
+    narrow_count = lax.axis_size("narrow")
+    wide_count = lax.axis_size("wide")
+    narrow_at = lax.axis_index("narrow")
+    packed_term = jnp.concatenate(
+        [
+            matrix.reshape(narrow_count, wide_count, -1, D).astype(jnp.bfloat16)
+            for matrix in matrices
+        ],
+        axis=2,
+    )
+    proj_bf = grad_proj_own.astype(jnp.bfloat16)
+    if meshed():
+        main = packed_term.reshape(PLANES, CHIPS, CORES, CHUNKS, CHUNK, D)
+        main = main.transpose(2, 3, 1, 0, 4, 5)
+        vec_rows = CORES * VROWS
+        vec_in = jnp.pad(vec_local.reshape(-1, D), ((0, vec_rows - vec_local.shape[0] // D), (0, 0)))
+        parts, vec_sum = reduce_grads(
+            main, proj_bf.reshape(CHIPS, PROJ, D), vec_in.reshape(CORES, VROWS, D)
+        )
+        vec_grad = vec_sum.reshape(-1)[: vec_local.shape[0]]
+        segments = []
+        offset = 0
+        for matrix in matrices:
+            height = matrix.shape[0] // (narrow_count * wide_count)
+            segments.append(parts[:, offset : offset + height].reshape(-1, D))
+            offset = offset + height
+        proj = parts[:, MAIN:].reshape(CHIPS, CORES, PLANES, PROJ, D)
+        segments.append(proj.transpose(1, 2, 0, 3, 4).reshape(-1, D))
+        return jnp.concatenate(segments, axis=0).astype(jnp.float32), vec_grad
+    vec_grad = lax.psum(vec_local, BOTH)
+    share = packed_term.shape[2]
+    terms = lax.all_to_all(
+        packed_term.transpose(1, 0, 2, 3).reshape(-1, share, D), BOTH, 0, 0, tiled=True
+    )
+    share_sum = jnp.sum(terms.astype(jnp.float32), axis=0)
+    parts = lax.all_gather(share_sum.astype(jnp.bfloat16), "wide", axis=0, tiled=False)
+    segments = []
+    offset = 0
+    for matrix in matrices:
+        height = matrix.shape[0] // (narrow_count * wide_count)
+        segments.append(parts[:, offset : offset + height].reshape(-1, D))
+        offset = offset + height
+    proj_grad = lax.all_gather(proj_bf, BOTH, axis=0, tiled=True)
+    proj_rows = OUTW // narrow_count
+    segments.append(lax.dynamic_slice_in_dim(proj_grad, narrow_at * proj_rows, proj_rows, 0))
+    return jnp.concatenate(segments, axis=0).astype(jnp.float32), vec_grad
+
+
+def orthogonal_rows(grad_block, momentum_block):
+    if meshed():
+        return newton_rows(grad_block, momentum_block)
+    narrow_count = lax.axis_size("narrow")
+    segments = block_slices(grad_block + MUON_BETA * momentum_block, narrow_count)
+    grams = lax.psum(jnp.stack([gram_of(segment) for segment in segments]), "narrow")
+    rows = []
+    for position, segment in enumerate(segments):
+        square = jnp.sum(jnp.diagonal(grams[position]))
+        norm = jnp.sqrt(square) + 1e-07
+        gram = grams[position] / (norm * norm)
+        chain = None
+        for sweep_index in range(5):
+            squared = jnp.dot(gram, gram, precision=HIGH)
+            poly = NEWTON_B * gram + NEWTON_C * squared + NEWTON_A * jnp.eye(D, dtype=jnp.float32)
+            chain = poly if chain is None else jnp.dot(chain, poly, precision=HIGH)
+            if sweep_index < 4:
+                gram = jnp.dot(jnp.dot(gram, poly, precision=HIGH), poly, precision=HIGH)
+        rows.append(jnp.dot(segment / norm, chain, precision=HIGH))
+    return jnp.concatenate(rows, axis=0)
 
 
 def on_device(
@@ -142,13 +910,7 @@
     wide_at = lax.axis_index("wide")
     narrow_at = lax.axis_index("narrow")
     me = wide_at * narrow_count + narrow_at
-    block_rows = mat_master.shape[1]
-    own_rows = block_rows // wide_count
-    own_part = lax.dynamic_slice_in_dim(mat_master[0], wide_at * own_rows, own_rows, 0)
-    packed_bf = lax.all_gather(
-        own_part.astype(jnp.bfloat16), ("narrow", "wide"), axis=0, tiled=True
-    ).reshape(narrow_count, block_rows, D)
-    w_qkv, w_out, w_up, w_down, w_proj = unpack(packed_bf, narrow_count)
+    w_qkv, w_out, w_up, w_down, w_proj = gather_weights(mat_master)
     (
         cls_vec,
         positions,
@@ -167,7 +929,7 @@
     slot_count = slot_ids.shape[0]
     group_rows = piece_table.shape[0]
     cap = piece_cap(group_rows)
-    every_ids = lax.all_gather(slot_ids, BOTH, axis=0, tiled=False)
+    every_ids = gather_ids(slot_ids)
     asked = every_ids // group_rows == me
     before = (
         lax.broadcasted_iota(jnp.int32, (slot_count, slot_count), 0)
@@ -252,7 +1014,7 @@
     )
     normed_three, norm3_pull = jax.vjp(layer_norm, second_residual, final_gain, final_shift)
     normed_three_bf = normed_three.astype(jnp.bfloat16)
-    every_normed = lax.all_gather(normed_three_bf, BOTH, axis=0, tiled=True)
+    every_normed = gather_entries(normed_three_bf)
     proj_own = lax.dynamic_slice_in_dim(w_proj, me * feature_rows, feature_rows, 0)
     bias_own = lax.dynamic_slice_in_dim(bias_out, me * feature_rows, feature_rows, 0)
     table_cols = (
@@ -318,54 +1080,20 @@
             ),
         ]
     )
-    vec_grad = lax.psum(vec_local, BOTH)
     grad_qkv = jnp.concatenate([grad_q_w, grad_kv_w], axis=0)
-    packed_term = jnp.concatenate(
+    grad_block, vec_grad = total_grads(
+        (grad_qkv, grad_out_w, grad_up, grad_down), grad_proj_own, vec_local
+    )
+    momentum_block = MUON_BETA * mat_momentum[0] + grad_block
+    ortho = orthogonal_rows(grad_block, momentum_block).astype(jnp.float32)
+    row_scale = jnp.concatenate(
         [
-            matrix.reshape(narrow_count, matrix.shape[0] // narrow_count, D)
-            for matrix in (grad_qkv, grad_out_w, grad_up, grad_down)
+            jnp.full((row_total // narrow_count, 1), MUON_RATE * math.sqrt(row_total / D))
+            for row_total in matrix_rows()
         ],
-        axis=1,
-    )
-    term_rows = packed_term.shape[1]
-    share = term_rows // wide_count
-    packed_term = (
-        packed_term.astype(jnp.bfloat16)
-        .reshape(narrow_count, wide_count, share, D)
-        .transpose(1, 0, 2, 3)
-        .reshape(device_count, share, D)
-    )
-    terms = lax.all_to_all(packed_term, BOTH, 0, 0, tiled=True)
-    share_sum = jnp.sum(terms.astype(jnp.float32), axis=0)
-    main_grad = lax.all_gather(share_sum.astype(jnp.bfloat16), "wide", axis=0, tiled=True)
-    proj_grad = lax.all_gather(grad_proj_own.astype(jnp.bfloat16), BOTH, axis=0, tiled=True)
-    proj_rows = OUTW // narrow_count
-    proj_grad = lax.dynamic_slice_in_dim(proj_grad, narrow_at * proj_rows, proj_rows, 0)
-    grad_block = jnp.concatenate([main_grad, proj_grad], axis=0).astype(jnp.float32)
-    momentum_block = MUON_BETA * mat_momentum[0] + grad_block
-    update_block = grad_block + MUON_BETA * momentum_block
-    segments = block_slices(update_block, narrow_count)
-    grams = lax.psum(jnp.stack([gram_of(segment) for segment in segments]), "narrow")
-    new_segments = []
-    for position, (row_total, master_seg, segment) in enumerate(
-        zip(matrix_rows(), block_slices(mat_master[0], narrow_count), segments)
-    ):
-        square = jnp.sum(jnp.diagonal(grams[position]))
-        norm = jnp.sqrt(square) + 1e-07
-        gram = grams[position] / (norm * norm)
-        chain = None
-        for sweep_index in range(5):
-            squared = jnp.dot(gram, gram, precision=HIGH)
-            poly = NEWTON_B * gram + NEWTON_C * squared + NEWTON_A * jnp.eye(D, dtype=jnp.float32)
-            chain = poly if chain is None else jnp.dot(chain, poly, precision=HIGH)
-            if sweep_index < 4:
-                gram = jnp.dot(jnp.dot(gram, poly, precision=HIGH), poly, precision=HIGH)
-        ortho = jnp.dot(segment / norm, chain, precision=HIGH)
-        new_segments.append(
-            master_seg * (1.0 - MUON_RATE * MUON_DECAY)
-            - MUON_RATE * math.sqrt(row_total / D) * ortho
-        )
-    weight_block = jnp.concatenate(new_segments, axis=0)[None]
+        axis=0,
+    ).astype(jnp.float32)
+    weight_block = (mat_master[0] * (1.0 - MUON_RATE * MUON_DECAY) - row_scale * ortho)[None]
     ema_block = EMA_DECAY * mat_ema + (1.0 - EMA_DECAY) * weight_block
     moment_one = ADAM_BETA1 * vec_moment1 + (1.0 - ADAM_BETA1) * vec_grad
     moment_two = ADAM_BETA2 * vec_moment2 + (1.0 - ADAM_BETA2) * vec_grad * vec_grad

time: 921 us -> 628 us (0.68)
  the two profiles are of different devices: /device:TPU:31 before, /device:TPU:29 now
where the time goes in v2:
time: 628 us; the launch traced here: 620 us
  Pallas kernels  236 us (38%)
  matrix products  97.3 us (15%)
  local copies, waits for them, and re-layouts  88.9 us (14%)
  blocking collectives  66.5 us (11%)
  other arithmetic  55 us (9%)
  waiting for transfers between devices  41.3 us (7%)
  starting transfers between devices  18.8 us (3%)
  between operations  15.5 us (2%)
    pallas_call x1, Pallas kernels, newton_rows(): pl.pallas_call(newton_kernel, out_shape=jax.ShapeDtypeStruct((tiles, TILE...  118 us
    all_gather x1, blocking collectives, gather_weights(): lax.all_gather(own_part.astype(jnp.bfloat16), ('narrow', 'wide'), axis=0,...  66.5 us
    pallas_call x1, Pallas kernels, reduce_grads(): pl.pallas_call(reduce_kernel, out_shape=(jax.ShapeDtypeStruct((CORES * CH...  59.5 us
    dot_general x16, matrix products, text_block(): lax.dot_general(masked_cot, onehot, (((1,), (1,)), ((), ())), preferred_e...  46.7 us
    all_gather x4, waiting for transfers between devices, gather_weights(): lax.all_gather(own_part.astype(jnp.bfloat16), ('narrow', 'wide'), axis=0,...  41.2 us
    pallas_call x1, Pallas kernels, spread(): pl.pallas_call(partial(spread_kernel, count), out_shape=tuple((jax.ShapeD...  30.4 us
    pallas_call x1, Pallas kernels, tell(): pl.pallas_call(tell_kernel, out_shape=jax.ShapeDtypeStruct((every,) + val...  28.5 us
    gather x1, local copies, waits for them, and re-layouts, on_device(): jnp.take(table_cols, flat_ids, axis=1)  28 us
  transfers between devices with their start and end apart: 7, of which 1 were waited for; matrix products, arithmetic and copies ran while one was open for 19% of the time, Pallas kernels for 24%

profile of v2, /device:TPU:29, one launch (start us, length us, event | category | flops | bytes accessed | tf_op | source)
XLA Modules:
  0.0 620.0 jit_solution(6231636701163848235)
XLA Ops:
  13.0 49.7 %while.15 = (s32[]{:T(128)}, f32[128,4096]{1,0:T(8,128)S(1)}, s32[8192]{0:T(1024)S(1)}, bf16[128,8192]{1,0:T(8,128)(2,1)}, s32[8192]{0:T(1024)S(1)}, /*index=5*/s32[]{:T(128)}, s32[]{:T(128)}, s32[]{:T(128)}, s32[]{:T(128)}) while((s32[]{:T(128)}, f32[128,4096]{1,0:T(8,128)S(1)}, s32[8192]{0:T(1024)S(1)}, ...), condition=%wide.region_11.12_spmd.clone, body=%wide.region_10.11_spmd.clone.sunk | while | flops 540082688 | bytes 4334761 | solution.py:981
  64.0 6.2 all-to-all-start.1
  72.9 28.5 %tell_ids.1 = s32[32,8,128]{2,1,0:T(8,128)} custom-call(s32[8,128]{1,0:T(8,128)} %pad_bitcast_fusion.own_ref), custom_call_target="tpu_custom_call" | custom-call | tf_op jit(solution)/shard_map/tell_ids/pallas_call | solution.py:774
  103.7 3.6 fusion.26
  107.3 6.4 %all-to-all-start = ((bf16[32,64,512]{2,1,0:T(8,128)(2,1)}), bf16[32,64,512]{2,1,0:T(8,128)(2,1)}, u32[]{:S(2)}, u32[]{:S(2)}) async-start(bf16[32,64,512]{2,1,0:T(8,128)(2,1)} %bitcast.237), calls=%async_computation | async-start | bytes 4194304 | tf_op jit(solution)/shard_map/all_to_all | solution.py:949
  123.8 66.5 %all-gather.2 = bf16[1,512,512]{2,1,0:T(8,128)(2,1)S(1)} all-gather(bf16[1,16,512]{2,1,0:T(8,128)(2,1)S(1)} %dynamic-slice_convert_fusion.4), channel_id=4, replica_groups=mesh['wide'=8,'narrow'=4] {'narrow','wide'}, dimensions={1}, use_global_device_ids=true | all-gather | bytes 540672 | tf_op jit(solution)/shard_map/all_gather | solution.py:798
  191.6 3.7 fusion.37
  220.7 41.2 %all-gather.10.cloned.1.call-done = bf16[1,4096,512]{2,1,0:T(8,128)(2,1)} async-done(((bf16[1,128,512]{2,1,0:T(8,128)(2,1)}), bf16[1,4096,512]{2,1,0:T(8,128)(2,1)}) %all-gather.10.cloned.1.call-update) | async-done | bytes 4194320 | tf_op jit(solution)/shard_map/all_gather | solution.py:798
  261.9 4.0 multiply_reduce_fusion.7
  287.4 4.3 bitcast_convert_fusion
  297.8 30.4 %spread_entries.1 = bf16[4,8,128,512]{3,2,1,0:T(8,128)(2,1)} custom-call(bf16[128,512]{1,0:T(8,128)(2,1)} %get-tuple-element.246.refs_0_), custom_call_target="tpu_custom_call" | custom-call | tf_op jit(solution)/shard_map/spread_entries/pallas_call | solution.py:738
  328.3 4.7 copy.80
  336.2 3.5 copy.142
  345.7 59.5 %reduce_grads.1 = (bf16[8,320,512]{2,1,0:T(8,128)(2,1)S(1)}, f32[2,16,512]{2,1,0:T(8,128)S(1)}) custom-call(bf16[2,4,4,4,48,512]{5,4,3,2,1,0:T(8,128)(2,1)S(1)} %bitcast.205, bf16[4,32,512]{2,1,0:T(8,128)(2,1)S(1)} %bitcast.207, f32[2,16,512]{2,1,0:T(8,128)S(1)} %bitcast.208), custom_call_target="tpu_custom_call" | custom-call | tf_op jit(solution)/shard_map/reduce_grads/pallas_call | solution.py:358
  408.0 3.7 convolution_add_fusion
  413.7 28.0 %gather_fusion = f32[8192,128]{1,0:T(8,128)} fusion(f32[128,4096]{0,1:T(8,128)S(1)} %copy.81, s32[8192]{0:T(1024)S(1)} %copy-done.30), kind=kCustom, calls=%fused_computation | custom fusion | bytes 8421376 | tf_op jit(solution)/shard_map/jit(_take)/gather | solution.py:1024
  441.7 9.7 %multiply_bitcast_fusion = f32[128,8192]{0,1:T(8,128)} fusion(f32[8192,128]{1,0:T(8,128)} %gather_fusion, f32[8192]{0:T(1024)S(1)} %copy-done.29, pred[8192]{0:T(1024)(128)(4,1)S(1)} %copy-done.41), kind=kLoop, calls=%fused_computation.33 | loop fusion | flops 2097152 | bytes 8429568 | tf_op jit(solution)/shard_map/mul | solution.py:1024
  451.3 5.7 copy.93
  457.9 3.9 fusion.27
  461.7 6.2 all-to-all-start.2
  473.3 3.4 bitcast_add_fusion.momentum_ref
  476.7 117.8 %newton_rows.1 = bf16[20,128,512]{2,1,0:T(8,128)(2,1)S(1)} custom-call(f32[2560,512]{1,0:T(8,128)} %convert_element_type.221.grad_ref, f32[2560,512]{1,0:T(8,128)} %bitcast_add_fusion.momentum_ref), custom_call_target="tpu_custom_call" | custom-call | tf_op jit(solution)/shard_map/newton_rows/pallas_call | solution.py:669
  597.0 10.4 %multiply_add_fusion = (f32[1,2560,512]{2,1,0:T(8,128)}, f32[1,2560,512]{2,1,0:T(8,128)}, f32[1,2560,512]{2,1,0:T(8,128)}, f32[1,2560,512]{2,1,0:T(8,128)}) fusion(f32[1,2560,512]{2,1,0:T(8,128)} %param.25, f32[2560]{0:T(1024)S(1)} %copy-done.55, f32[1,2560,512]{2,1,0:T(8,128)S(1)} %bitcast.219, bf16[1,2560,512]{2,1,0:T(8,128)(2,1)} %copy-done.15, ...), kind=kLoop, calls=%fused_computation.28 | loop fusion | flops 13107200 | bytes 41953280 | tf_op jit(solution)/shard_map/add | solution.py:1097
  607.4 5.8 fusion.11
  (382 shorter events, 147.3 us)
Async XLA Ops:
  7.2 96.5 %copy-start = (bf16[1024,512]{1,0:T(8,128)(2,1)S(1)}, bf16[1024,512]{1,0:T(8,128)(2,1)}, u32[]{:S(2)}) copy-start(bf16[1024,512]{1,0:T(8,128)(2,1)} %param.17) | copy-start | bytes 3145732
  7.2 184.4 %all-gather.12.cloned.1.call-start = ((), (), s32[]{:S(2)}) async-start(), calls=%async_computation.4 | async-start | bytes 1622016 | tf_op jit(solution)/shard_map/all_gather | solution.py:798
  9.2 204.7 %all-gather.14.cloned.1.call-start = ((), (), s32[]{:S(2)}) async-start(), calls=%async_computation.5 | async-start | bytes 2162688 | tf_op jit(solution)/shard_map/all_gather | solution.py:798
  11.6 205.7 %all-gather.16.cloned.1.call-start = ((), (), s32[]{:S(2)}) async-start(), calls=%async_computation.6 | async-start | bytes 2162688 | tf_op jit(solution)/shard_map/all_gather | solution.py:798
  64.0 7.9 %copy-start.73 = (s32[128,7]{0,1:T(8,128)S(1)}, s32[128,7]{0,1:T(8,128)}, u32[]{:S(2)}) copy-start(s32[128,7]{0,1:T(8,128)} %param.18) | copy-start | bytes 10756
  64.0 43.2 %all-to-all-start.1 = ((bf16[128,32,128]{0,2,1:T(8,128)(2,1)}), bf16[128,32,128]{0,2,1:T(8,128)(2,1)S(1)}, u32[]{:S(2)}, u32[]{:S(2)}) async-start(bf16[128,32,128]{0,2,1:T(8,128)(2,1)} %bitcast.29), calls=%async_computation.1 | async-start | bytes 2097152 | tf_op jit(solution)/shard_map/all_to_all | solution.py:985
  107.3 8.1 %copy-start.28 = (f32[14336]{0:T(1024)S(1)}, f32[14336]{0:T(1024)}, u32[]{:S(2)}) copy-start(f32[14336]{0:T(1024)} %param.26) | copy-start | bytes 172036
  107.3 9.5 %slice-start.5 = ((f32[14336]{0:T(1024)}), f32[3584]{0:T(1024)S(1)}, s32[]{:S(2)}) async-start(f32[14336]{0:T(1024)} %param.26), calls=%async_computation.12 | async-start | bytes 32768 | tf_op jit(solution)/shard_map/slice | solution.py:990
  107.3 9.5 %slice-start.6 = ((f32[14336]{0:T(1024)}), f32[4096]{0:T(1024)S(1)}, s32[]{:S(2)}) async-start(f32[14336]{0:T(1024)} %param.26), calls=%async_computation.13 | async-start | bytes 32768 | tf_op jit(solution)/shard_map/slice | solution.py:55
  107.3 84.3 %all-to-all-start = ((bf16[32,64,512]{2,1,0:T(8,128)(2,1)}), bf16[32,64,512]{2,1,0:T(8,128)(2,1)}, u32[]{:S(2)}, u32[]{:S(2)}) async-start(bf16[32,64,512]{2,1,0:T(8,128)(2,1)} %bitcast.237), calls=%async_computation | async-start | bytes 4194304 | tf_op jit(solution)/shard_map/all_to_all | solution.py:949
  113.6 8.9 %copy-start.75 = (s32[128,7]{0,1:T(8,128)S(1)}, s32[128,7]{0,1:T(8,128)}, u32[]{:S(2)}) copy-start(s32[128,7]{0,1:T(8,128)} %param.19) | copy-start | bytes 10756
  113.7 148.3 %all-gather.10.cloned.1.call-start = ((), (), s32[]{:S(2)}) async-start(), calls=%async_computation.3 | async-start | bytes 4325376 | tf_op jit(solution)/shard_map/all_gather | solution.py:798
  122.5 72.8 %copy-start.45 = (f32[512]{0:T(512)}, f32[512]{0:T(512)S(1)}, u32[]{:S(2)}) copy-start(f32[512]{0:T(512)S(1)} %get-tuple-element.255) | copy-start | bytes 6148
  122.5 88.4 %copy-start.35 = (pred[128,8]{0,1:T(8,128)(4,1)}, pred[128,8]{0,1:T(8,128)(4,1)S(1)}, u32[]{:S(2)}) copy-start(pred[128,8]{0,1:T(8,128)(4,1)S(1)} %pad_compare_fusion) | copy-start | bytes 3076
  217.3 44.6 %copy-start.39 = (f32[512]{0:T(512)S(1)}, f32[512]{0:T(512)}, u32[]{:S(2)}) copy-start(f32[512]{0:T(512)} %get-tuple-element.249) | copy-start | bytes 6148
  219.9 46.0 %copy-start.67 = (f32[128]{0:T(128)}, f32[128]{0:T(128)S(1)}, u32[]{:S(2)}) copy-start(f32[128]{0:T(128)S(1)} %broadcast_multiply_fusion.1) | copy-start | bytes 1540
  220.1 45.8 %copy-start.71 = (f32[128]{0:T(128)}, f32[128]{0:T(128)S(1)}, u32[]{:S(2)}) copy-start(f32[128]{0:T(128)S(1)} %fusion.107) | copy-start | bytes 1540
  267.6 8.9 %copy-start.56 = (f32[128]{0:T(128)}, f32[128]{0:T(128)S(1)}, u32[]{:S(2)}) copy-start(f32[128]{0:T(128)S(1)} %negate_multiply_fusion.2) | copy-start | bytes 1540
  413.7 28.0 %copy-start.29 = (f32[8192]{0:T(1024)S(1)}, f32[8192]{0:T(1024)}, u32[]{:S(2)}) copy-start(f32[8192]{0:T(1024)} %get-tuple-element.261) | copy-start | bytes 98308
  413.7 28.0 %copy-start.41 = (pred[8192]{0:T(1024)(128)(4,1)S(1)}, pred[8192]{0:T(1024)(128)(4,1)}, u32[]{:S(2)}) copy-start(pred[8192]{0:T(1024)(128)(4,1)} %compare_and_fusion) | copy-start | bytes 24580
  461.7 145.7 %all-to-all-start.2 = ((bf16[32,64,512]{2,1,0:T(8,128)(2,1)}), bf16[32,64,512]{2,1,0:T(8,128)(2,1)}, u32[]{:S(2)}, u32[]{:S(2)}) async-start(bf16[32,64,512]{2,1,0:T(8,128)(2,1)} %bitcast.238), calls=%async_computation.2 | async-start | bytes 4194304 | tf_op jit(solution)/shard_map/all_to_all | solution.py:1061
  473.3 123.7 %slice-start.2 = ((s8[5242880]{0:T(1024)(128)(4,1)}), s8[4194304]{0:T(1024)(128)(4,1)S(1)}, s32[]{:S(2)}) async-start(s8[5242880]{0:T(1024)(128)(4,1)} %bitcast.218), calls=%async_computation.9 | async-start | bytes 8388608
  476.7 120.3 %slice-start.3 = ((s8[5242880]{0:T(1024)(128)(4,1)}), s8[1048576]{0:T(1024)(128)(4,1)S(1)}, s32[]{:S(2)}) async-start(s8[5242880]{0:T(1024)(128)(4,1)} %bitcast.218), calls=%async_computation.10 | async-start | bytes 2097152
  597.0 10.4 %copy-start.63 = (s32[2048]{0:T(1024)S(1)}, s32[2048]{0:T(1024)}, u32[]{:S(2)}) copy-start(s32[2048]{0:T(1024)} %copy-done.62) | copy-start | bytes 24580
  (71 other events, 222.8 us)
Sparse Core Ops, SparseCore 0:
  11.5 55.2 all-gather.11
  69.6 62.2 all-gather.13
  134.8 63.7 all-gather.15
  201.3 60.5 all-gather.9

commit v3 on v1

--- a/solution.py
+++ b/solution.py
@@ -4,6 +4,8 @@
 import jax
 import jax.numpy as jnp
 from jax import lax
+from jax.experimental import pallas as pl
+from jax.experimental.pallas import tpu as pltpu
 from jax.sharding import PartitionSpec as P
 
 D = 512
@@ -121,7 +123,17 @@
     return lax.dot_general(block, block, (((0,), (0,)), ((), ())), precision=HIGHEST)
 
 
-def on_device(
+def adam(vec_grad, vec_master, vec_moment1, vec_moment2, vec_ema):
+    moment_one = ADAM_BETA1 * vec_moment1 + (1.0 - ADAM_BETA1) * vec_grad
+    moment_two = ADAM_BETA2 * vec_moment2 + (1.0 - ADAM_BETA2) * vec_grad * vec_grad
+    corrected_one = moment_one / (1.0 - ADAM_BETA1**STEP)
+    corrected_two = moment_two / (1.0 - ADAM_BETA2**STEP)
+    vec_weight = vec_master - ADAM_RATE * corrected_one / (jnp.sqrt(corrected_two) + ADAM_EPSILON)
+    vec_ema_new = EMA_DECAY * vec_ema + (1.0 - EMA_DECAY) * vec_weight
+    return vec_grad, moment_one, moment_two, vec_weight, vec_ema_new
+
+
+def on_device_plain(
     piece_table,
     piece_ids,
     slot_mask,
@@ -367,12 +379,6 @@
         )
     weight_block = jnp.concatenate(new_segments, axis=0)[None]
     ema_block = EMA_DECAY * mat_ema + (1.0 - EMA_DECAY) * weight_block
-    moment_one = ADAM_BETA1 * vec_moment1 + (1.0 - ADAM_BETA1) * vec_grad
-    moment_two = ADAM_BETA2 * vec_moment2 + (1.0 - ADAM_BETA2) * vec_grad * vec_grad
-    corrected_one = moment_one / (1.0 - ADAM_BETA1**STEP)
-    corrected_two = moment_two / (1.0 - ADAM_BETA2**STEP)
-    vec_weight = vec_master - ADAM_RATE * corrected_one / (jnp.sqrt(corrected_two) + ADAM_EPSILON)
-    vec_ema_new = EMA_DECAY * vec_ema + (1.0 - EMA_DECAY) * vec_weight
     return (
         text_embeds,
         piece_grad,
@@ -380,12 +386,1656 @@
         momentum_block[None],
         weight_block,
         ema_block,
-        vec_grad,
-        moment_one,
-        moment_two,
-        vec_weight,
-        vec_ema_new,
-    )
+    ) + adam(vec_grad, vec_master, vec_moment1, vec_moment2, vec_ema)
+
+
+MESH_ID = pl.DeviceIdType.MESH
+CORES = 2
+CHIPS = 4
+PLANES = 4
+MAIN = 192
+CHUNKS = 3
+CHUNK = MAIN // CHUNKS
+PROJ = 32
+PART = MAIN + PLANES * PROJ
+VROWS = 16
+
+
+def place():
+    wide_at = lax.axis_index("wide")
+    plane = lax.axis_index("narrow")
+    chip = wide_at // CORES
+    core = lax.rem(wide_at, CORES)
+    return wide_at, plane, chip, core
+
+
+def enter(targets):
+    barrier = pltpu.get_barrier_semaphore()
+    for target in targets:
+        pl.semaphore_signal(barrier, inc=1, device_id=target, device_id_type=MESH_ID)
+    pl.semaphore_wait(barrier, len(targets))
+
+
+def neighbours(wide_at, plane, chip, core):
+    sibling = (chip * CORES + 1 - core, plane)
+    chips = [(lax.rem(chip + k, CHIPS) * CORES + core, plane) for k in range(1, CHIPS)]
+    planes = [(wide_at, lax.rem(plane + k, PLANES)) for k in range(1, PLANES)]
+    return sibling, chips, planes
+
+
+def remote(src, dst, sems, index, target):
+    return pltpu.make_async_remote_copy(
+        src_ref=src,
+        dst_ref=dst,
+        send_sem=sems[0].at[index],
+        recv_sem=sems[1].at[index],
+        device_id=target,
+        device_id_type=MESH_ID,
+    )
+
+OWNERS = (6, 7, 2, 4, 0)
+BLOCK_TILES = (3, 1, 4, 4, 8)
+MOST_TILES = max(BLOCK_TILES)
+MAIN_TILES = 12
+BANDS = 4
+TEXT_TILE = 512
+TILE = 128
+SIDE = 2
+STRIPS = 8
+STRIP = D // STRIPS
+PACKED = 640
+PIECES = ((0, 64, 1024), (64, 64, 512), (128, 16, 384), (144, 48, 0))
+
+
+def halves(value):
+    high = value.astype(jnp.bfloat16)
+    return high, (value - high.astype(jnp.float32)).astype(jnp.bfloat16)
+
+
+def plain_dot(left, right):
+    return jnp.dot(left, right, preferred_element_type=jnp.float32)
+
+
+def split_dot(left, right):
+    return plain_dot(left[0], right[0]) + (
+        plain_dot(left[0], right[1]) + plain_dot(left[1], right[0])
+    )
+
+
+def dot_nt(left, right):
+    return lax.dot_general(
+        left, right, (((1,), (1,)), ((), ())), preferred_element_type=jnp.float32
+    )
+
+
+def dot_tn(left, right):
+    return lax.dot_general(
+        left, right, (((0,), (0,)), ((), ())), preferred_element_type=jnp.float32
+    )
+
+
+def band_onehot(ids, rows):
+    place_in = lax.rem(ids, rows)
+    spots = lax.broadcasted_iota(jnp.int32, (rows, ids.shape[1]), 0)
+    return jnp.where(spots == place_in, 1.0, 0.0).astype(jnp.bfloat16)
+
+
+def across(wide_at, plane, chip, core):
+    x_at = lax.rem(chip, SIDE)
+    x_chip = chip + 1 - 2 * x_at
+    y_chip = lax.rem(chip + SIDE, CHIPS)
+    return x_chip * CORES + core, y_chip * CORES + core
+
+
+def owner_tiles(wide_at):
+    tile_count = jnp.int32(0)
+    tile_first = jnp.int32(0)
+    begin = 0
+    for owner, count in zip(OWNERS, BLOCK_TILES):
+        tile_count = tile_count + jnp.where(wide_at == owner, count, 0)
+        tile_first = tile_first + jnp.where(wide_at == owner, begin, 0)
+        begin = begin + count
+    return tile_count, tile_first
+
+
+def settle_kernel(
+    every,
+    main_ref,
+    vec_ref,
+    grad_ref,
+    proj_ref,
+    bias_ref,
+    momentum_ref,
+    ids_ref,
+    mask_ref,
+    text_ref,
+    sum_ref,
+    proj_sum_ref,
+    vec_out_ref,
+    gram_ref,
+    high_ref,
+    low_ref,
+    table_ref,
+    text_tiles,
+    near,
+    first,
+    x_first,
+    y_first,
+    x_second,
+    y_second,
+    second,
+    deep,
+    proj_own,
+    proj_far,
+    part,
+    proj_part,
+    vec_near,
+    vec_far,
+    vec_deep,
+    main_tiles,
+    proj_tiles,
+    momentum_tiles,
+    packs,
+    pieces,
+    totals,
+    local_sem,
+    tile_sem,
+    text_sem,
+    main_send,
+    main_recv,
+    far_send,
+    far_recv,
+    deep_send,
+    deep_recv,
+    done_send,
+    done_recv,
+    pass_send,
+    pass_recv,
+    proj_send,
+    proj_recv,
+    vec_send,
+    vec_recv,
+    gram_send,
+    gram_recv,
+):
+    wide_at, plane, chip, core = place()
+    sibling, chips, planes = neighbours(wide_at, plane, chip, core)
+    x_wide, y_wide = across(wide_at, plane, chip, core)
+    x_near, y_near = (x_wide, plane), (y_wide, plane)
+    diagonal_wide = (CHIPS - 1 - chip) * CORES + core
+    other = 1 - core
+    x_at = lax.rem(chip, SIDE)
+    y_at = chip // SIDE
+    tile_count, tile_first = owner_tiles(wide_at)
+
+    own_main = pltpu.make_async_copy(main_ref.at[core], first, local_sem.at[0])
+    own_main.start()
+
+    def momentum_load(tile):
+        source = pl.ds(pl.multiple_of((tile_first + tile) * TILE, TILE), TILE)
+        return pltpu.make_async_copy(
+            momentum_ref.at[source], momentum_tiles.at[tile], tile_sem.at[0, tile]
+        )
+
+    @pl.loop(0, tile_count)
+    def _(tile):
+        momentum_load(tile).start()
+
+    enter([sibling] + chips + planes)
+
+    vec_sems = (vec_send, vec_recv)
+    vec_copies = [remote(vec_ref.at[other], vec_near, vec_sems, 0, sibling)]
+    vec_copies[0].start()
+    main_sems = (main_send, main_recv)
+    near_copies = []
+    for chunk in range(CHUNKS):
+        copy = remote(main_ref.at[other, chunk], near.at[chunk], main_sems, chunk, sibling)
+        copy.start()
+        near_copies.append(copy)
+
+    count = every.shape[2]
+    features = proj_ref.shape[0]
+    wide_count = CHIPS * CORES
+    per_band = grad_ref.shape[0] // BANDS
+    total = jnp.zeros((features, D), jnp.float32)
+    for block in range(PLANES * wide_count):
+        rows = every[block % PLANES, block // PLANES]
+        total = total + dot_tn(grad_ref[block], rows)
+    proj_own[...] = total.astype(jnp.bfloat16).reshape(CHIPS, PROJ, D)
+
+    proj_sems = (proj_send, proj_recv)
+    proj_copies = []
+    for k, target in enumerate(chips):
+        to_chip = lax.rem(chip + k + 1, CHIPS)
+        copy = remote(proj_own.at[to_chip], proj_far.at[chip], proj_sems, k, target)
+        copy.start()
+        proj_copies.append(copy)
+    proj_far[chip] = proj_own[chip]
+
+    own_main.wait()
+    vec_copies[0].wait_recv()
+    vec_far[chip] = vec_ref[core] + vec_near[...]
+    for k, target in enumerate(chips):
+        copy = remote(vec_far.at[chip], vec_far.at[chip], vec_sems, 1 + k, target)
+        copy.start()
+        vec_copies.append(copy)
+
+    far_sems = (far_send, far_recv)
+    lows, highs = pl.ds(0, 2), pl.ds(2, 2)
+    firsts = []
+    for chunk in range(CHUNKS):
+        near_copies[chunk].wait_recv()
+
+        @pl.loop(0, CHIPS * PLANES)
+        def _(step, chunk=chunk):
+            y, x, m = step // (SIDE * PLANES), lax.rem(step // PLANES, SIDE), lax.rem(step, PLANES)
+            first[chunk, y, x, m] = (
+                first[chunk, y, x, m].astype(jnp.float32)
+                + near[chunk, y, x, m].astype(jnp.float32)
+            ).astype(jnp.bfloat16)
+
+        by_x = remote(
+            first.at[chunk, :, 1 - x_at, lows], x_first.at[chunk], far_sems, chunk * 4, x_near
+        )
+        by_y = remote(
+            first.at[chunk, 1 - y_at, :, highs], y_first.at[chunk], far_sems, chunk * 4 + 1, y_near
+        )
+        by_x.start()
+        by_y.start()
+        firsts.append((by_x, by_y))
+
+    seconds = []
+
+    def second_step(chunk):
+        by_x, by_y = firsts[chunk]
+        by_x.wait_recv()
+        for y in range(SIDE):
+            for m in range(2):
+                first[chunk, y, x_at, m] = (
+                    first[chunk, y, x_at, m].astype(jnp.float32)
+                    + x_first[chunk, y, m].astype(jnp.float32)
+                ).astype(jnp.bfloat16)
+        next_y = remote(
+            first.at[chunk, 1 - y_at, x_at, lows],
+            y_second.at[chunk],
+            far_sems,
+            chunk * 4 + 2,
+            y_near,
+        )
+        next_y.start()
+        by_y.wait_recv()
+        for x in range(SIDE):
+            for m in range(2):
+                first[chunk, y_at, x, 2 + m] = (
+                    first[chunk, y_at, x, 2 + m].astype(jnp.float32)
+                    + y_first[chunk, x, m].astype(jnp.float32)
+                ).astype(jnp.bfloat16)
+        next_x = remote(
+            first.at[chunk, y_at, 1 - x_at, highs],
+            x_second.at[chunk],
+            far_sems,
+            chunk * 4 + 3,
+            x_near,
+        )
+        next_x.start()
+        seconds.append((next_y, next_x))
+
+    deep_sems = (deep_send, deep_recv)
+    deep_copies = []
+
+    def deep_step(chunk):
+        next_y, next_x = seconds[chunk]
+        next_y.wait_recv()
+        for m in range(2):
+            second[chunk, m] = (
+                first[chunk, y_at, x_at, m].astype(jnp.float32)
+                + y_second[chunk, m].astype(jnp.float32)
+            ).astype(jnp.bfloat16)
+        next_x.wait_recv()
+        for m in range(2):
+            second[chunk, 2 + m] = (
+                first[chunk, y_at, x_at, 2 + m].astype(jnp.float32)
+                + x_second[chunk, m].astype(jnp.float32)
+            ).astype(jnp.bfloat16)
+        copies = []
+        for k, target in enumerate(planes):
+            to_plane = lax.rem(plane + k + 1, PLANES)
+            copy = remote(
+                second.at[chunk, to_plane], deep.at[chunk, k], deep_sems, chunk * 3 + k, target
+            )
+            copy.start()
+            copies.append(copy)
+        deep_copies.append(copies)
+
+    for block in range(PLANES * wide_count):
+        rows = every[block % PLANES, block // PLANES]
+        band, spot = divmod(block, per_band)
+        table_ref[band * features : (band + 1) * features, spot * count : (spot + 1) * count] = (
+            dot_nt(proj_ref[...], rows) + bias_ref[...]
+        ).astype(jnp.bfloat16)
+
+    text_rows = table_ref.shape[1]
+    text_count = ids_ref.shape[1] // TEXT_TILE
+
+    def text_copy(step):
+        slot = lax.rem(step, 2)
+        lanes = pl.ds(pl.multiple_of(step * TEXT_TILE, TEXT_TILE), TEXT_TILE)
+        return pltpu.make_async_copy(text_tiles.at[slot], text_ref.at[:, lanes], text_sem.at[slot])
+
+    def text_steps(begin, end):
+        @pl.loop(begin, end)
+        def _(step):
+            lanes = pl.ds(pl.multiple_of(step * TEXT_TILE, TEXT_TILE), TEXT_TILE)
+            ids = ids_ref[:, lanes]
+            values = plain_dot(table_ref[...], band_onehot(ids, text_rows))
+            band = jnp.where(mask_ref[:, lanes] > 0, ids // text_rows, -1)
+            total = jnp.zeros((features, TEXT_TILE), jnp.float32)
+            for b in range(BANDS):
+                total = jnp.where(band == b, values[b * features : (b + 1) * features], total)
+
+            @pl.when(step >= 2)
+            def _():
+                text_copy(step - 2).wait()
+
+            text_tiles[lax.rem(step, 2)] = total
+            text_copy(step).start()
+
+    text_steps(0, 4)
+    second_step(0)
+    second_step(1)
+    second_step(2)
+    text_steps(4, 6)
+    deep_step(0)
+    deep_step(1)
+    deep_step(2)
+
+    for copy in vec_copies[1:4]:
+        copy.wait()
+    vec_deep[plane] = (vec_far[0] + vec_far[1]) + (vec_far[2] + vec_far[3])
+    for k, target in enumerate(planes):
+        copy = remote(vec_deep.at[plane], vec_deep.at[plane], vec_sems, 4 + k, target)
+        copy.start()
+        vec_copies.append(copy)
+
+    for copy in proj_copies:
+        copy.wait()
+    proj_copies = []
+    for k, target in enumerate(planes):
+        to_plane = lax.rem(plane + k + 1, PLANES)
+        copy = remote(proj_far.at[to_plane], proj_part.at[plane], proj_sems, 3 + k, target)
+        copy.start()
+        proj_copies.append(copy)
+    proj_part[plane] = proj_far[plane]
+    text_steps(6, 12)
+
+    done_sems = (done_send, done_recv)
+    pass_sems = (pass_send, pass_recv)
+    done_copies = []
+    locals_done = []
+
+    def natural(index, wide):
+        _, size, base = PIECES[index]
+        return sum_ref.at[pl.ds(pl.multiple_of(base + wide * size, 16), size)]
+
+    def proj_natural(at_chip, at_core):
+        return proj_sum_ref.at[at_core, :, at_chip]
+
+    def publish(index, src, spot):
+        copies = []
+        for k, target in enumerate([sibling] + chips):
+            copy = remote(src, spot, done_sems, index * 4 + k, target)
+            copy.start()
+            copies.append(copy)
+        done_copies.append(copies)
+        copy = pltpu.make_async_copy(src, spot, local_sem.at[2 + index])
+        copy.start()
+        locals_done.append(copy)
+
+    for chunk in range(CHUNKS):
+        for copy in deep_copies[chunk]:
+            copy.wait_recv()
+        value = second[chunk, plane].astype(jnp.float32)
+        for k in range(3):
+            value = value + deep[chunk, k].astype(jnp.float32)
+        part[chunk * CHUNK : (chunk + 1) * CHUNK, :] = value.astype(jnp.bfloat16)
+        for index, (offset, size, _) in enumerate(PIECES):
+            if offset // CHUNK == chunk:
+                publish(index, part.at[pl.ds(offset, size)], natural(index, wide_at))
+    for copy in proj_copies:
+        copy.wait()
+    publish(len(PIECES), proj_part, proj_natural(chip, core))
+
+    for copy in vec_copies[4:7]:
+        copy.wait()
+    vec_out_ref[core] = (vec_deep[0] + vec_deep[1]) + (vec_deep[2] + vec_deep[3])
+    copy = remote(vec_out_ref.at[core], vec_out_ref.at[core], vec_sems, 7, sibling)
+    copy.start()
+    vec_copies.append(copy)
+
+    pass_copies = []
+    for index in range(len(PIECES) + 1):
+        for k in range(3):
+            done_copies[index][1 + k].wait_recv()
+            from_chip = lax.rem(chip + CHIPS - 1 - k, CHIPS)
+            if index < len(PIECES):
+                spot = natural(index, from_chip * CORES + core)
+            else:
+                spot = proj_natural(from_chip, core)
+            copy = remote(spot, spot, pass_sems, index * 3 + k, sibling)
+            copy.start()
+            pass_copies.append(copy)
+
+    text_steps(12, text_count)
+    for copies in done_copies:
+        copies[0].wait_recv()
+    for copy in pass_copies:
+        copy.wait_recv()
+    for copy in locals_done:
+        copy.wait()
+
+    gram_sems = (gram_send, gram_recv)
+
+    def add_tile(tile, gradient):
+        momentum_load(tile).wait()
+        gradient = gradient.astype(jnp.float32)
+        update = gradient + MUON_BETA * (MUON_BETA * momentum_tiles[tile] + gradient)
+        high, low = halves(update)
+        high_ref[tile] = high
+        low_ref[tile] = low
+        gram_ref[...] += dot_tn(high, high)
+        cross = dot_tn(high, low)
+        gram_ref[...] += cross + cross.T
+
+    @pl.when(tile_count > 0)
+    def _():
+        gram_ref[...] = jnp.zeros_like(gram_ref)
+
+    @pl.when(wide_at == OWNERS[4])
+    def _():
+        loads = [
+            pltpu.make_async_copy(
+                proj_sum_ref.at[tile // PLANES, tile % PLANES],
+                proj_tiles.at[tile],
+                tile_sem.at[1, tile],
+            )
+            for tile in range(MOST_TILES)
+        ]
+        for copy in loads:
+            copy.start()
+        for copy in loads:
+            copy.wait()
+
+        @pl.loop(0, MOST_TILES)
+        def _(tile):
+            add_tile(tile, proj_tiles[tile].reshape(TILE, D))
+
+    @pl.when((tile_count > 0) & (wide_at != OWNERS[4]))
+    def _():
+        def load(tile):
+            source = pl.ds(pl.multiple_of((tile_first + tile) * TILE, TILE), TILE)
+            return pltpu.make_async_copy(
+                sum_ref.at[source], main_tiles.at[tile], tile_sem.at[1, tile]
+            )
+
+        @pl.loop(0, tile_count)
+        def _(tile):
+            load(tile).start()
+
+        @pl.loop(0, tile_count)
+        def _(tile):
+            load(tile).wait()
+            add_tile(tile, main_tiles[tile])
+
+    @pl.when(tile_count > 0)
+    def _():
+        for t in range(PLANES):
+            for strip, lane in ((t, 0), (STRIPS - 1 - t, 1)):
+                begin = strip // 2 * TILE
+                value = gram_ref[strip * STRIP : (strip + 1) * STRIP, begin:]
+                width = D - begin
+                at = 0 if lane == 0 else PACKED - width
+                packs[t, :, at : at + width] = value
+        copies = []
+        for k, target in enumerate(planes):
+            to_plane = lax.rem(plane + k + 1, PLANES)
+            copy = remote(packs.at[to_plane], pieces.at[plane], gram_sems, k, target)
+            copy.start()
+            copies.append(copy)
+        pieces[plane] = packs[plane]
+        for copy in copies:
+            copy.wait()
+        totals[plane] = (pieces[0] + pieces[1]) + (pieces[2] + pieces[3])
+        copies = []
+        for k, target in enumerate(planes):
+            copy = remote(totals.at[plane], totals.at[plane], gram_sems, 3 + k, target)
+            copy.start()
+            copies.append(copy)
+        for copy in copies:
+            copy.wait()
+        for t in range(PLANES):
+            for strip, lane in ((t, 0), (STRIPS - 1 - t, 1)):
+                begin = strip // 2 * TILE
+                width = D - begin
+                at = 0 if lane == 0 else PACKED - width
+                gram_ref[strip * STRIP : (strip + 1) * STRIP, begin:] = totals[
+                    t, :, at : at + width
+                ]
+        row_block = lax.broadcasted_iota(jnp.int32, (D, D), 0) // TILE
+        lane_block = lax.broadcasted_iota(jnp.int32, (D, D), 1) // TILE
+        value = gram_ref[...]
+        gram_ref[...] = jnp.where(lane_block >= row_block, value, value.T)
+
+    for copies in done_copies:
+        for copy in copies:
+            copy.wait_send()
+    for copy in pass_copies:
+        copy.wait_send()
+    for copy in near_copies:
+        copy.wait_send()
+    for pair in firsts + seconds:
+        for copy in pair:
+            copy.wait_send()
+    for copies in deep_copies:
+        for copy in copies:
+            copy.wait_send()
+    vec_copies[0].wait_send()
+    vec_copies[7].wait()
+    text_copy(text_count - 2).wait()
+    text_copy(text_count - 1).wait()
+
+
+def settle(every, main, vec, grad_own, proj_own, bias_own, momentum, flat_ids, flat_mask):
+    dma = pltpu.SemaphoreType.DMA
+    f32, bf = jnp.float32, jnp.bfloat16
+    features, tokens = proj_own.shape[0], flat_ids.shape[0]
+    rows = grad_own.shape[0] * grad_own.shape[1] // BANDS
+    hbm = pl.BlockSpec(memory_space=pl.ANY)
+    vmem = pl.BlockSpec(memory_space=pltpu.VMEM)
+    grid = (CHUNKS, SIDE, SIDE, PLANES, CHUNK, D)
+    return pl.pallas_call(
+        settle_kernel,
+        out_shape=(
+            jax.ShapeDtypeStruct((features, tokens), f32),
+            jax.ShapeDtypeStruct((MAIN_TILES * TILE, D), bf),
+            jax.ShapeDtypeStruct((CORES, PLANES, CHIPS, PROJ, D), bf),
+            jax.ShapeDtypeStruct((CORES, VROWS, D), f32),
+            jax.ShapeDtypeStruct((D, D), f32),
+            jax.ShapeDtypeStruct((MOST_TILES, TILE, D), bf),
+            jax.ShapeDtypeStruct((MOST_TILES, TILE, D), bf),
+        ),
+        in_specs=[vmem, hbm, vmem, vmem, vmem, vmem, hbm, vmem, vmem],
+        out_specs=(hbm, hbm, hbm, vmem, vmem, vmem, vmem),
+        scratch_shapes=[
+            pltpu.VMEM((BANDS * features, rows), bf),
+            pltpu.VMEM((2, features, TEXT_TILE), f32),
+            pltpu.VMEM(grid, bf),
+            pltpu.VMEM(grid, bf),
+            pltpu.VMEM((CHUNKS, SIDE, 2, CHUNK, D), bf),
+            pltpu.VMEM((CHUNKS, SIDE, 2, CHUNK, D), bf),
+            pltpu.VMEM((CHUNKS, 2, CHUNK, D), bf),
+            pltpu.VMEM((CHUNKS, 2, CHUNK, D), bf),
+            pltpu.VMEM((CHUNKS, PLANES, CHUNK, D), bf),
+            pltpu.VMEM((CHUNKS, 3, CHUNK, D), bf),
+            pltpu.VMEM((CHIPS, PROJ, D), bf),
+            pltpu.VMEM((CHIPS, PROJ, D), bf),
+            pltpu.VMEM((MAIN, D), bf),
+            pltpu.VMEM((PLANES, PROJ, D), bf),
+            pltpu.VMEM((VROWS, D), f32),
+            pltpu.VMEM((CHIPS, VROWS, D), f32),
+            pltpu.VMEM((PLANES, VROWS, D), f32),
+            pltpu.VMEM((4, TILE, D), bf),
+            pltpu.VMEM((MOST_TILES, CHIPS, PROJ, D), bf),
+            pltpu.VMEM((MOST_TILES, TILE, D), f32),
+            pltpu.VMEM((PLANES, STRIP, PACKED), f32),
+            pltpu.VMEM((PLANES, STRIP, PACKED), f32),
+            pltpu.VMEM((PLANES, STRIP, PACKED), f32),
+            dma((8,)),
+            dma((2, MOST_TILES)),
+            dma((2,)),
+            dma((CHUNKS,)),
+            dma((CHUNKS,)),
+            dma((CHUNKS * 4,)),
+            dma((CHUNKS * 4,)),
+            dma((CHUNKS * 3,)),
+            dma((CHUNKS * 3,)),
+            dma((20,)),
+            dma((20,)),
+            dma((15,)),
+            dma((15,)),
+            dma((6,)),
+            dma((6,)),
+            dma((8,)),
+            dma((8,)),
+            dma((6,)),
+            dma((6,)),
+        ],
+        compiler_params=pltpu.CompilerParams(
+            collective_id=3, has_side_effects=True, vmem_limit_bytes=58 * 2**20
+        ),
+        name="settle",
+    )(
+        every,
+        main.reshape((CORES,) + grid),
+        vec,
+        grad_own,
+        proj_own,
+        bias_own,
+        momentum,
+        flat_ids[None],
+        flat_mask[None],
+    )
+
+
+SHARES = ((6, 0, 0, 384), (7, 0, 384, 128), (2, 0, 512, 512), (4, 0, 1024, 512)) + (
+    (0, 0, 1536, 512),
+    (0, 512, 2048, 512),
+)
+
+
+def muon_kernel(
+    gram_ref,
+    high_ref,
+    low_ref,
+    out_ref,
+    gram,
+    poly,
+    chain,
+    rows_out,
+    local_sem,
+    rows_send,
+    rows_recv,
+):
+    wide_at, plane, chip, core = place()
+    sibling, chips, planes = neighbours(wide_at, plane, chip, core)
+    x_wide, y_wide = across(wide_at, plane, chip, core)
+    x_near, y_near = (x_wide, plane), (y_wide, plane)
+    tile_count, _ = owner_tiles(wide_at)
+    enter([sibling, x_near, y_near])
+
+    @pl.when(tile_count > 0)
+    def _():
+        diagonal = lax.broadcasted_iota(jnp.int32, (D, D), 0) == lax.broadcasted_iota(
+            jnp.int32, (D, D), 1
+        )
+        square = jnp.sum(jnp.where(diagonal, gram_ref[...], 0.0))
+        inverse = 1.0 / (jnp.sqrt(jnp.full((1, 1), square)) + 1e-07)
+        gram[...] = gram_ref[...] * (inverse * inverse)
+
+        def make_poly():
+            value = gram[...]
+            parts = halves(value)
+            diagonal = lax.broadcasted_iota(jnp.int32, (D, D), 0) == lax.broadcasted_iota(
+                jnp.int32, (D, D), 1
+            )
+            poly[...] = (
+                NEWTON_B * value
+                + NEWTON_C * split_dot(parts, parts)
+                + jnp.where(diagonal, NEWTON_A, 0.0)
+            )
+
+        def next_gram():
+            parts = halves(poly[...])
+            half_way = split_dot(halves(gram[...]), parts)
+            gram[...] = split_dot(halves(half_way), parts)
+
+        def extend():
+            chain[...] = split_dot(halves(chain[...]), halves(poly[...]))
+
+        make_poly()
+        chain[...] = poly[...]
+        next_gram()
+
+        @pl.loop(0, 3)
+        def _(sweep):
+            make_poly()
+            extend()
+            next_gram()
+
+        make_poly()
+        extend()
+        chain_parts = halves(chain[...] * inverse)
+
+        @pl.loop(0, tile_count)
+        def _(tile):
+            rows = pl.ds(pl.multiple_of(tile * TILE, TILE), TILE)
+            rows_out[rows, :] = split_dot((high_ref[tile], low_ref[tile]), chain_parts).astype(
+                jnp.bfloat16
+            )
+
+    sems = (rows_send, rows_recv)
+
+    def share_copies(index):
+        owner, source, begin, size = SHARES[index]
+        owner_chip, owner_core = divmod(owner, CORES)
+        mine = rows_out.at[pl.ds(source, size)]
+        spot = out_ref.at[pl.ds(begin, size)]
+        first = out_ref.at[pl.ds(begin, size // 2)]
+        last = out_ref.at[pl.ds(begin + size // 2, size // 2)]
+        base = index * 9
+        roles = {
+            "x": (owner_chip ^ 1) * CORES + owner_core,
+            "y": (owner_chip ^ 2) * CORES + owner_core,
+            "d": (owner_chip ^ 3) * CORES + owner_core,
+        }
+        sends = {
+            "o": [
+                (mine, spot, base, x_near),
+                (mine, spot, base + 1, y_near),
+                (mine, spot, base + 2, sibling),
+            ],
+            "x": [(first, first, base + 3, y_near), (spot, spot, base + 5, sibling)],
+            "y": [(last, last, base + 4, x_near), (spot, spot, base + 6, sibling)],
+            "d": [(first, first, base + 7, sibling), (last, last, base + 8, sibling)],
+        }
+        gets = {
+            "x": [(spot, base)],
+            "y": [(spot, base + 1)],
+            "d": [(first, base + 3), (last, base + 4)],
+            "so": [(spot, base + 2)],
+            "sx": [(spot, base + 5)],
+            "sy": [(spot, base + 6)],
+            "sd": [(first, base + 7), (last, base + 8)],
+        }
+        roles["o"] = owner
+        for role in ("o", "x", "y", "d"):
+            at = roles[role]
+            roles["s" + role] = at // CORES * CORES + 1 - at % CORES
+        local = (mine, spot, local_sem.at[index])
+        return roles, sends, gets, local
+
+    def started(entry):
+        src, dst, index, target = entry
+        return remote(src, dst, sems, index, target)
+
+    def arriving(entry):
+        spot, index = entry
+        return remote(spot, spot, sems, index, sibling)
+
+    plans = [share_copies(index) for index in range(len(SHARES))]
+    for roles, sends, gets, local in plans:
+
+        @pl.when(wide_at == roles["o"])
+        def _(sends=sends, local=local):
+            for entry in sends["o"]:
+                started(entry).start()
+            pltpu.make_async_copy(*local).start()
+
+    for phase in (("x", "y"), ("d",)):
+        for roles, sends, gets, local in plans:
+            for role in phase:
+
+                @pl.when(wide_at == roles[role])
+                def _(sends=sends, gets=gets, role=role):
+                    for got, entry in zip(gets[role] * 2, sends[role]):
+                        if role == "d" or entry is sends[role][0]:
+                            arriving(got).wait_recv()
+                        started(entry).start()
+
+    for roles, sends, gets, local in plans:
+        for role in ("so", "sx", "sy", "sd"):
+
+            @pl.when(wide_at == roles[role])
+            def _(gets=gets, role=role):
+                for got in gets[role]:
+                    arriving(got).wait_recv()
+
+        for role in ("o", "x", "y", "d"):
+
+            @pl.when(wide_at == roles[role])
+            def _(sends=sends, local=local, role=role):
+                for entry in sends[role]:
+                    started(entry).wait_send()
+                if role == "o":
+                    pltpu.make_async_copy(*local).wait()
+
+
+def muon_rows(gram, high, low):
+    dma = pltpu.SemaphoreType.DMA
+    vmem = pl.BlockSpec(memory_space=pltpu.VMEM)
+    total = (MAIN_TILES + MOST_TILES) * TILE
+    return pl.pallas_call(
+        muon_kernel,
+        out_shape=jax.ShapeDtypeStruct((total, D), jnp.bfloat16),
+        in_specs=[vmem] * 3,
+        out_specs=pl.BlockSpec(memory_space=pl.ANY),
+        scratch_shapes=[
+            pltpu.VMEM((D, D), jnp.float32),
+            pltpu.VMEM((D, D), jnp.float32),
+            pltpu.VMEM((D, D), jnp.float32),
+            pltpu.VMEM((MOST_TILES * TILE, D), jnp.bfloat16),
+            dma((len(SHARES),)),
+            dma((len(SHARES) * 9,)),
+            dma((len(SHARES) * 9,)),
+        ],
+        compiler_params=pltpu.CompilerParams(
+            collective_id=4, has_side_effects=True, vmem_limit_bytes=40 * 2**20
+        ),
+        name="muon_rows",
+    )(gram, high, low)
+
+
+def finish_kernel(main_ref, proj_ref, rows_ref, momentum_ref, master_ref, ema_ref, *outs):
+    grad_ref, momentum_new_ref, weight_ref, ema_new_ref = outs
+    tile = pl.program_id(0)
+    main = main_ref[...].astype(jnp.float32)
+    proj = proj_ref[...].reshape(TILE, D).astype(jnp.float32)
+    gradient = jnp.where(tile < MAIN_TILES, main, proj)
+    grad_ref[0] = gradient
+    momentum_new_ref[0] = MUON_BETA * momentum_ref[0] + gradient
+    scale = jnp.float32(0.0)
+    begin = 0
+    for row_total, count in zip(matrix_rows(), BLOCK_TILES):
+        inside = (tile >= begin) & (tile < begin + count)
+        scale = jnp.where(inside, MUON_RATE * math.sqrt(row_total / D), scale)
+        begin = begin + count
+    weight = master_ref[0] * (1.0 - MUON_RATE * MUON_DECAY) - scale * rows_ref[...].astype(
+        jnp.float32
+    )
+    weight_ref[0] = weight
+    ema_new_ref[0] = EMA_DECAY * ema_ref[0] + (1.0 - EMA_DECAY) * weight
+
+
+def finish(main_sum, proj_sum, rows, momentum, master, ema):
+    block = pl.BlockSpec((1, TILE, D), lambda i: (0, i, 0))
+    proj = proj_sum.reshape((MOST_TILES,) + proj_sum.shape[2:])
+    return pl.pallas_call(
+        finish_kernel,
+        grid=(MAIN_TILES + MOST_TILES,),
+        out_shape=(jax.ShapeDtypeStruct(master.shape, jnp.float32),) * 4,
+        in_specs=[
+            pl.BlockSpec((TILE, D), lambda i: (jnp.minimum(i, MAIN_TILES - 1), 0)),
+            pl.BlockSpec(
+                (1,) + proj.shape[1:], lambda i: (jnp.maximum(i - MAIN_TILES, 0), 0, 0, 0)
+            ),
+            pl.BlockSpec((TILE, D), lambda i: (i, 0)),
+            block,
+            block,
+            block,
+        ],
+        out_specs=(block,) * 4,
+        cost_estimate=pl.CostEstimate(
+            flops=12 * master.size, bytes_accessed=32 * master.size, transcendentals=0
+        ),
+        name="finish",
+    )(main_sum, proj, rows, momentum, master, ema)
+
+def tell_kernel(own_ref, out_ref, send_sem, recv_sem):
+    wide_at, plane, chip, core = place()
+    wide_count = CHIPS * CORES
+    peers = [
+        (lax.rem(wide_at + k // PLANES, wide_count), lax.rem(plane + k % PLANES, PLANES))
+        for k in range(1, wide_count * PLANES)
+    ]
+    enter(peers)
+    spot = out_ref.at[wide_at * PLANES + plane]
+    copies = [
+        remote(own_ref, spot, (send_sem, recv_sem), k, target) for k, target in enumerate(peers)
+    ]
+    for copy in copies:
+        copy.start()
+    out_ref[wide_at * PLANES + plane] = own_ref[...]
+    for copy in copies:
+        copy.wait()
+
+
+def tell(values, collective_id):
+    dma = pltpu.SemaphoreType.DMA
+    every = PLANES * CHIPS * CORES
+    return pl.pallas_call(
+        tell_kernel,
+        out_shape=jax.ShapeDtypeStruct((every,) + values.shape, values.dtype),
+        in_specs=[pl.BlockSpec(memory_space=pltpu.VMEM)],
+        out_specs=pl.BlockSpec(memory_space=pltpu.VMEM),
+        scratch_shapes=[dma((every - 1,)), dma((every - 1,))],
+        compiler_params=pltpu.CompilerParams(collective_id=collective_id, has_side_effects=True),
+        name="tell_ids",
+    )(values)
+
+def two_part_dot(left, right):
+    high, low = halves(left)
+    return plain_dot(high, right) + plain_dot(low, right)
+
+
+def normalize(values):
+    center = values - jnp.mean(values, axis=-1, keepdims=True)
+    spread = jnp.mean(center * center, axis=-1, keepdims=True)
+    scale = lax.rsqrt(spread + 1e-05)
+    return center * scale, scale
+
+
+def normalize_back(grad, gain, hat, scale):
+    grad_hat = grad * gain
+    return scale * (
+        grad_hat
+        - jnp.mean(grad_hat, axis=-1, keepdims=True)
+        - hat * jnp.mean(grad_hat * hat, axis=-1, keepdims=True)
+    )
+
+
+def over_rows(values):
+    return jnp.sum(values, axis=0, keepdims=True)
+
+
+def spread_steps(own, held, sems, base, at):
+    wide_at, plane, chip, core = at
+    sibling = (chip * CORES + 1 - core, plane)
+    x_wide, y_wide = across(wide_at, plane, chip, core)
+    x_near, y_near = (x_wide, plane), (y_wide, plane)
+    diagonal_wide = (CHIPS - 1 - chip) * CORES + core
+    half = own.shape[0] // 2
+    tops, bottoms = pl.ds(0, half), pl.ds(half, half)
+    above, below = (wide_at, plane + 1), (wide_at, plane - 1)
+
+    def climb(distance, source, src):
+        spot = held.at[source, wide_at]
+        return remote(spot if src is None else src, spot, sems, base + distance - 1, above)
+
+    def sink(distance, source, src):
+        spot = held.at[source, wide_at]
+        return remote(spot if src is None else src, spot, sems, base + 2 + distance, below)
+
+    def plane_copy(source, kind, src=None):
+        index = base + 6 + 9 * source + kind
+        own_spot = held.at[source, wide_at]
+        x_spot, y_spot = held.at[source, x_wide], held.at[source, y_wide]
+        far_spot = held.at[source, diagonal_wide]
+        if kind in (0, 1, 2):
+            target = (x_near, y_near, sibling)[kind]
+            return remote(own_spot if src is None else src, own_spot, sems, index, target)
+        if kind == 3:
+            return remote(x_spot.at[tops], x_spot.at[tops], sems, index, y_near)
+        if kind == 5:
+            return remote(y_spot.at[bottoms], y_spot.at[bottoms], sems, index, x_near)
+        if kind in (4, 6):
+            spot = x_spot if kind == 4 else y_spot
+            return remote(spot, spot, sems, index, sibling)
+        rows = tops if kind == 7 else bottoms
+        return remote(far_spot.at[rows], far_spot.at[rows], sems, index, sibling)
+
+    def plane_send(source, src=None):
+        for kind in (0, 1, 2):
+            plane_copy(source, kind, src).start()
+
+    def begin():
+        @pl.when(plane < PLANES - 1)
+        def _():
+            climb(1, plane, own).start()
+
+        @pl.when(plane > 0)
+        def _():
+            sink(1, plane, own).start()
+
+        plane_send(plane, own)
+
+    def arrive(distance):
+        @pl.when(plane >= distance)
+        def _():
+            source = plane - distance
+            climb(distance, source, None).wait_recv()
+            if distance < PLANES - 1:
+
+                @pl.when(plane < PLANES - 1)
+                def _():
+                    climb(distance + 1, source, None).start()
+
+            plane_send(source)
+
+        @pl.when(plane + distance < PLANES)
+        def _():
+            source = plane + distance
+            sink(distance, source, None).wait_recv()
+            if distance < PLANES - 1:
+
+                @pl.when(plane > 0)
+                def _():
+                    sink(distance + 1, source, None).start()
+
+            plane_send(source)
+
+    def at_distance(distance, step):
+        if distance == 0:
+            step(plane)
+            return
+
+        @pl.when(plane >= distance)
+        def _():
+            step(plane - distance)
+
+        @pl.when(plane + distance < PLANES)
+        def _():
+            step(plane + distance)
+
+    def relay_one(source):
+        plane_copy(source, 0).wait_recv()
+        plane_copy(source, 3).start()
+        plane_copy(source, 4).start()
+        plane_copy(source, 1).wait_recv()
+        plane_copy(source, 5).start()
+        plane_copy(source, 6).start()
+
+    def finish_one(source):
+        plane_copy(source, 3).wait_recv()
+        plane_copy(source, 7).start()
+        plane_copy(source, 5).wait_recv()
+        plane_copy(source, 8).start()
+
+    def settle_one(source):
+        for kind in (2, 4, 6, 7, 8):
+            plane_copy(source, kind).wait_recv()
+        for kind in range(9):
+            plane_copy(source, kind).wait_send()
+
+    def relay(distance):
+        at_distance(distance, relay_one)
+
+    def finish(distance):
+        at_distance(distance, finish_one)
+
+    def settled():
+        for distance in range(PLANES):
+            at_distance(distance, settle_one)
+        for distance in range(1, PLANES):
+            source = plane - distance + 1
+
+            @pl.when((plane < PLANES - 1) & (source >= 0))
+            def _(distance=distance, source=source):
+                climb(distance, source, None).wait_send()
+
+            down_source = plane + distance - 1
+
+            @pl.when((plane > 0) & (down_source < PLANES))
+            def _(distance=distance, down_source=down_source):
+                sink(distance, down_source, None).wait_send()
+
+    return begin, arrive, relay, finish, settled
+
+
+def layer_kernel(
+    outgoing_in_ref,
+    own_ref,
+    ids_ref,
+    mask_ref,
+    cot_ref,
+    spots_ref,
+    live_ref,
+    cls_ref,
+    pos_ref,
+    norms_ref,
+    bias_up_ref,
+    bias_down_ref,
+    every_ref,
+    main_ref,
+    outgoing_ref,
+    vec_ref,
+    wide_ref,
+    own_grad_ref,
+    own_bias_ref,
+    own_proj_ref,
+    incoming_ref,
+    grad_ref,
+    packed,
+    text_total,
+    z_ref,
+    onehot,
+    hats,
+    scales,
+    normed,
+    keys,
+    probs,
+    grad_kv,
+    grad_normed,
+    grad_pieces,
+    active,
+    slope,
+    sums,
+    local_sem,
+    piece_send,
+    piece_recv,
+    table_send,
+    table_recv,
+    body_send,
+    body_recv,
+    proj_send,
+    proj_recv,
+    z_send,
+    z_recv,
+):
+    at = place()
+    wide_at, plane, chip, core = at
+    me = wide_at * PLANES + plane
+    wide_count = CHIPS * CORES
+    cap = outgoing_in_ref.shape[1]
+    peers = [
+        (lax.rem(wide_at + k // PLANES, wide_count), lax.rem(plane + k % PLANES, PLANES))
+        for k in range(1, wide_count * PLANES)
+    ]
+
+    def spread_of(own, held, sems):
+        return spread_steps(own, held, sems, 0, at)
+
+    body_part, proj_part = own_ref.at[pl.ds(0, MAIN)], own_ref.at[pl.ds(MAIN, PART - MAIN)]
+    body_spread = spread_of(body_part, packed.at[:, :, pl.ds(0, MAIN)], (body_send, body_recv))
+    proj_spread = spread_of(
+        proj_part, packed.at[:, :, pl.ds(MAIN, PART - MAIN)], (proj_send, proj_recv)
+    )
+    z_spread = spread_of(z_ref, every_ref, (z_send, z_recv))
+    body_begin, body_arrive, body_relay, body_finish, body_settled = body_spread
+    proj_begin, proj_arrive, proj_relay, proj_finish, proj_settled = proj_spread
+    z_begin, z_arrive, z_relay, z_finish, z_settled = z_spread
+
+    own_copies = [
+        pltpu.make_async_copy(own_ref, packed.at[plane, wide_at], local_sem.at[0]),
+        pltpu.make_async_copy(
+            outgoing_in_ref.at[me],
+            incoming_ref.at[pl.ds(pl.multiple_of(me * cap, cap), cap)],
+            local_sem.at[1],
+        ),
+    ]
+    for copy in own_copies:
+        copy.start()
+    enter(peers)
+    piece_copies = []
+    for index, (wide_to, plane_to) in enumerate(peers):
+        copy = remote(
+            outgoing_in_ref.at[wide_to * PLANES + plane_to],
+            incoming_ref.at[pl.ds(pl.multiple_of(me * cap, cap), cap)],
+            (piece_send, piece_recv),
+            index,
+            (wide_to, plane_to),
+        )
+        copy.start()
+        piece_copies.append(copy)
+    body_begin()
+
+    text_rows = own_grad_ref.shape[0] * own_grad_ref.shape[1] // BANDS
+    features = cot_ref.shape[0]
+    text_total[...] = jnp.zeros_like(text_total)
+
+    def text_steps(begin, end):
+        @pl.loop(begin, end)
+        def _(step):
+            lanes = pl.ds(pl.multiple_of(step * TEXT_TILE, TEXT_TILE), TEXT_TILE)
+            ids = ids_ref[:, lanes]
+            chosen = band_onehot(ids, text_rows)
+            band = jnp.where(mask_ref[:, lanes] > 0, ids // text_rows, -1)
+            cot = cot_ref[:, lanes].astype(jnp.float32)
+            banded = jnp.concatenate(
+                [jnp.where(band == b, cot, 0.0).astype(jnp.bfloat16) for b in range(BANDS)], axis=0
+            )
+            text_total[...] += dot_nt(chosen, banded)
+
+    text_tiles = ids_ref.shape[1] // TEXT_TILE
+    text_steps(0, text_tiles // 4)
+    body_arrive(1)
+    text_steps(text_tiles // 4, text_tiles // 2)
+    body_relay(0)
+    body_arrive(2)
+    text_steps(text_tiles // 2, text_tiles * 3 // 4)
+    body_relay(1)
+    body_arrive(3)
+    text_steps(text_tiles * 3 // 4, text_tiles)
+    bias_total = jnp.zeros((1, features), jnp.float32)
+    blocks = own_grad_ref.shape[0] // BANDS
+    for b in range(BANDS):
+        rounded = text_total[:, b * features : (b + 1) * features].astype(jnp.bfloat16)
+        own_grad_ref[b * blocks : (b + 1) * blocks] = rounded.reshape(
+            (blocks,) + own_grad_ref.shape[1:]
+        )
+        bias_total = bias_total + over_rows(rounded.astype(jnp.float32))
+    own_bias_ref[...] = bias_total
+    proj_begin()
+    table_copies = []
+    for index, (wide_to, plane_to) in enumerate(peers):
+        copy = remote(
+            own_grad_ref.at[wide_to * PLANES + plane_to],
+            grad_ref.at[me],
+            (table_send, table_recv),
+            index,
+            (wide_to, plane_to),
+        )
+        copy.start()
+        table_copies.append(copy)
+    grad_ref[me] = own_grad_ref[me]
+    body_relay(2)
+    body_relay(3)
+    for distance in range(PLANES):
+        body_finish(distance)
+    proj_arrive(1)
+    proj_arrive(2)
+    proj_arrive(3)
+    for copy in own_copies:
+        copy.wait()
+    body_settled()
+    for copy in piece_copies:
+        copy.wait()
+    def weight_rows(begin, size, plane_at=None):
+        rows = slice(begin, begin + size)
+        if plane_at is None:
+            return packed[:, :, rows, :].reshape(PLANES * wide_count * size, D)
+        return packed[plane_at, :, rows, :].reshape(wide_count * size, D)
+
+    qkv_at, out_at, up_at, down_at, proj_at = 0, 48, 64, 128, MAIN
+    entries = z_ref.shape[0]
+    spot_count = incoming_ref.shape[0]
+    gain_one, shift_one = norms_ref[0:1, :], norms_ref[1:2, :]
+    gain_two, shift_two = norms_ref[2:3, :], norms_ref[3:4, :]
+    gain_end, shift_end = norms_ref[4:5, :], norms_ref[5:6, :]
+
+    def slot_rows(slot):
+        return pl.ds(pl.multiple_of(slot * entries, entries), entries)
+
+    def piece_lanes(slot):
+        return pl.ds(pl.multiple_of((slot - 1) * entries, entries), entries)
+
+    @pl.loop(1, SLOTS)
+    def _(slot):
+        places = lax.broadcasted_iota(jnp.int32, (spot_count, entries), 0)
+        chosen = jnp.where(places == spots_ref[pl.ds(slot, 1), :], 1.0, 0.0).astype(jnp.bfloat16)
+        onehot[:, piece_lanes(slot)] = chosen
+        hats[slot_rows(slot), :] = dot_tn(chosen, incoming_ref[...]) + pos_ref[pl.ds(slot, 1), :]
+
+    first_row = cls_ref[...] + pos_ref[0:1, :]
+    hats[0:entries, :] = jnp.broadcast_to(first_row, (entries, D))
+    sums[...] = jnp.zeros_like(sums)
+
+    @pl.loop(0, SLOTS)
+    def _(slot):
+        rows = slot_rows(slot)
+        hat, scale = normalize(hats[rows, :])
+        hats[rows, :] = hat
+        scales[rows, :] = jnp.broadcast_to(scale, (entries, 128))
+        part = (hat * gain_one + shift_one).astype(jnp.bfloat16)
+        normed[rows, :] = part
+        keys[rows, :] = dot_nt(part, weight_rows(qkv_at, 48)[D:, :])
+
+    query = dot_nt(normed[0:entries, :], weight_rows(qkv_at, 48)[0:D, :])
+    lane_head = lax.broadcasted_iota(jnp.int32, (D, 128), 0) // HDIM
+    to_heads = jnp.where(
+        lane_head == lax.broadcasted_iota(jnp.int32, (D, 128), 1), 1.0, 0.0
+    ).astype(jnp.bfloat16)
+    head_lane = lax.broadcasted_iota(jnp.int32, (128, D), 1) // HDIM
+    from_heads = jnp.where(
+        head_lane == lax.broadcasted_iota(jnp.int32, (128, D), 0), 1.0, 0.0
+    ).astype(jnp.bfloat16)
+    root = 1.0 / math.sqrt(HDIM)
+    scores = []
+    for slot in range(SLOTS):
+        rows = slice(slot * entries, (slot + 1) * entries)
+        value = two_part_dot(query * keys[rows, 0:D], to_heads) * root
+        scores.append(jnp.where(live_ref[:, slot : slot + 1] > 0, value, -1e30))
+    top = scores[0]
+    for value in scores[1:]:
+        top = jnp.maximum(top, value)
+    scores = [jnp.exp(value - top) for value in scores]
+    whole = scores[0]
+    for value in scores[1:]:
+        whole = whole + value
+    attended = jnp.zeros((entries, D), jnp.float32)
+    for slot in range(SLOTS):
+        rows = slice(slot * entries, (slot + 1) * entries)
+        share = scores[slot] / whole
+        probs[rows, :] = share
+        attended = attended + two_part_dot(share, from_heads) * keys[rows, D:]
+    attended_bf = attended.astype(jnp.bfloat16)
+    residual = first_row + dot_nt(attended_bf, weight_rows(out_at, 16))
+    hat_two, scale_two = normalize(residual)
+    normed_two = (hat_two * gain_two + shift_two).astype(jnp.bfloat16)
+    span = 512
+    second = residual + bias_down_ref[...]
+    for begin in range(0, FF, span):
+        lanes = slice(begin, begin + span)
+        gate = dot_nt(normed_two, weight_rows(up_at, 64, begin // span)) + bias_up_ref[:, lanes]
+        square = gate * gate
+        bend = jnp.tanh(math.sqrt(2.0 / math.pi) * (gate + 0.044715 * square * gate))
+        part = (0.5 * gate * (1.0 + bend)).astype(jnp.bfloat16)
+        active[:, lanes] = part
+        slope[:, lanes] = 0.5 * (1.0 + bend) + 0.5 * gate * (1.0 - bend * bend) * (
+            math.sqrt(2.0 / math.pi) * (1.0 + 3.0 * 0.044715 * square)
+        )
+        second = second + plain_dot(part, weight_rows(down_at, 64, begin // span))
+    hat_end, scale_end = normalize(second)
+    z_ref[...] = (hat_end * gain_end + shift_end).astype(jnp.bfloat16)
+
+    z_begin()
+    own_z = pltpu.make_async_copy(z_ref, every_ref.at[plane, wide_at], local_sem.at[2])
+    own_z.start()
+    for distance in range(PLANES):
+        proj_relay(distance)
+    for distance in range(PLANES):
+        proj_finish(distance)
+    z_arrive(1)
+    proj_settled()
+    for copy in table_copies:
+        copy.wait()
+    own_proj_ref[...] = packed[me // wide_count, lax.rem(me, wide_count), MAIN:, :]
+    grad_z = jnp.zeros((entries, D), jnp.float32)
+    for source in range(grad_ref.shape[0]):
+        grad_z = grad_z + plain_dot(
+            grad_ref[source], packed[source // wide_count, source % wide_count, MAIN:, :]
+        )
+    vec_ref[...] = jnp.zeros_like(vec_ref)
+    vec_ref[13:14, :] = over_rows(grad_z * hat_end)
+    vec_ref[14:15, :] = over_rows(grad_z)
+    grad_second = normalize_back(grad_z, gain_end, hat_end, scale_end)
+    branch_two = grad_second.astype(jnp.bfloat16)
+    vec_ref[15:16, :] = over_rows(branch_two.astype(jnp.float32))
+
+    def store(value, block, chunk, height, offset):
+        for chip_at in range(CHIPS):
+            for core_at in range(CORES):
+                top = (chip_at * CORES + core_at) * height
+                main_ref[core_at, chunk, chip_at, block, offset : offset + height, :] = value[
+                    top : top + height, :
+                ].astype(jnp.bfloat16)
+
+    z_arrive(2)
+    z_relay(0)
+    grad_two = jnp.zeros((entries, D), jnp.float32)
+    for block in range(PLANES):
+        lanes = slice(block * span, (block + 1) * span)
+        store(dot_tn(active[:, lanes], branch_two), block, 0, 64, 0)
+        gate_grad = (dot_nt(branch_two, weight_rows(down_at, 64, block)) * slope[:, lanes]).astype(jnp.bfloat16)
+        wide_ref[:, lanes] = over_rows(gate_grad.astype(jnp.float32))
+        store(dot_tn(gate_grad, normed_two), block, 1, 64, 0)
+        grad_two = grad_two + plain_dot(gate_grad, weight_rows(up_at, 64, block))
+    z_arrive(3)
+    z_relay(1)
+    vec_ref[11:12, :] = over_rows(grad_two * hat_two)
+    vec_ref[12:13, :] = over_rows(grad_two)
+    grad_residual = grad_second + normalize_back(grad_two, gain_two, hat_two, scale_two)
+    branch_one = grad_residual.astype(jnp.bfloat16)
+    grad_out = dot_tn(branch_one, attended_bf)
+    for block in range(PLANES):
+        store(grad_out[block * 128 : (block + 1) * 128, :], block, 2, 16, 0)
+    grad_attended = plain_dot(branch_one, weight_rows(out_at, 16))
+
+    z_relay(2)
+    z_finish(0)
+    inner = jnp.zeros((entries, 128), jnp.float32)
+    slides = []
+    for slot in range(SLOTS):
+        rows = slice(slot * entries, (slot + 1) * entries)
+        value = two_part_dot(grad_attended * keys[rows, D:], to_heads)
+        slides.append(value)
+        inner = inner + probs[rows, :] * value
+    grad_query = jnp.zeros((entries, D), jnp.float32)
+    for slot in range(SLOTS):
+        rows = slice(slot * entries, (slot + 1) * entries)
+        share = probs[rows, :]
+        grad_kv[rows, D:] = (two_part_dot(share, from_heads) * grad_attended).astype(jnp.bfloat16)
+        push = two_part_dot(share * (slides[slot] - inner), from_heads) * root
+        grad_query = grad_query + push * keys[rows, 0:D]
+        grad_kv[rows, 0:D] = (push * query).astype(jnp.bfloat16)
+    z_relay(3)
+    z_finish(1)
+    query_bf = grad_query.astype(jnp.bfloat16)
+
+    grad_q = dot_tn(query_bf, normed[0:entries, :])
+    grad_k = dot_tn(grad_kv[:, 0:D], normed[...])
+    grad_v = dot_tn(grad_kv[:, D:], normed[...])
+    third = D * 3 // PLANES
+    every = jnp.concatenate([grad_q, grad_k, grad_v], axis=0)
+    for block in range(PLANES):
+        store(every[block * third : (block + 1) * third, :], block, 2, 48, 16)
+
+    @pl.loop(0, SLOTS)
+    def _(slot):
+        rows = slot_rows(slot)
+        grad_normed[rows, :] = plain_dot(grad_kv[rows, :], weight_rows(qkv_at, 48)[D:, :])
+
+    grad_normed[0:entries, :] += plain_dot(query_bf, weight_rows(qkv_at, 48)[0:D, :])
+
+    @pl.loop(0, SLOTS)
+    def _(slot):
+        rows = slot_rows(slot)
+        grad = grad_normed[rows, :]
+        hat = hats[rows, :]
+        sums[0:1, :] += over_rows(grad * hat)
+        sums[1:2, :] += over_rows(grad)
+        grad_x = normalize_back(grad, gain_one, hat, scales[rows, 0:1])
+        vec_ref[pl.ds(1 + slot, 1), :] = over_rows(grad_x)
+
+        @pl.when(slot > 0)
+        def _():
+            grad_pieces[pl.ds(pl.multiple_of((slot - 1) * entries, entries), entries), :] = (
+                grad_x.astype(jnp.bfloat16)
+            )
+
+    z_finish(2)
+    z_finish(3)
+    vec_ref[9:11, :] = sums[0:2, :]
+    vec_ref[1:2, :] += over_rows(grad_residual)
+    vec_ref[0:1, :] = vec_ref[1:2, :]
+    tile = 256
+    for begin in range(0, spot_count, tile):
+        outgoing_ref[begin : begin + tile, :] = plain_dot(
+            onehot[begin : begin + tile, :], grad_pieces[...]
+        ).astype(jnp.bfloat16)
+    own_z.wait()
+    z_settled()
+
+
+def layer(outgoing, own_part, flat_ids, flat_mask, text_cot, spots, live, vectors):
+    f32, bf = jnp.float32, jnp.bfloat16
+    dma = pltpu.SemaphoreType.DMA
+    count, cap = outgoing.shape[:2]
+    entries = live.shape[0]
+    features = text_cot.shape[0]
+    rows = entries * SLOTS
+    hbm = pl.BlockSpec(memory_space=pl.ANY)
+    vmem = pl.BlockSpec(memory_space=pltpu.VMEM)
+    spread_count = 6 + 9 * PLANES
+    return pl.pallas_call(
+        layer_kernel,
+        out_shape=(
+            jax.ShapeDtypeStruct((PLANES, CHIPS * CORES, entries, D), bf),
+            jax.ShapeDtypeStruct((CORES, CHUNKS, CHIPS, PLANES, CHUNK, D), bf),
+            jax.ShapeDtypeStruct((count * cap, D), bf),
+            jax.ShapeDtypeStruct((16, D), f32),
+            jax.ShapeDtypeStruct((1, FF), f32),
+            jax.ShapeDtypeStruct((count, entries, features), bf),
+            jax.ShapeDtypeStruct((1, features), f32),
+            jax.ShapeDtypeStruct((features, D), bf),
+        ),
+        in_specs=[hbm, hbm] + [vmem] * 10,
+        out_specs=(hbm,) + (vmem,) * 7,
+        scratch_shapes=[
+            pltpu.VMEM((count * cap, D), bf),
+            pltpu.VMEM((count, entries, features), bf),
+            pltpu.VMEM((PLANES, CHIPS * CORES, PART, D), bf),
+            pltpu.VMEM((count * entries // BANDS, BANDS * features), f32),
+            pltpu.VMEM((entries, D), bf),
+            pltpu.VMEM((count * cap, entries * PSLOTS), bf),
+            pltpu.VMEM((rows, D), f32),
+            pltpu.VMEM((rows, 128), f32),
+            pltpu.VMEM((rows, D), bf),
+            pltpu.VMEM((rows, 2 * D), f32),
+            pltpu.VMEM((rows, 128), f32),
+            pltpu.VMEM((rows, 2 * D), bf),
+            pltpu.VMEM((rows, D), f32),
+            pltpu.VMEM((entries * PSLOTS, D), bf),
+            pltpu.VMEM((entries, FF), bf),
+            pltpu.VMEM((entries, FF), f32),
+            pltpu.VMEM((8, D), f32),
+            dma((3,)),
+            dma((count - 1,)),
+            dma((count - 1,)),
+            dma((count - 1,)),
+            dma((count - 1,)),
+            dma((spread_count,)),
+            dma((spread_count,)),
+            dma((spread_count,)),
+            dma((spread_count,)),
+            dma((spread_count,)),
+            dma((spread_count,)),
+        ],
+        compiler_params=pltpu.CompilerParams(
+            collective_id=5, has_side_effects=True, vmem_limit_bytes=62 * 2**20
+        ),
+        name="layer",
+    )(outgoing, own_part, flat_ids[None], flat_mask[None], text_cot, spots, live, *vectors)
+
+
+def own_weight_part(mat_master):
+    wide_count = CHIPS * CORES
+    wide_at = lax.axis_index("wide")
+    parts = []
+    for segment in block_slices(mat_master[0], PLANES):
+        rows = segment.shape[0] // wide_count
+        parts.append(
+            lax.dynamic_slice_in_dim(segment, wide_at * rows, rows, 0).astype(jnp.bfloat16)
+        )
+    return jnp.concatenate(parts, axis=0)
+
+
+def gather_ids(slot_ids):
+    count = slot_ids.shape[0]
+    lanes = 128
+    rows = -(-count // (8 * lanes)) * 8
+    padded = jnp.pad(slot_ids, (0, rows * lanes - count)).reshape(rows, lanes)
+    every = tell(padded, 1)
+    return every.reshape(every.shape[0], rows * lanes)[:, :count]
+
+
+def asked_onehot_of(every_ids, group_rows, cap):
+    me = lax.axis_index("wide") * PLANES + lax.axis_index("narrow")
+    slot_count = every_ids.shape[1]
+    asked = every_ids // group_rows == me
+    before = (
+        lax.broadcasted_iota(jnp.int32, (slot_count, slot_count), 0)
+        < lax.broadcasted_iota(jnp.int32, (slot_count, slot_count), 1)
+    )
+    asked_rank = jnp.dot(
+        asked.astype(jnp.bfloat16), before.astype(jnp.bfloat16), preferred_element_type=jnp.float32
+    ).astype(jnp.int32)
+    asked_rank = jnp.where(asked, asked_rank, -1)
+    chosen = asked_rank[:, None, :] == lax.iota(jnp.int32, cap)[None, :, None]
+    local_ids = every_ids - me * group_rows + 1
+    asked_rows = jnp.sum(jnp.where(chosen, local_ids[:, None, :], 0), axis=2).reshape(-1) - 1
+    return (asked_rows[:, None] == lax.iota(jnp.int32, group_rows)[None, :]).astype(jnp.bfloat16)
+
+
+def own_spots_of(slot_ids, group_rows, cap):
+    slot_count = slot_ids.shape[0]
+    before = (
+        lax.broadcasted_iota(jnp.int32, (slot_count, slot_count), 0)
+        > lax.broadcasted_iota(jnp.int32, (slot_count, slot_count), 1)
+    )
+    own_group = slot_ids // group_rows
+    same = (own_group[:, None] == own_group[None, :]) & before
+    own_rank = jnp.sum(same.astype(jnp.int32), axis=1)
+    return (own_group * cap + own_rank).reshape(-1, PSLOTS)
+
+
+def on_device(
+    piece_table,
+    piece_ids,
+    slot_mask,
+    text_ids,
+    text_mask,
+    text_cot,
+    mat_master,
+    mat_momentum,
+    mat_ema,
+    vec_master,
+    vec_moment1,
+    vec_moment2,
+    vec_ema,
+):
+    device_count = PLANES * CHIPS * CORES
+    me = lax.axis_index("wide") * PLANES + lax.axis_index("narrow")
+    (
+        cls_vec,
+        positions,
+        ln1_gain,
+        ln1_shift,
+        ln2_gain,
+        ln2_shift,
+        final_gain,
+        final_shift,
+        bias_up,
+        bias_down,
+        bias_out,
+    ) = split_vectors(vec_master)
+    entries = piece_ids.shape[0]
+    slot_ids = piece_ids.reshape(-1)
+    group_rows = piece_table.shape[0]
+    cap = piece_cap(group_rows)
+    flat_ids = text_ids.reshape(-1)
+    flat_mask = text_mask.reshape(-1)
+    feature_rows = text_cot.shape[0]
+
+    every_ids = gather_ids(slot_ids)
+    asked_onehot = asked_onehot_of(every_ids, group_rows, cap)
+    outgoing = jnp.dot(asked_onehot, piece_table, preferred_element_type=jnp.float32)
+    outgoing = outgoing.astype(jnp.bfloat16).reshape(device_count, cap, D)
+    spots = own_spots_of(slot_ids, group_rows, cap)
+    spots = jnp.pad(spots.T, ((1, 0), (0, 0)))
+    live = jnp.concatenate([jnp.ones((entries, 1), jnp.int32), slot_mask], axis=1)
+    live = jnp.pad(live.astype(jnp.float32), ((0, 0), (0, 128 - SLOTS)))
+
+    norms = jnp.stack([ln1_gain, ln1_shift, ln2_gain, ln2_shift, final_gain, final_shift])
+    (
+        every_normed,
+        main,
+        grad_outgoing,
+        vec_rows,
+        grad_bias_up,
+        grad_own,
+        grad_bias_own,
+        proj_own,
+    ) = layer(
+        outgoing,
+        own_weight_part(mat_master),
+        flat_ids,
+        flat_mask,
+        text_cot,
+        spots,
+        live,
+        (cls_vec[None], positions, norms, bias_up[None], bias_down[None]),
+    )
+    bias_own = lax.dynamic_slice_in_dim(bias_out, me * feature_rows, feature_rows, 0)
+    vec_local = jnp.concatenate(
+        [
+            vec_rows[:15].reshape(-1),
+            grad_bias_up[0],
+            vec_rows[15],
+            lax.dynamic_update_slice_in_dim(
+                jnp.zeros((OUTW,), jnp.float32), grad_bias_own[0], me * feature_rows, 0
+            ),
+        ]
+    )
+    vec_rows = vec_local.reshape(-1, D)
+    vec_rows = jnp.pad(vec_rows, ((0, CORES * VROWS - vec_rows.shape[0]), (0, 0)))
+    text_embeds, main_sum, proj_sum, vec_sum, gram, high, low = settle(
+        every_normed,
+        main,
+        vec_rows.reshape(CORES, VROWS, D),
+        grad_own,
+        proj_own,
+        bias_own[:, None],
+        mat_momentum[0],
+        flat_ids,
+        flat_mask,
+    )
+    vec_grad = vec_sum.reshape(-1)[: vec_local.shape[0]]
+    grad_outgoing, _ = lax.optimization_barrier((grad_outgoing, gram))
+    grad_incoming = lax.all_to_all(
+        grad_outgoing.reshape(device_count, cap, D), BOTH, 0, 0, tiled=True
+    ).reshape(device_count * cap, D)
+    rows = muon_rows(gram, high, low)
+    grad_block, momentum_block, weight_block, ema_block = finish(
+        main_sum, proj_sum, rows, mat_momentum, mat_master, mat_ema
+    )
+    piece_grad = contract_rows(asked_onehot, grad_incoming)
+    return (
+        text_embeds,
+        piece_grad,
+        grad_block,
+        momentum_block,
+        weight_block,
+        ema_block,
+    ) + adam(vec_grad, vec_master, vec_moment1, vec_moment2, vec_ema)
 
 
 def solution(mesh):
@@ -417,6 +2067,8 @@
         P(),
         P(),
     )
+    fits = mesh.shape["wide"] == CHIPS * CORES and mesh.shape["narrow"] == PLANES
+    step = on_device if fits else on_device_plain
     return jax.shard_map(
-        on_device, mesh=mesh, in_specs=in_specs, out_specs=out_specs, check_vma=False
-    )
+        step, mesh=mesh, in_specs=in_specs, out_specs=out_specs, check_vma=False
+    )

time: 921 us -> 408 us (0.44)
  Pallas kernels: 0 us -> 338 us
  waiting for transfers between devices: 293 us -> 0.01 us
  matrix products: 228 us -> 10.5 us
  blocking collectives: 146 us -> 0 us
  local copies, waits for them, and re-layouts: 129 us -> 33.8 us
  other arithmetic: 59.9 us -> 6.41 us
  starting transfers between devices: 32.6 us -> 10.6 us
  between operations: 19.6 us -> 1.18 us
    pallas_call x0 -> x5, Pallas kernels: none -> 338 us  [the longest x1 162 us: layer(): pl.pallas_call(layer_kernel, out_shape=(jax.ShapeDtypeStruct((PLANES, CHI...]
    dot_general x126 -> x1, matrix products: 211 us -> 0.35 us  [asked_onehot_of(): jnp.dot(asked.astype(jnp.bfloat16), before.astype(jnp.bfloat16), preferre...]
    all_to_all x3 -> x0, waiting for transfers between devices: 145 us -> none  [the longest x1 103 us: on_device(): terms = lax.all_to_all(packed_term, BOTH, 0, 0, tiled=True)]
    all_gather x1 -> x0, blocking collectives: 101 us -> none  [on_device(): every_ids = lax.all_gather(slot_ids, BOTH, axis=0, tiled=False)]
    psum x1 -> x0, waiting for transfers between devices: 77.9 us -> none  [on_device(): lax.psum(jnp.stack([gram_of(segment) for segment in segments]), 'narrow')]
    all_gather x4 -> x0, waiting for transfers between devices: 70.1 us -> none  [the longest x1 47.7 us: on_device(): every_normed = lax.all_gather(normed_three_bf, BOTH, axis=0, tiled=True)]
    gather x6 -> x0, local copies, waits for them, and re-layouts: 64.7 us -> none  [the longest x5 36.8 us: on_device(): square = jnp.sum(jnp.diagonal(grams[position]))]
    psum x1 -> x0, blocking collectives: 44.6 us -> none  [on_device(): vec_grad = lax.psum(vec_local, BOTH)]
  transfers between devices with their start and end apart: 9 -> 1, of which waited for: 5 -> 0; matrix products, arithmetic and copies ran while one was open for 22% -> 0% of each run, Pallas kernels for 0% -> 17%
where the time goes in v3:
time: 408 us; the launch traced here: 401 us
  Pallas kernels  338 us (83%)
  local copies, waits for them, and re-layouts  33.8 us (8%)
  starting transfers between devices  10.6 us (3%)
  matrix products  10.5 us (3%)
  other arithmetic  6.41 us (2%)
    pallas_call x1, Pallas kernels, layer(): pl.pallas_call(layer_kernel, out_shape=(jax.ShapeDtypeStruct((PLANES, CHI...  162 us
    pallas_call x1, Pallas kernels, settle(): pl.pallas_call(settle_kernel, out_shape=(jax.ShapeDtypeStruct((features,...  98.3 us
    pallas_call x1, Pallas kernels, muon_rows(): pl.pallas_call(muon_kernel, out_shape=jax.ShapeDtypeStruct((total, D), jn...  45.6 us
    pallas_call x1, Pallas kernels, finish(): pl.pallas_call(finish_kernel, grid=(MAIN_TILES + MOST_TILES,), out_shape=...  21 us
    pallas_call x1, Pallas kernels, tell(): pl.pallas_call(tell_kernel, out_shape=jax.ShapeDtypeStruct((every,) + val...  10.8 us
    all_to_all x1, starting transfers between devices, on_device(): lax.all_to_all(grad_outgoing.reshape(device_count, cap, D), BOTH, 0, 0, t...  10.6 us
    unnamed x49, local copies, waits for them, and re-layouts  10.2 us
  transfers between devices with their start and end apart: 1, of which 0 were waited for; matrix products, arithmetic and copies ran while one was open for 0% of the time, Pallas kernels for 17%

profile of v3, /device:TPU:31, one launch (start us, length us, event | category | flops | bytes accessed | tf_op | source)
XLA Modules:
  0.0 400.6 jit_solution(2467895282912527012)
XLA Ops:
  0.7 1.3 slice.76
  1.9 1.6 slice.77
  3.6 1.7 fusion.46
  5.3 1.7 slice.80
  10.0 1.4 fusion.48
  11.4 1.4 fusion.47
  12.8 1.3 slice.90
  14.1 10.8 %tell_ids.1 = s32[32,8,128]{2,1,0:T(8,128)} custom-call(s32[8,128]{1,0:T(8,128)} %pad_bitcast_fusion.own_ref), custom_call_target="tpu_custom_call" | custom-call | tf_op jit(solution)/shard_map/tell_ids/pallas_call | solution.py:1284
  27.7 1.4 copy.35
  29.1 1.4 copy.36
  34.8 1.4 copy.32
  36.2 1.6 pad_convert_fusion
  37.8 1.3 slice.83.pos_ref
  39.1 4.3 %fusion.6 = bf16[2048,512]{1,0:T(8,128)(2,1)} fusion(bf16[1024,512]{1,0:T(8,128)(2,1)S(1)} %copy-done, s32[2048]{0:T(1024)} %sub.33), kind=kOutput, calls=%fused_computation.12 | convolution fusion | flops 2150629376 | bytes 3153920 | tf_op jit(solution)/shard_map/dot_general | solution.py:1970
  44.1 1.5 pad.19.live_ref
  45.7 1.3 stack.27.norms_ref
  47.0 162.4 %layer.1 = (bf16[4,8,128,512]{3,2,1,0:T(8,128)(2,1)}, bf16[2,3,4,4,64,512]{5,4,3,2,1,0:T(8,128)(2,1)}, bf16[2048,512]{1,0:T(8,128)(2,1)}, f32[16,512]{1,0:T(8,12...) custom-call(bf16[32,64,512]{2,1,0:T(8,128)(2,1)} %bitcast.64, ...), custom_call_target="tpu_custom_call" | custom-call | tf_op jit(solution)/shard_map/layer/pallas_call | solution.py:1828
  214.5 98.3 %settle.1 = (f32[128,8192]{1,0:T(8,128)}, bf16[1536,512]{1,0:T(8,128)(2,1)}, bf16[2,4,4,32,512]{4,3,2,1,0:T(8,128)(2,1)}, f32[2,16,512]{2,1,0:T(8,128)}, f32[512...) custom-call(bf16[4,8,128,512]{3,2,1,0:T(8,128)(2,1)} %get-tuple-element.31.every, ...), custom_call_target="tpu_custom_call" | custom-call | tf_op jit(solution)/shard_map/settle/pallas_call | solution.py:955
  312.8 10.6 %all-to-all-start = ((bf16[32,64,512]{2,1,0:T(8,128)(2,1)}), bf16[32,64,512]{2,1,0:T(8,128)(2,1)}, u32[]{:S(2)}, u32[]{:S(2)}) async-start(bf16[32,64,512]{2,1,0:T(8,128)(2,1)} %bitcast.63), calls=%async_computation | async-start | bytes 4194304 | tf_op jit(solution)/shard_map/all_to_all | solution.py:2023
  323.5 45.6 %muon_rows.1.rows_ref = bf16[2560,512]{1,0:T(8,128)(2,1)S(1)} custom-call(f32[512,512]{1,0:T(8,128)S(1)} %copy-done.3, bf16[8,128,512]{2,1,0:T(8,128)(2,1)S(1)} %copy-done.4, bf16[8,128,512]{2,1,0:T(8,128)(2,1)S(1)} %copy-done.5), custom_call_target="tpu_custom_call" | custom-call | tf_op jit(solution)/shard_map/muon_rows/pallas_call | solution.py:1196
  369.2 1.5 copy-done.2
  370.7 21.0 %finish.1 = (f32[1,2560,512]{2,1,0:T(8,128)}, f32[1,2560,512]{2,1,0:T(8,128)}, f32[1,2560,512]{2,1,0:T(8,128)}, f32[1,2560,512]{2,1,0:T(8,128)}) custom-call(bf16[1536,512]{1,0:T(8,128)(2,1)} %get-tuple-element.42.main_ref, bf16[8,4,32,512]{3,2,1,0:T(8,128)(2,1)} %bitcast.65, bf16[2560,512]{1,0:T(8,128)(2,1)} %copy-done.2, f32[1,2560,512]{2,1,0:T(8,128)} %momentum_ref.1, ...), custom_call_target="tpu_custom_call" | custom-call | flops 15728640 | bytes 41943040 | tf_op jit(solution)/shard_map/finish/pallas_call | solution.py:1241
  392.4 5.9 %fusion = f32[1024,512]{1,0:T(8,128)} fusion(bf16[2048,512]{1,0:T(8,128)(2,1)} %bitcast.25, s32[2048]{0:T(1024)S(1)} %copy-done.18), kind=kOutput, calls=%fused_computation.1 | convolution fusion | flops 2149580800 | bytes 4202496 | tf_op jit(solution)/shard_map/dot_general | solution.py:117
  398.3 2.0 copy.46
  (69 shorter events, 16.7 us)
Async XLA Ops:
  0.6 38.5 %copy-start = (bf16[1024,512]{1,0:T(8,128)(2,1)S(1)}, bf16[1024,512]{1,0:T(8,128)(2,1)}, u32[]{:S(2)}) copy-start(bf16[1024,512]{1,0:T(8,128)(2,1)} %param.13) | copy-start | bytes 3145732
  0.7 6.3 %copy-start.13 = (s32[128,7]{0,1:T(8,128)S(1)}, s32[128,7]{0,1:T(8,128)}, u32[]{:S(2)}) copy-start(s32[128,7]{0,1:T(8,128)} %param.14) | copy-start | bytes 10756
  39.1 6.5 %copy-start.14 = (f32[512]{0:T(512)S(1)}, f32[512]{0:T(512)}, u32[]{:S(2)}) copy-start(f32[512]{0:T(512)} %get-tuple-element.61) | copy-start | bytes 6148
  39.1 6.5 %copy-start.15 = (f32[512]{0:T(512)S(1)}, f32[512]{0:T(512)}, u32[]{:S(2)}) copy-start(f32[512]{0:T(512)} %get-tuple-element.62) | copy-start | bytes 6148
  39.1 6.5 %copy-start.16 = (f32[512]{0:T(512)S(1)}, f32[512]{0:T(512)}, u32[]{:S(2)}) copy-start(f32[512]{0:T(512)} %get-tuple-element.63) | copy-start | bytes 6148
  39.1 6.6 %copy-start.17 = (f32[512]{0:T(512)S(1)}, f32[512]{0:T(512)}, u32[]{:S(2)}) copy-start(f32[512]{0:T(512)} %get-tuple-element.64) | copy-start | bytes 6148
  45.6 1.4 copy-start.7
  312.8 10.7 %copy-start.9 = (f32[2,16,512]{2,1,0:T(8,128)S(1)}, f32[2,16,512]{2,1,0:T(8,128)}, u32[]{:S(2)}) copy-start(f32[2,16,512]{2,1,0:T(8,128)} %get-tuple-element.50) | copy-start | bytes 196612
  312.8 10.7 %copy-start.3 = (f32[512,512]{1,0:T(8,128)S(1)}, f32[512,512]{1,0:T(8,128)}, u32[]{:S(2)}) copy-start(f32[512,512]{1,0:T(8,128)} %get-tuple-element.40.gram_ref) | copy-start | bytes 3145732
  312.8 10.7 %copy-start.4 = (bf16[8,128,512]{2,1,0:T(8,128)(2,1)S(1)}, bf16[8,128,512]{2,1,0:T(8,128)(2,1)}, u32[]{:S(2)}) copy-start(bf16[8,128,512]{2,1,0:T(8,128)(2,1)} %get-tuple-element.44.high_ref) | copy-start | bytes 3145732
  312.8 10.7 %copy-start.5 = (bf16[8,128,512]{2,1,0:T(8,128)(2,1)S(1)}, bf16[8,128,512]{2,1,0:T(8,128)(2,1)}, u32[]{:S(2)}) copy-start(bf16[8,128,512]{2,1,0:T(8,128)(2,1)} %get-tuple-element.45.low_ref) | copy-start | bytes 3145732
  312.8 79.6 %all-to-all-start = ((bf16[32,64,512]{2,1,0:T(8,128)(2,1)}), bf16[32,64,512]{2,1,0:T(8,128)(2,1)}, u32[]{:S(2)}, u32[]{:S(2)}) async-start(bf16[32,64,512]{2,1,0:T(8,128)(2,1)} %bitcast.63), calls=%async_computation | async-start | bytes 4194304 | tf_op jit(solution)/shard_map/all_to_all | solution.py:2023
  369.2 1.5 copy-start.2
  370.7 21.0 %copy-start.8 = (f32[14336]{0:T(1024)S(1)}, f32[14336]{0:T(1024)}, u32[]{:S(2)}) copy-start(f32[14336]{0:T(1024)} %param.22) | copy-start | bytes 172036
  370.7 21.0 %copy-start.10 = (f32[14336]{0:T(1024)S(1)}, f32[14336]{0:T(1024)}, u32[]{:S(2)}) copy-start(f32[14336]{0:T(1024)} %param.25) | copy-start | bytes 172036
  370.7 21.0 %copy-start.11 = (f32[14336]{0:T(1024)S(1)}, f32[14336]{0:T(1024)}, u32[]{:S(2)}) copy-start(f32[14336]{0:T(1024)} %param.24) | copy-start | bytes 172036
  370.7 21.1 %copy-start.12 = (f32[14336]{0:T(1024)S(1)}, f32[14336]{0:T(1024)}, u32[]{:S(2)}) copy-start(f32[14336]{0:T(1024)} %param.23) | copy-start | bytes 172036
  370.7 21.8 %copy-start.18 = (s32[2048]{0:T(1024)S(1)}, s32[2048]{0:T(1024)}, u32[]{:S(2)}) copy-start(s32[2048]{0:T(1024)} %sub.33) | copy-start | bytes 24580
  392.4 5.9 %copy-start.6 = (f32[128,8192]{1,0:T(8,128)S(1)}, f32[128,8192]{1,0:T(8,128)}, u32[]{:S(2)}) copy-start(f32[128,8192]{1,0:T(8,128)} %get-tuple-element.79) | copy-start | bytes 12582916
  398.3 2.0 copy-start.1

commit v4 on v1

--- a/solution.py
+++ b/solution.py
@@ -4,6 +4,8 @@
 import jax
 import jax.numpy as jnp
 from jax import lax
+from jax.experimental import pallas as pl
+from jax.experimental.pallas import tpu as pltpu
 from jax.sharding import PartitionSpec as P
 
 D = 512
@@ -121,7 +123,17 @@
     return lax.dot_general(block, block, (((0,), (0,)), ((), ())), precision=HIGHEST)
 
 
-def on_device(
+def adam(vec_grad, vec_master, vec_moment1, vec_moment2, vec_ema):
+    moment_one = ADAM_BETA1 * vec_moment1 + (1.0 - ADAM_BETA1) * vec_grad
+    moment_two = ADAM_BETA2 * vec_moment2 + (1.0 - ADAM_BETA2) * vec_grad * vec_grad
+    corrected_one = moment_one / (1.0 - ADAM_BETA1**STEP)
+    corrected_two = moment_two / (1.0 - ADAM_BETA2**STEP)
+    vec_weight = vec_master - ADAM_RATE * corrected_one / (jnp.sqrt(corrected_two) + ADAM_EPSILON)
+    vec_ema_new = EMA_DECAY * vec_ema + (1.0 - EMA_DECAY) * vec_weight
+    return vec_grad, moment_one, moment_two, vec_weight, vec_ema_new
+
+
+def on_device_plain(
     piece_table,
     piece_ids,
     slot_mask,
@@ -367,12 +379,6 @@
         )
     weight_block = jnp.concatenate(new_segments, axis=0)[None]
     ema_block = EMA_DECAY * mat_ema + (1.0 - EMA_DECAY) * weight_block
-    moment_one = ADAM_BETA1 * vec_moment1 + (1.0 - ADAM_BETA1) * vec_grad
-    moment_two = ADAM_BETA2 * vec_moment2 + (1.0 - ADAM_BETA2) * vec_grad * vec_grad
-    corrected_one = moment_one / (1.0 - ADAM_BETA1**STEP)
-    corrected_two = moment_two / (1.0 - ADAM_BETA2**STEP)
-    vec_weight = vec_master - ADAM_RATE * corrected_one / (jnp.sqrt(corrected_two) + ADAM_EPSILON)
-    vec_ema_new = EMA_DECAY * vec_ema + (1.0 - EMA_DECAY) * vec_weight
     return (
         text_embeds,
         piece_grad,
@@ -380,12 +386,1725 @@
         momentum_block[None],
         weight_block,
         ema_block,
-        vec_grad,
-        moment_one,
-        moment_two,
-        vec_weight,
-        vec_ema_new,
-    )
+    ) + adam(vec_grad, vec_master, vec_moment1, vec_moment2, vec_ema)
+
+
+MESH_ID = pl.DeviceIdType.MESH
+CORES = 2
+CHIPS = 4
+PLANES = 4
+MAIN = 192
+CHUNKS = 3
+CHUNK = MAIN // CHUNKS
+PROJ = 32
+PART = MAIN + PLANES * PROJ
+VROWS = 16
+
+
+def place():
+    wide_at = lax.axis_index("wide")
+    plane = lax.axis_index("narrow")
+    chip = wide_at // CORES
+    core = lax.rem(wide_at, CORES)
+    return wide_at, plane, chip, core
+
+
+def enter(targets):
+    barrier = pltpu.get_barrier_semaphore()
+    for target in targets:
+        pl.semaphore_signal(barrier, inc=1, device_id=target, device_id_type=MESH_ID)
+    pl.semaphore_wait(barrier, len(targets))
+
+
+def neighbours(wide_at, plane, chip, core):
+    sibling = (chip * CORES + 1 - core, plane)
+    chips = [(lax.rem(chip + k, CHIPS) * CORES + core, plane) for k in range(1, CHIPS)]
+    planes = [(wide_at, lax.rem(plane + k, PLANES)) for k in range(1, PLANES)]
+    return sibling, chips, planes
+
+
+def remote(src, dst, sems, index, target):
+    return pltpu.make_async_remote_copy(
+        src_ref=src,
+        dst_ref=dst,
+        send_sem=sems[0].at[index],
+        recv_sem=sems[1].at[index],
+        device_id=target,
+        device_id_type=MESH_ID,
+    )
+
+OWNERS = (6, 7, 2, 4, 0)
+BLOCK_TILES = (3, 1, 4, 4, 8)
+MOST_TILES = max(BLOCK_TILES)
+MAIN_TILES = 12
+BANDS = 4
+TEXT_TILE = 512
+TILE = 128
+SIDE = 2
+STRIPS = 8
+STRIP = D // STRIPS
+PACKED = 640
+PIECES = ((0, 64, 1024), (64, 64, 512), (128, 16, 384), (144, 48, 0))
+
+
+def halves(value):
+    high = value.astype(jnp.bfloat16)
+    return high, (value - high.astype(jnp.float32)).astype(jnp.bfloat16)
+
+
+def plain_dot(left, right):
+    return jnp.dot(left, right, preferred_element_type=jnp.float32)
+
+
+def split_dot(left, right):
+    return plain_dot(left[0], right[0]) + (
+        plain_dot(left[0], right[1]) + plain_dot(left[1], right[0])
+    )
+
+
+def dot_nt(left, right):
+    return lax.dot_general(
+        left, right, (((1,), (1,)), ((), ())), preferred_element_type=jnp.float32
+    )
+
+
+def dot_tn(left, right):
+    return lax.dot_general(
+        left, right, (((0,), (0,)), ((), ())), preferred_element_type=jnp.float32
+    )
+
+
+def band_onehot(ids, rows):
+    place_in = lax.rem(ids, rows)
+    spots = lax.broadcasted_iota(jnp.int32, (rows, ids.shape[1]), 0)
+    return jnp.where(spots == place_in, 1.0, 0.0).astype(jnp.bfloat16)
+
+
+def across(wide_at, plane, chip, core):
+    x_at = lax.rem(chip, SIDE)
+    x_chip = chip + 1 - 2 * x_at
+    y_chip = lax.rem(chip + SIDE, CHIPS)
+    return x_chip * CORES + core, y_chip * CORES + core
+
+
+def owner_tiles(wide_at):
+    tile_count = jnp.int32(0)
+    tile_first = jnp.int32(0)
+    begin = 0
+    for owner, count in zip(OWNERS, BLOCK_TILES):
+        tile_count = tile_count + jnp.where(wide_at == owner, count, 0)
+        tile_first = tile_first + jnp.where(wide_at == owner, begin, 0)
+        begin = begin + count
+    return tile_count, tile_first
+
+
+def spread_steps(own, held, sems, base, at):
+    wide_at, plane, chip, core = at
+    sibling = (chip * CORES + 1 - core, plane)
+    x_wide, y_wide = across(wide_at, plane, chip, core)
+    x_near, y_near = (x_wide, plane), (y_wide, plane)
+    diagonal_wide = (CHIPS - 1 - chip) * CORES + core
+    half = own.shape[0] // 2
+    tops, bottoms = pl.ds(0, half), pl.ds(half, half)
+    above, below = (wide_at, plane + 1), (wide_at, plane - 1)
+
+    def climb(distance, source, src):
+        spot = held.at[source, wide_at]
+        return remote(spot if src is None else src, spot, sems, base + distance - 1, above)
+
+    def sink(distance, source, src):
+        spot = held.at[source, wide_at]
+        return remote(spot if src is None else src, spot, sems, base + 2 + distance, below)
+
+    def plane_copy(source, kind, src=None):
+        index = base + 6 + 9 * source + kind
+        own_spot = held.at[source, wide_at]
+        x_spot, y_spot = held.at[source, x_wide], held.at[source, y_wide]
+        far_spot = held.at[source, diagonal_wide]
+        if kind in (0, 1, 2):
+            target = (x_near, y_near, sibling)[kind]
+            return remote(own_spot if src is None else src, own_spot, sems, index, target)
+        if kind == 3:
+            return remote(x_spot.at[tops], x_spot.at[tops], sems, index, y_near)
+        if kind == 5:
+            return remote(y_spot.at[bottoms], y_spot.at[bottoms], sems, index, x_near)
+        if kind in (4, 6):
+            spot = x_spot if kind == 4 else y_spot
+            return remote(spot, spot, sems, index, sibling)
+        rows = tops if kind == 7 else bottoms
+        return remote(far_spot.at[rows], far_spot.at[rows], sems, index, sibling)
+
+    def plane_send(source, src=None):
+        for kind in (0, 1, 2):
+            plane_copy(source, kind, src).start()
+
+    def begin():
+        @pl.when(plane < PLANES - 1)
+        def _():
+            climb(1, plane, own).start()
+
+        @pl.when(plane > 0)
+        def _():
+            sink(1, plane, own).start()
+
+        plane_send(plane, own)
+
+    def arrive(distance):
+        @pl.when(plane >= distance)
+        def _():
+            source = plane - distance
+            climb(distance, source, None).wait_recv()
+            if distance < PLANES - 1:
+
+                @pl.when(plane < PLANES - 1)
+                def _():
+                    climb(distance + 1, source, None).start()
+
+            plane_send(source)
+
+        @pl.when(plane + distance < PLANES)
+        def _():
+            source = plane + distance
+            sink(distance, source, None).wait_recv()
+            if distance < PLANES - 1:
+
+                @pl.when(plane > 0)
+                def _():
+                    sink(distance + 1, source, None).start()
+
+            plane_send(source)
+
+    def at_distance(distance, step):
+        if distance == 0:
+            step(plane)
+            return
+
+        @pl.when(plane >= distance)
+        def _():
+            step(plane - distance)
+
+        @pl.when(plane + distance < PLANES)
+        def _():
+            step(plane + distance)
+
+    def relay_one(source):
+        plane_copy(source, 0).wait_recv()
+        plane_copy(source, 3).start()
+        plane_copy(source, 4).start()
+        plane_copy(source, 1).wait_recv()
+        plane_copy(source, 5).start()
+        plane_copy(source, 6).start()
+
+    def finish_one(source):
+        plane_copy(source, 3).wait_recv()
+        plane_copy(source, 7).start()
+        plane_copy(source, 5).wait_recv()
+        plane_copy(source, 8).start()
+
+    def settle_one(source):
+        for kind in (2, 4, 6, 7, 8):
+            plane_copy(source, kind).wait_recv()
+        for kind in range(9):
+            plane_copy(source, kind).wait_send()
+
+    def relay(distance):
+        at_distance(distance, relay_one)
+
+    def finish(distance):
+        at_distance(distance, finish_one)
+
+    def settled():
+        for distance in range(PLANES):
+            at_distance(distance, settle_one)
+        for distance in range(1, PLANES):
+            source = plane - distance + 1
+
+            @pl.when((plane < PLANES - 1) & (source >= 0))
+            def _(distance=distance, source=source):
+                climb(distance, source, None).wait_send()
+
+            down_source = plane + distance - 1
+
+            @pl.when((plane > 0) & (down_source < PLANES))
+            def _(distance=distance, down_source=down_source):
+                sink(distance, down_source, None).wait_send()
+
+    return begin, arrive, relay, finish, settled
+
+
+def settle_kernel(
+    z_ref,
+    main_ref,
+    vec_ref,
+    grad_ref,
+    proj_ref,
+    bias_ref,
+    momentum_ref,
+    ids_ref,
+    mask_ref,
+    text_ref,
+    sum_ref,
+    proj_sum_ref,
+    vec_out_ref,
+    gram_ref,
+    high_ref,
+    low_ref,
+    every,
+    table_ref,
+    text_tiles,
+    near,
+    first,
+    x_first,
+    y_first,
+    x_second,
+    y_second,
+    second,
+    deep,
+    proj_own,
+    proj_far,
+    part,
+    proj_part,
+    vec_near,
+    vec_far,
+    vec_deep,
+    main_tiles,
+    proj_tiles,
+    momentum_tiles,
+    packs,
+    pieces,
+    totals,
+    local_sem,
+    tile_sem,
+    text_sem,
+    z_send,
+    z_recv,
+    main_send,
+    main_recv,
+    far_send,
+    far_recv,
+    deep_send,
+    deep_recv,
+    done_send,
+    done_recv,
+    pass_send,
+    pass_recv,
+    proj_send,
+    proj_recv,
+    vec_send,
+    vec_recv,
+    gram_send,
+    gram_recv,
+):
+    wide_at, plane, chip, core = place()
+    sibling, chips, planes = neighbours(wide_at, plane, chip, core)
+    x_wide, y_wide = across(wide_at, plane, chip, core)
+    x_near, y_near = (x_wide, plane), (y_wide, plane)
+    diagonal_wide = (CHIPS - 1 - chip) * CORES + core
+    other = 1 - core
+    x_at = lax.rem(chip, SIDE)
+    y_at = chip // SIDE
+    tile_count, tile_first = owner_tiles(wide_at)
+
+    own_main = pltpu.make_async_copy(main_ref.at[core], first, local_sem.at[0])
+    own_main.start()
+
+    def momentum_load(tile):
+        source = pl.ds(pl.multiple_of((tile_first + tile) * TILE, TILE), TILE)
+        return pltpu.make_async_copy(
+            momentum_ref.at[source], momentum_tiles.at[tile], tile_sem.at[0, tile]
+        )
+
+    @pl.loop(0, tile_count)
+    def _(tile):
+        momentum_load(tile).start()
+
+    enter([sibling] + chips + planes)
+
+    vec_sems = (vec_send, vec_recv)
+    vec_copies = [remote(vec_ref.at[other], vec_near, vec_sems, 0, sibling)]
+    vec_copies[0].start()
+    z_begin, z_arrive, z_relay, z_finish, z_settled = spread_steps(
+        z_ref, every, (z_send, z_recv), 0, place()
+    )
+    own_z = pltpu.make_async_copy(z_ref, every.at[plane, wide_at], local_sem.at[1])
+    own_z.start()
+    main_sems = (main_send, main_recv)
+    near_copies = []
+    for chunk in range(CHUNKS):
+        copy = remote(main_ref.at[other, chunk], near.at[chunk], main_sems, chunk, sibling)
+        copy.start()
+        near_copies.append(copy)
+
+    def vec_far_step():
+        vec_copies[0].wait_recv()
+        vec_far[chip] = vec_ref[core] + vec_near[...]
+        for k, target in enumerate(chips):
+            copy = remote(vec_far.at[chip], vec_far.at[chip], vec_sems, 1 + k, target)
+            copy.start()
+            vec_copies.append(copy)
+
+    def vec_deep_step():
+        for copy in vec_copies[1:4]:
+            copy.wait()
+        vec_deep[plane] = (vec_far[0] + vec_far[1]) + (vec_far[2] + vec_far[3])
+        for k, target in enumerate(planes):
+            copy = remote(vec_deep.at[plane], vec_deep.at[plane], vec_sems, 4 + k, target)
+            copy.start()
+            vec_copies.append(copy)
+
+    def vec_last_step():
+        for copy in vec_copies[4:7]:
+            copy.wait()
+        vec_out_ref[core] = (vec_deep[0] + vec_deep[1]) + (vec_deep[2] + vec_deep[3])
+        copy = remote(vec_out_ref.at[core], vec_out_ref.at[core], vec_sems, 7, sibling)
+        copy.start()
+        vec_copies.append(copy)
+
+    far_sems = (far_send, far_recv)
+    lows, highs = pl.ds(0, 2), pl.ds(2, 2)
+    firsts = []
+
+    def first_step(chunk):
+        near_copies[chunk].wait_recv()
+
+        @pl.loop(0, CHIPS * PLANES)
+        def _(step):
+            y, x, m = step // (SIDE * PLANES), lax.rem(step // PLANES, SIDE), lax.rem(step, PLANES)
+            first[chunk, y, x, m] = (
+                first[chunk, y, x, m].astype(jnp.float32)
+                + near[chunk, y, x, m].astype(jnp.float32)
+            ).astype(jnp.bfloat16)
+
+        by_x = remote(
+            first.at[chunk, :, 1 - x_at, lows], x_first.at[chunk], far_sems, chunk * 4, x_near
+        )
+        by_y = remote(
+            first.at[chunk, 1 - y_at, :, highs], y_first.at[chunk], far_sems, chunk * 4 + 1, y_near
+        )
+        by_x.start()
+        by_y.start()
+        firsts.append((by_x, by_y))
+
+    seconds = []
+
+    def second_step(chunk):
+        by_x, by_y = firsts[chunk]
+        by_x.wait_recv()
+        for y in range(SIDE):
+            for m in range(2):
+                first[chunk, y, x_at, m] = (
+                    first[chunk, y, x_at, m].astype(jnp.float32)
+                    + x_first[chunk, y, m].astype(jnp.float32)
+                ).astype(jnp.bfloat16)
+        next_y = remote(
+            first.at[chunk, 1 - y_at, x_at, lows],
+            y_second.at[chunk],
+            far_sems,
+            chunk * 4 + 2,
+            y_near,
+        )
+        next_y.start()
+        by_y.wait_recv()
+        for x in range(SIDE):
+            for m in range(2):
+                first[chunk, y_at, x, 2 + m] = (
+                    first[chunk, y_at, x, 2 + m].astype(jnp.float32)
+                    + y_first[chunk, x, m].astype(jnp.float32)
+                ).astype(jnp.bfloat16)
+        next_x = remote(
+            first.at[chunk, y_at, 1 - x_at, highs],
+            x_second.at[chunk],
+            far_sems,
+            chunk * 4 + 3,
+            x_near,
+        )
+        next_x.start()
+        seconds.append((next_y, next_x))
+
+    deep_sems = (deep_send, deep_recv)
+    deep_copies = []
+
+    def deep_step(chunk):
+        next_y, next_x = seconds[chunk]
+        next_y.wait_recv()
+        for m in range(2):
+            second[chunk, m] = (
+                first[chunk, y_at, x_at, m].astype(jnp.float32)
+                + y_second[chunk, m].astype(jnp.float32)
+            ).astype(jnp.bfloat16)
+        next_x.wait_recv()
+        for m in range(2):
+            second[chunk, 2 + m] = (
+                first[chunk, y_at, x_at, 2 + m].astype(jnp.float32)
+                + x_second[chunk, m].astype(jnp.float32)
+            ).astype(jnp.bfloat16)
+        copies = []
+        for k, target in enumerate(planes):
+            to_plane = lax.rem(plane + k + 1, PLANES)
+            copy = remote(
+                second.at[chunk, to_plane], deep.at[chunk, k], deep_sems, chunk * 3 + k, target
+            )
+            copy.start()
+            copies.append(copy)
+        deep_copies.append(copies)
+
+    count = every.shape[2]
+    features = proj_ref.shape[0]
+    wide_count = CHIPS * CORES
+    per_band = grad_ref.shape[0] // BANDS
+    proj_sems = (proj_send, proj_recv)
+    proj_copies = []
+
+    def proj_near_step():
+        total = jnp.zeros((features, D), jnp.float32)
+        for block in range(PLANES * wide_count):
+            rows = every[block % PLANES, block // PLANES]
+            total = total + dot_tn(grad_ref[block], rows)
+        proj_own[...] = total.astype(jnp.bfloat16).reshape(CHIPS, PROJ, D)
+        for k, target in enumerate(chips):
+            to_chip = lax.rem(chip + k + 1, CHIPS)
+            copy = remote(proj_own.at[to_chip], proj_far.at[chip], proj_sems, k, target)
+            copy.start()
+            proj_copies.append(copy)
+        proj_far[chip] = proj_own[chip]
+
+    def proj_far_step():
+        for copy in proj_copies:
+            copy.wait()
+        for k, target in enumerate(planes):
+            to_plane = lax.rem(plane + k + 1, PLANES)
+            copy = remote(proj_far.at[to_plane], proj_part.at[plane], proj_sems, 3 + k, target)
+            copy.start()
+            proj_copies.append(copy)
+        proj_part[plane] = proj_far[plane]
+
+    def publish_proj():
+        for copy in proj_copies[3:]:
+            copy.wait()
+        publish(len(PIECES), proj_part, proj_natural(chip, core))
+
+    done_sems = (done_send, done_recv)
+    pass_sems = (pass_send, pass_recv)
+    done_copies = []
+    locals_done = []
+
+    def natural(index, wide):
+        _, size, base = PIECES[index]
+        return sum_ref.at[pl.ds(pl.multiple_of(base + wide * size, 16), size)]
+
+    def proj_natural(at_chip, at_core):
+        return proj_sum_ref.at[at_core, :, at_chip]
+
+    def publish(index, src, spot):
+        copies = []
+        for k, target in enumerate([sibling] + chips):
+            copy = remote(src, spot, done_sems, index * 4 + k, target)
+            copy.start()
+            copies.append(copy)
+        done_copies.append(copies)
+        copy = pltpu.make_async_copy(src, spot, local_sem.at[2 + index])
+        copy.start()
+        locals_done.append(copy)
+
+    def publish_step(chunk):
+        for copy in deep_copies[chunk]:
+            copy.wait_recv()
+        value = second[chunk, plane].astype(jnp.float32)
+        for k in range(3):
+            value = value + deep[chunk, k].astype(jnp.float32)
+        part[chunk * CHUNK : (chunk + 1) * CHUNK, :] = value.astype(jnp.bfloat16)
+        for index, (offset, size, _) in enumerate(PIECES):
+            if offset // CHUNK == chunk:
+                publish(index, part.at[pl.ds(offset, size)], natural(index, wide_at))
+
+    pass_copies = []
+
+    def pass_step(index):
+        for k in range(3):
+            done_copies[index][1 + k].wait_recv()
+            from_chip = lax.rem(chip + CHIPS - 1 - k, CHIPS)
+            if index < len(PIECES):
+                spot = natural(index, from_chip * CORES + core)
+            else:
+                spot = proj_natural(from_chip, core)
+            copy = remote(spot, spot, pass_sems, index * 3 + k, sibling)
+            copy.start()
+            pass_copies.append(copy)
+
+    def table_step():
+        for block in range(PLANES * wide_count):
+            rows = every[block % PLANES, block // PLANES]
+            band, spot = divmod(block, per_band)
+            table_ref[band * features : (band + 1) * features, spot * count : (spot + 1) * count] = (
+                dot_nt(proj_ref[...], rows) + bias_ref[...]
+            ).astype(jnp.bfloat16)
+
+    text_rows = table_ref.shape[1]
+    row_tiles = ids_ref.shape[1] // TEXT_TILE
+    text_count = ids_ref.shape[0] * row_tiles
+
+    def text_copy(step):
+        slot = lax.rem(step, 2)
+        lanes = pl.ds(pl.multiple_of(step * TEXT_TILE, TEXT_TILE), TEXT_TILE)
+        return pltpu.make_async_copy(text_tiles.at[slot], text_ref.at[:, lanes], text_sem.at[slot])
+
+    def text_steps(begin, end):
+        @pl.loop(begin, end)
+        def _(step):
+            row = pl.ds(step // row_tiles, 1)
+            start = lax.rem(step, row_tiles) * TEXT_TILE
+            id_lanes = pl.ds(pl.multiple_of(start, TEXT_TILE), TEXT_TILE)
+            ids = ids_ref[row, id_lanes]
+            values = plain_dot(table_ref[...], band_onehot(ids, text_rows))
+            band = jnp.where(mask_ref[row, id_lanes] > 0, ids // text_rows, -1)
+            total = jnp.zeros((features, TEXT_TILE), jnp.float32)
+            for b in range(BANDS):
+                total = jnp.where(band == b, values[b * features : (b + 1) * features], total)
+
+            @pl.when(step >= 2)
+            def _():
+                text_copy(step - 2).wait()
+
+            text_tiles[lax.rem(step, 2)] = total
+            text_copy(step).start()
+
+    own_main.wait()
+    z_begin()
+    first_step(0)
+    vec_far_step()
+    first_step(1)
+    z_arrive(1)
+    first_step(2)
+    z_relay(0)
+    z_arrive(2)
+    second_step(0)
+    z_relay(1)
+    z_arrive(3)
+    second_step(1)
+    z_finish(0)
+    z_relay(2)
+    second_step(2)
+    deep_step(0)
+    z_finish(1)
+    z_relay(3)
+    deep_step(1)
+    z_finish(2)
+    z_finish(3)
+    deep_step(2)
+    own_z.wait()
+    z_settled()
+    proj_near_step()
+    vec_deep_step()
+    publish_step(0)
+    publish_step(1)
+    proj_far_step()
+    publish_step(2)
+    table_step()
+    vec_last_step()
+    publish_proj()
+    for index in range(len(PIECES) + 1):
+        pass_step(index)
+    for copies in done_copies:
+        copies[0].wait_recv()
+    for copy in pass_copies:
+        copy.wait_recv()
+    for copy in locals_done:
+        copy.wait()
+
+    gram_sems = (gram_send, gram_recv)
+
+    def add_tile(tile, gradient):
+        momentum_load(tile).wait()
+        gradient = gradient.astype(jnp.float32)
+        update = gradient + MUON_BETA * (MUON_BETA * momentum_tiles[tile] + gradient)
+        high, low = halves(update)
+        rows = pl.ds(pl.multiple_of(tile * TILE, TILE), TILE)
+        high_ref[rows, :] = high
+        low_ref[rows, :] = low
+
+    @pl.when(wide_at == OWNERS[4])
+    def _():
+        loads = [
+            pltpu.make_async_copy(
+                proj_sum_ref.at[tile // PLANES, tile % PLANES],
+                proj_tiles.at[tile],
+                tile_sem.at[1, tile],
+            )
+            for tile in range(MOST_TILES)
+        ]
+        for copy in loads:
+            copy.start()
+        for copy in loads:
+            copy.wait()
+
+        @pl.loop(0, MOST_TILES)
+        def _(tile):
+            add_tile(tile, proj_tiles[tile].reshape(TILE, D))
+
+    @pl.when((tile_count > 0) & (wide_at != OWNERS[4]))
+    def _():
+        def load(tile):
+            source = pl.ds(pl.multiple_of((tile_first + tile) * TILE, TILE), TILE)
+            return pltpu.make_async_copy(
+                sum_ref.at[source], main_tiles.at[tile], tile_sem.at[1, tile]
+            )
+
+        @pl.loop(0, tile_count)
+        def _(tile):
+            load(tile).start()
+
+        @pl.loop(0, tile_count)
+        def _(tile):
+            load(tile).wait()
+            add_tile(tile, main_tiles[tile])
+
+    for count_here in sorted(set(BLOCK_TILES)):
+
+        @pl.when(tile_count == count_here)
+        def _(count_here=count_here):
+            high = high_ref[0 : count_here * TILE, :]
+            cross = dot_tn(high, low_ref[0 : count_here * TILE, :])
+            gram_ref[...] = dot_tn(high, high) + (cross + cross.T)
+
+    def gram_copies(first_index):
+        copies = []
+        for k, target in enumerate(planes):
+            to_plane = lax.rem(plane + k + 1, PLANES)
+            if first_index == 0:
+                src, dst = packs.at[to_plane], pieces.at[plane]
+            else:
+                src, dst = totals.at[plane], totals.at[plane]
+            copies.append(remote(src, dst, gram_sems, first_index + k, target))
+        return copies
+
+    owning = tile_count > 0
+
+    @pl.when(owning)
+    def _():
+        for t in range(PLANES):
+            for strip, lane in ((t, 0), (STRIPS - 1 - t, 1)):
+                begin = strip // 2 * TILE
+                value = gram_ref[strip * STRIP : (strip + 1) * STRIP, begin:]
+                width = D - begin
+                at = 0 if lane == 0 else PACKED - width
+                packs[t, :, at : at + width] = value
+        for copy in gram_copies(0):
+            copy.start()
+        pieces[plane] = packs[plane]
+
+    text_steps(0, text_count // 2)
+
+    @pl.when(owning)
+    def _():
+        for copy in gram_copies(0):
+            copy.wait()
+        totals[plane] = (pieces[0] + pieces[1]) + (pieces[2] + pieces[3])
+        for copy in gram_copies(3):
+            copy.start()
+
+    text_steps(text_count // 2, text_count)
+
+    @pl.when(owning)
+    def _():
+        for copy in gram_copies(3):
+            copy.wait()
+        for t in range(PLANES):
+            for strip, lane in ((t, 0), (STRIPS - 1 - t, 1)):
+                begin = strip // 2 * TILE
+                width = D - begin
+                at = 0 if lane == 0 else PACKED - width
+                gram_ref[strip * STRIP : (strip + 1) * STRIP, begin:] = totals[
+                    t, :, at : at + width
+                ]
+        row_block = lax.broadcasted_iota(jnp.int32, (D, D), 0) // TILE
+        lane_block = lax.broadcasted_iota(jnp.int32, (D, D), 1) // TILE
+        value = gram_ref[...]
+        gram_ref[...] = jnp.where(lane_block >= row_block, value, value.T)
+
+    for copies in done_copies:
+        for copy in copies:
+            copy.wait_send()
+    for copy in pass_copies:
+        copy.wait_send()
+    for copy in near_copies:
+        copy.wait_send()
+    for pair in firsts + seconds:
+        for copy in pair:
+            copy.wait_send()
+    for copies in deep_copies:
+        for copy in copies:
+            copy.wait_send()
+    vec_copies[0].wait_send()
+    vec_copies[7].wait()
+    text_copy(text_count - 2).wait()
+    text_copy(text_count - 1).wait()
+
+
+def settle(z_own, main, vec, grad_own, proj_own, bias_own, momentum, text_ids, text_mask):
+    dma = pltpu.SemaphoreType.DMA
+    f32, bf = jnp.float32, jnp.bfloat16
+    features, tokens = proj_own.shape[0], text_ids.size
+    rows = grad_own.shape[0] * grad_own.shape[1] // BANDS
+    hbm = pl.BlockSpec(memory_space=pl.ANY)
+    vmem = pl.BlockSpec(memory_space=pltpu.VMEM)
+    grid = (CHUNKS, SIDE, SIDE, PLANES, CHUNK, D)
+    return pl.pallas_call(
+        settle_kernel,
+        out_shape=(
+            jax.ShapeDtypeStruct((features, tokens), f32),
+            jax.ShapeDtypeStruct((MAIN_TILES * TILE, D), bf),
+            jax.ShapeDtypeStruct((CORES, PLANES, CHIPS, PROJ, D), bf),
+            jax.ShapeDtypeStruct((CORES, VROWS, D), f32),
+            jax.ShapeDtypeStruct((D, D), f32),
+            jax.ShapeDtypeStruct((MOST_TILES * TILE, D), bf),
+            jax.ShapeDtypeStruct((MOST_TILES * TILE, D), bf),
+        ),
+        in_specs=[vmem, hbm, vmem, vmem, vmem, vmem, hbm, vmem, vmem],
+        out_specs=(hbm, hbm, hbm, vmem, vmem, vmem, vmem),
+        scratch_shapes=[
+            pltpu.VMEM((PLANES, CHIPS * CORES) + z_own.shape, bf),
+            pltpu.VMEM((BANDS * features, rows), bf),
+            pltpu.VMEM((2, features, TEXT_TILE), f32),
+            pltpu.VMEM(grid, bf),
+            pltpu.VMEM(grid, bf),
+            pltpu.VMEM((CHUNKS, SIDE, 2, CHUNK, D), bf),
+            pltpu.VMEM((CHUNKS, SIDE, 2, CHUNK, D), bf),
+            pltpu.VMEM((CHUNKS, 2, CHUNK, D), bf),
+            pltpu.VMEM((CHUNKS, 2, CHUNK, D), bf),
+            pltpu.VMEM((CHUNKS, PLANES, CHUNK, D), bf),
+            pltpu.VMEM((CHUNKS, 3, CHUNK, D), bf),
+            pltpu.VMEM((CHIPS, PROJ, D), bf),
+            pltpu.VMEM((CHIPS, PROJ, D), bf),
+            pltpu.VMEM((MAIN, D), bf),
+            pltpu.VMEM((PLANES, PROJ, D), bf),
+            pltpu.VMEM((VROWS, D), f32),
+            pltpu.VMEM((CHIPS, VROWS, D), f32),
+            pltpu.VMEM((PLANES, VROWS, D), f32),
+            pltpu.VMEM((4, TILE, D), bf),
+            pltpu.VMEM((MOST_TILES, CHIPS, PROJ, D), bf),
+            pltpu.VMEM((MOST_TILES, TILE, D), f32),
+            pltpu.VMEM((PLANES, STRIP, PACKED), f32),
+            pltpu.VMEM((PLANES, STRIP, PACKED), f32),
+            pltpu.VMEM((PLANES, STRIP, PACKED), f32),
+            dma((8,)),
+            dma((2, MOST_TILES)),
+            dma((2,)),
+            dma((6 + 9 * PLANES,)),
+            dma((6 + 9 * PLANES,)),
+            dma((CHUNKS,)),
+            dma((CHUNKS,)),
+            dma((CHUNKS * 4,)),
+            dma((CHUNKS * 4,)),
+            dma((CHUNKS * 3,)),
+            dma((CHUNKS * 3,)),
+            dma((20,)),
+            dma((20,)),
+            dma((15,)),
+            dma((15,)),
+            dma((6,)),
+            dma((6,)),
+            dma((8,)),
+            dma((8,)),
+            dma((6,)),
+            dma((6,)),
+        ],
+        compiler_params=pltpu.CompilerParams(
+            collective_id=3, has_side_effects=True, vmem_limit_bytes=58 * 2**20
+        ),
+        name="settle",
+    )(
+        z_own,
+        main.reshape((CORES,) + grid),
+        vec,
+        grad_own,
+        proj_own,
+        bias_own,
+        momentum,
+        text_ids,
+        text_mask,
+    )
+
+
+SHARES = ((6, 0, 0, 384), (7, 0, 384, 128), (2, 0, 512, 512), (4, 0, 1024, 512)) + (
+    (0, 0, 1536, 512),
+    (0, 512, 2048, 512),
+)
+
+
+def muon_kernel(
+    gram_ref,
+    high_ref,
+    low_ref,
+    out_ref,
+    gram,
+    poly,
+    chain,
+    chain_high,
+    chain_low,
+    rows_out,
+    local_sem,
+    rows_send,
+    rows_recv,
+):
+    wide_at, plane, chip, core = place()
+    sibling, chips, planes = neighbours(wide_at, plane, chip, core)
+    x_wide, y_wide = across(wide_at, plane, chip, core)
+    x_near, y_near = (x_wide, plane), (y_wide, plane)
+    tile_count, _ = owner_tiles(wide_at)
+    enter([sibling, x_near, y_near])
+
+    @pl.when(tile_count > 0)
+    def _():
+        diagonal = lax.broadcasted_iota(jnp.int32, (D, D), 0) == lax.broadcasted_iota(
+            jnp.int32, (D, D), 1
+        )
+        square = jnp.sum(jnp.where(diagonal, gram_ref[...], 0.0))
+        inverse = 1.0 / (jnp.sqrt(jnp.full((1, 1), square)) + 1e-07)
+        gram[...] = gram_ref[...] * (inverse * inverse)
+
+        def make_poly():
+            value = gram[...]
+            parts = halves(value)
+            diagonal = lax.broadcasted_iota(jnp.int32, (D, D), 0) == lax.broadcasted_iota(
+                jnp.int32, (D, D), 1
+            )
+            poly[...] = (
+                NEWTON_B * value
+                + NEWTON_C * split_dot(parts, parts)
+                + jnp.where(diagonal, NEWTON_A, 0.0)
+            )
+
+        def next_gram():
+            parts = halves(poly[...])
+            half_way = split_dot(halves(gram[...]), parts)
+            gram[...] = split_dot(halves(half_way), parts)
+
+        def extend():
+            chain[...] = split_dot(halves(chain[...]), halves(poly[...]))
+
+        make_poly()
+        chain[...] = poly[...]
+        next_gram()
+
+        @pl.loop(0, 3)
+        def _(sweep):
+            make_poly()
+            extend()
+            next_gram()
+
+        make_poly()
+        extend()
+        high, low = halves(chain[...] * inverse)
+        chain_high[...] = high
+        chain_low[...] = low
+
+    sems = (rows_send, rows_recv)
+
+    def share_copies(index):
+        owner, source, begin, size = SHARES[index]
+        owner_chip, owner_core = divmod(owner, CORES)
+        mine = rows_out.at[pl.ds(source, size)]
+        spot = out_ref.at[pl.ds(begin, size)]
+        first = out_ref.at[pl.ds(begin, size // 2)]
+        last = out_ref.at[pl.ds(begin + size // 2, size // 2)]
+        base = index * 9
+        roles = {
+            "x": (owner_chip ^ 1) * CORES + owner_core,
+            "y": (owner_chip ^ 2) * CORES + owner_core,
+            "d": (owner_chip ^ 3) * CORES + owner_core,
+        }
+        sends = {
+            "o": [
+                (mine, spot, base, x_near),
+                (mine, spot, base + 1, y_near),
+                (mine, spot, base + 2, sibling),
+            ],
+            "x": [(first, first, base + 3, y_near), (spot, spot, base + 5, sibling)],
+            "y": [(last, last, base + 4, x_near), (spot, spot, base + 6, sibling)],
+            "d": [(first, first, base + 7, sibling), (last, last, base + 8, sibling)],
+        }
+        gets = {
+            "x": [(spot, base)],
+            "y": [(spot, base + 1)],
+            "d": [(first, base + 3), (last, base + 4)],
+            "so": [(spot, base + 2)],
+            "sx": [(spot, base + 5)],
+            "sy": [(spot, base + 6)],
+            "sd": [(first, base + 7), (last, base + 8)],
+        }
+        roles["o"] = owner
+        for role in ("o", "x", "y", "d"):
+            at = roles[role]
+            roles["s" + role] = at // CORES * CORES + 1 - at % CORES
+        local = (mine, spot, local_sem.at[index])
+        return roles, sends, gets, local
+
+    def started(entry):
+        src, dst, index, target = entry
+        return remote(src, dst, sems, index, target)
+
+    def arriving(entry):
+        spot, index = entry
+        return remote(spot, spot, sems, index, sibling)
+
+    plans = [share_copies(index) for index in range(len(SHARES))]
+    for (roles, sends, gets, local), (_, source, _, size) in zip(plans, SHARES):
+
+        @pl.when(wide_at == roles["o"])
+        def _(sends=sends, local=local, source=source, size=size):
+            rows = slice(source, source + size)
+            rows_out[rows, :] = split_dot(
+                (high_ref[rows, :], low_ref[rows, :]), (chain_high[...], chain_low[...])
+            ).astype(jnp.bfloat16)
+            for entry in sends["o"]:
+                started(entry).start()
+            pltpu.make_async_copy(*local).start()
+
+    for phase in (("x", "y"), ("d",)):
+        for roles, sends, gets, local in plans:
+            for role in phase:
+
+                @pl.when(wide_at == roles[role])
+                def _(sends=sends, gets=gets, role=role):
+                    for got, entry in zip(gets[role] * 2, sends[role]):
+                        if role == "d" or entry is sends[role][0]:
+                            arriving(got).wait_recv()
+                        started(entry).start()
+
+    for roles, sends, gets, local in plans:
+        for role in ("so", "sx", "sy", "sd"):
+
+            @pl.when(wide_at == roles[role])
+            def _(gets=gets, role=role):
+                for got in gets[role]:
+                    arriving(got).wait_recv()
+
+        for role in ("o", "x", "y", "d"):
+
+            @pl.when(wide_at == roles[role])
+            def _(sends=sends, local=local, role=role):
+                for entry in sends[role]:
+                    started(entry).wait_send()
+                if role == "o":
+                    pltpu.make_async_copy(*local).wait()
+
+
+def muon_rows(gram, high, low):
+    dma = pltpu.SemaphoreType.DMA
+    vmem = pl.BlockSpec(memory_space=pltpu.VMEM)
+    total = (MAIN_TILES + MOST_TILES) * TILE
+    return pl.pallas_call(
+        muon_kernel,
+        out_shape=jax.ShapeDtypeStruct((total, D), jnp.bfloat16),
+        in_specs=[vmem] * 3,
+        out_specs=pl.BlockSpec(memory_space=pl.ANY),
+        scratch_shapes=[
+            pltpu.VMEM((D, D), jnp.float32),
+            pltpu.VMEM((D, D), jnp.float32),
+            pltpu.VMEM((D, D), jnp.float32),
+            pltpu.VMEM((D, D), jnp.bfloat16),
+            pltpu.VMEM((D, D), jnp.bfloat16),
+            pltpu.VMEM((MOST_TILES * TILE, D), jnp.bfloat16),
+            dma((len(SHARES),)),
+            dma((len(SHARES) * 9,)),
+            dma((len(SHARES) * 9,)),
+        ],
+        compiler_params=pltpu.CompilerParams(
+            collective_id=4, has_side_effects=True, vmem_limit_bytes=40 * 2**20
+        ),
+        name="muon_rows",
+    )(gram, high, low)
+
+
+def finish_kernel(main_ref, proj_ref, rows_ref, momentum_ref, master_ref, ema_ref, *outs):
+    grad_ref, momentum_new_ref, weight_ref, ema_new_ref = outs
+    tile = pl.program_id(0)
+    height = rows_ref.shape[0]
+    main = main_ref[...].astype(jnp.float32)
+    proj = proj_ref[...].reshape(height, D).astype(jnp.float32)
+    gradient = jnp.where(tile < MAIN_TILES * TILE // height, main, proj)
+    grad_ref[0] = gradient
+    momentum_new_ref[0] = MUON_BETA * momentum_ref[0] + gradient
+    row = lax.broadcasted_iota(jnp.int32, (height, 1), 0) + tile * height
+    scale = jnp.zeros((height, 1), jnp.float32)
+    begin = 0
+    for row_total, count in zip(matrix_rows(), BLOCK_TILES):
+        inside = (row >= begin * TILE) & (row < (begin + count) * TILE)
+        scale = jnp.where(inside, MUON_RATE * math.sqrt(row_total / D), scale)
+        begin = begin + count
+    weight = master_ref[0] * (1.0 - MUON_RATE * MUON_DECAY) - scale * rows_ref[...].astype(
+        jnp.float32
+    )
+    weight_ref[0] = weight
+    ema_new_ref[0] = EMA_DECAY * ema_ref[0] + (1.0 - EMA_DECAY) * weight
+
+
+def finish(main_sum, proj_sum, rows, momentum, master, ema):
+    height = 2 * TILE
+    tall = height // TILE
+    main_steps = MAIN_TILES // tall
+    block = pl.BlockSpec((1, height, D), lambda i: (0, i, 0))
+    proj = proj_sum.reshape((MOST_TILES,) + proj_sum.shape[2:])
+    return pl.pallas_call(
+        finish_kernel,
+        grid=((MAIN_TILES + MOST_TILES) // tall,),
+        out_shape=(jax.ShapeDtypeStruct(master.shape, jnp.float32),) * 4,
+        in_specs=[
+            pl.BlockSpec((height, D), lambda i: (jnp.minimum(i, main_steps - 1), 0)),
+            pl.BlockSpec(
+                (tall,) + proj.shape[1:], lambda i: (jnp.maximum(i - main_steps, 0), 0, 0, 0)
+            ),
+            pl.BlockSpec((height, D), lambda i: (i, 0)),
+            block,
+            block,
+            block,
+        ],
+        out_specs=(block,) * 4,
+        cost_estimate=pl.CostEstimate(
+            flops=12 * master.size, bytes_accessed=32 * master.size, transcendentals=0
+        ),
+        compiler_params=pltpu.CompilerParams(vmem_limit_bytes=32 * 2**20),
+        name="finish",
+    )(main_sum, proj, rows, momentum, master, ema)
+
+def two_part_dot(left, right):
+    high, low = halves(left)
+    return plain_dot(high, right) + plain_dot(low, right)
+
+
+def normalize(values):
+    center = values - jnp.mean(values, axis=-1, keepdims=True)
+    spread = jnp.mean(center * center, axis=-1, keepdims=True)
+    scale = lax.rsqrt(spread + 1e-05)
+    return center * scale, scale
+
+
+def normalize_back(grad, gain, hat, scale):
+    grad_hat = grad * gain
+    return scale * (
+        grad_hat
+        - jnp.mean(grad_hat, axis=-1, keepdims=True)
+        - hat * jnp.mean(grad_hat * hat, axis=-1, keepdims=True)
+    )
+
+
+def over_rows(values):
+    return jnp.sum(values, axis=0, keepdims=True)
+
+
+def layer_kernel(
+    master_ref,
+    pieces_ref,
+    table_ref,
+    ids_ref,
+    mask_ref,
+    cot_ref,
+    live_ref,
+    param_ref,
+    z_ref,
+    main_ref,
+    outgoing_ref,
+    vec_ref,
+    own_grad_ref,
+    own_proj_ref,
+    rows_ref,
+    own_rows,
+    every_ids,
+    spots_ref,
+    asked_ranks,
+    asked_locals,
+    incoming_ref,
+    grad_ref,
+    packed,
+    text_total,
+    onehot,
+    hats,
+    scales,
+    normed,
+    keys,
+    probs,
+    grad_kv,
+    grad_normed,
+    grad_pieces,
+    active,
+    slope,
+    slides,
+    sums,
+    local_sem,
+    tell_send,
+    tell_recv,
+    piece_send,
+    piece_recv,
+    table_send,
+    table_recv,
+    body_send,
+    body_recv,
+    proj_send,
+    proj_recv,
+):
+    at = place()
+    wide_at, plane, chip, core = at
+    me = wide_at * PLANES + plane
+    wide_count = CHIPS * CORES
+    group_rows = table_ref.shape[0]
+    cap = outgoing_ref.shape[0] // (wide_count * PLANES)
+    entries = z_ref.shape[0]
+    peers = [
+        (lax.rem(wide_at + k // PLANES, wide_count), lax.rem(plane + k % PLANES, PLANES))
+        for k in range(1, wide_count * PLANES)
+    ]
+
+    def spread_of(own, held, sems):
+        return spread_steps(own, held, sems, 0, at)
+
+    body_held = packed.at[:, :, pl.ds(0, MAIN)]
+    proj_held = packed.at[:, :, pl.ds(MAIN, PART - MAIN)]
+    body_spread = spread_of(body_held.at[plane, wide_at], body_held, (body_send, body_recv))
+    proj_spread = spread_of(proj_held.at[plane, wide_at], proj_held, (proj_send, proj_recv))
+    body_begin, body_arrive, body_relay, body_finish, body_settled = body_spread
+    proj_begin, proj_arrive, proj_relay, proj_finish, proj_settled = proj_spread
+
+    loads = []
+    begin = 0
+    block = 0
+    for index, row_total in enumerate(matrix_rows()):
+        height = row_total // PLANES
+        size = height // wide_count
+        copy = pltpu.make_async_copy(
+            master_ref.at[pl.ds(pl.multiple_of(block + wide_at * size, 16), size)],
+            own_rows.at[pl.ds(begin, size)],
+            local_sem.at[index],
+        )
+        copy.start()
+        loads.append(copy)
+        begin = begin + size
+        block = block + height
+    enter(peers)
+    tell_copies = []
+    for index, target in enumerate(peers):
+        copy = remote(pieces_ref, every_ids.at[me], (tell_send, tell_recv), index, target)
+        copy.start()
+        tell_copies.append(copy)
+    every_ids[me] = pieces_ref[...]
+    for copy in loads:
+        copy.wait()
+    packed[plane, wide_at] = own_rows[...].astype(jnp.bfloat16)
+    piece_copies = []
+    table_copies = []
+
+    def piece_rows(device):
+        return pl.ds(pl.multiple_of(device * cap, cap), cap)
+
+    def send_pieces(begin, end):
+        for index in range(begin, end):
+            wide_to, plane_to = peers[index]
+            copy = remote(
+                outgoing_ref.at[piece_rows(wide_to * PLANES + plane_to)],
+                incoming_ref.at[piece_rows(me)],
+                (piece_send, piece_recv),
+                index,
+                (wide_to, plane_to),
+            )
+            copy.start()
+            piece_copies.append(copy)
+
+    def send_table(begin, end):
+        for index in range(begin, end):
+            wide_to, plane_to = peers[index]
+            copy = remote(
+                own_grad_ref.at[wide_to * PLANES + plane_to],
+                grad_ref.at[me],
+                (table_send, table_recv),
+                index,
+                (wide_to, plane_to),
+            )
+            copy.start()
+            table_copies.append(copy)
+
+    text_rows = own_grad_ref.shape[0] * own_grad_ref.shape[1] // BANDS
+    features = cot_ref.shape[0]
+    text_total[...] = jnp.zeros_like(text_total)
+
+    row_tiles = ids_ref.shape[1] // TEXT_TILE
+
+    def build_pieces():
+        for copy in tell_copies:
+            copy.wait()
+        device_count = wide_count * PLANES
+        slot_count = entries * PSLOTS
+        asked_ids = jnp.concatenate([every_ids[:, slot, :] for slot in range(PSLOTS)], axis=1)
+        own_ids = jnp.concatenate([pieces_ref[slot : slot + 1, :] for slot in range(PSLOTS)], axis=1)
+        asked = asked_ids // group_rows == me
+        own_group = own_ids // group_rows
+        group_at = lax.broadcasted_iota(jnp.int32, (device_count, slot_count), 0)
+        grouped = jnp.where(group_at == own_group, 1.0, 0.0)
+        marks = jnp.concatenate([jnp.where(asked, 1.0, 0.0), grouped], axis=0).astype(jnp.bfloat16)
+        earlier = jnp.where(
+            lax.broadcasted_iota(jnp.int32, (slot_count, slot_count), 0)
+            < lax.broadcasted_iota(jnp.int32, (slot_count, slot_count), 1),
+            1.0,
+            0.0,
+        ).astype(jnp.bfloat16)
+        ranks = plain_dot(marks, earlier)
+        own_rank = over_rows(grouped * ranks[device_count:, :])
+        spots = own_group * cap + own_rank.astype(jnp.int32)
+        for slot in range(PSLOTS):
+            spots_ref[slot + 1 : slot + 2, :] = spots[:, slot * entries : (slot + 1) * entries]
+        asked_ranks[...] = jnp.where(asked, ranks[:device_count, :], -1.0)
+        asked_locals[...] = (asked_ids - me * group_rows + 1).astype(jnp.float32)
+
+        @pl.loop(0, device_count)
+        def _(device):
+            here = pl.ds(device, 1)
+            rank_at = lax.broadcasted_iota(jnp.int32, (cap, slot_count), 0).astype(jnp.float32)
+            rows = jnp.sum(
+                jnp.where(rank_at == asked_ranks[here, :], asked_locals[here, :], 0.0),
+                axis=1,
+                keepdims=True,
+            )
+            rows_ref[piece_rows(device), :] = rows.astype(jnp.int32) - 1
+
+        tile = 512
+        for begin in range(0, device_count * cap, tile):
+            row_at = lax.broadcasted_iota(jnp.int32, (tile, group_rows), 1)
+            chosen = jnp.where(row_at == rows_ref[begin : begin + tile, :], 1.0, 0.0)
+            outgoing_ref[begin : begin + tile, :] = plain_dot(
+                chosen.astype(jnp.bfloat16), table_ref[...]
+            ).astype(jnp.bfloat16)
+        incoming_ref[piece_rows(me), :] = outgoing_ref[piece_rows(me), :]
+
+    def text_steps(begin, end):
+        @pl.loop(begin, end)
+        def _(step):
+            lanes = pl.ds(pl.multiple_of(step * TEXT_TILE, TEXT_TILE), TEXT_TILE)
+            row = pl.ds(step // row_tiles, 1)
+            start = lax.rem(step, row_tiles) * TEXT_TILE
+            id_lanes = pl.ds(pl.multiple_of(start, TEXT_TILE), TEXT_TILE)
+            ids = ids_ref[row, id_lanes]
+            chosen = band_onehot(ids, text_rows)
+            band = jnp.where(mask_ref[row, id_lanes] > 0, ids // text_rows, -1)
+            cot = cot_ref[:, lanes].astype(jnp.float32)
+            banded = jnp.concatenate(
+                [jnp.where(band == b, cot, 0.0).astype(jnp.bfloat16) for b in range(BANDS)], axis=0
+            )
+            text_total[...] += dot_nt(chosen, banded)
+
+    text_tiles = ids_ref.shape[0] * row_tiles
+    body_begin()
+    proj_begin()
+    text_steps(0, 1)
+    body_arrive(1)
+    build_pieces()
+    send_pieces(0, 6)
+    text_steps(1, 3)
+    body_relay(0)
+    body_arrive(2)
+    send_pieces(6, 12)
+    text_steps(3, 5)
+    body_arrive(3)
+    body_relay(1)
+    body_finish(0)
+    send_pieces(12, 18)
+    text_steps(5, 8)
+    body_relay(2)
+    body_finish(1)
+    send_pieces(18, 24)
+    text_steps(8, 11)
+    body_relay(3)
+    body_finish(2)
+    send_pieces(24, 31)
+    text_steps(11, 16)
+    bias_total = jnp.zeros((1, features), jnp.float32)
+    blocks = own_grad_ref.shape[0] // BANDS
+    for b in range(BANDS):
+        rounded = text_total[:, b * features : (b + 1) * features].astype(jnp.bfloat16)
+        own_grad_ref[b * blocks : (b + 1) * blocks] = rounded.reshape(
+            (blocks,) + own_grad_ref.shape[1:]
+        )
+        bias_total = bias_total + over_rows(rounded.astype(jnp.float32))
+    grad_ref[me] = own_grad_ref[me]
+    body_finish(3)
+    proj_arrive(1)
+    send_table(0, 8)
+    proj_relay(0)
+    proj_arrive(2)
+    send_table(8, 16)
+    proj_relay(1)
+    proj_arrive(3)
+    send_table(16, 31)
+    proj_finish(0)
+    body_settled()
+    for copy in piece_copies:
+        copy.wait()
+    def weight_rows(begin, size, plane_at=None):
+        rows = slice(begin, begin + size)
+        if plane_at is None:
+            return packed[:, :, rows, :].reshape(PLANES * wide_count * size, D)
+        return packed[plane_at, :, rows, :].reshape(wide_count * size, D)
+
+    qkv_at, out_at, up_at, down_at, proj_at = 0, 48, 64, 128, MAIN
+    spot_count = incoming_ref.shape[0]
+    gain_one, shift_one = param_ref[9:10, :], param_ref[10:11, :]
+    gain_two, shift_two = param_ref[11:12, :], param_ref[12:13, :]
+    gain_end, shift_end = param_ref[13:14, :], param_ref[14:15, :]
+
+    def slot_rows(slot):
+        return pl.ds(pl.multiple_of(slot * entries, entries), entries)
+
+    def piece_lanes(slot):
+        return pl.ds(pl.multiple_of((slot - 1) * entries, entries), entries)
+
+    @pl.loop(1, SLOTS)
+    def _(slot):
+        places = lax.broadcasted_iota(jnp.int32, (spot_count, entries), 0)
+        chosen = jnp.where(places == spots_ref[pl.ds(slot, 1), :], 1.0, 0.0).astype(jnp.bfloat16)
+        onehot[:, piece_lanes(slot)] = chosen
+
+    bounds = (0, 4 * entries, PSLOTS * entries)
+    for begin, end in zip(bounds[:-1], bounds[1:]):
+        hats[entries + begin : entries + end, :] = dot_tn(onehot[:, begin:end], incoming_ref[...])
+
+    first_row = param_ref[0:1, :] + param_ref[1:2, :]
+    hats[0:entries, :] = jnp.broadcast_to(param_ref[0:1, :], (entries, D))
+    sums[...] = jnp.zeros_like(sums)
+
+    @pl.loop(0, SLOTS)
+    def _(slot):
+        rows = slot_rows(slot)
+        hat, scale = normalize(hats[rows, :] + param_ref[pl.ds(1 + slot, 1), :])
+        hats[rows, :] = hat
+        scales[rows, :] = jnp.broadcast_to(scale, (entries, 128))
+        part = (hat * gain_one + shift_one).astype(jnp.bfloat16)
+        normed[rows, :] = part
+
+    wholes = SLOTS * entries
+    tall = wholes // 2
+    for begin in range(0, wholes, tall):
+        rows = slice(begin, begin + tall)
+        keys[rows, :] = dot_nt(normed[rows, :], weight_rows(qkv_at, 48)[D:, :])
+
+    proj_relay(2)
+    proj_finish(1)
+    query = dot_nt(normed[0:entries, :], weight_rows(qkv_at, 48)[0:D, :])
+    lane_head = lax.broadcasted_iota(jnp.int32, (D, 128), 0) // HDIM
+    to_heads = jnp.where(
+        lane_head == lax.broadcasted_iota(jnp.int32, (D, 128), 1), 1.0, 0.0
+    ).astype(jnp.bfloat16)
+    head_lane = lax.broadcasted_iota(jnp.int32, (128, D), 1) // HDIM
+    from_heads = jnp.where(
+        head_lane == lax.broadcasted_iota(jnp.int32, (128, D), 0), 1.0, 0.0
+    ).astype(jnp.bfloat16)
+    root = 1.0 / math.sqrt(HDIM)
+    for slot in range(SLOTS):
+        rows = slice(slot * entries, (slot + 1) * entries)
+        grad_normed[rows, :] = query * keys[rows, 0:D]
+    for begin in range(0, wholes, tall):
+        rows = slice(begin, begin + tall)
+        probs[rows, :] = two_part_dot(grad_normed[rows, :], to_heads) * root
+    scores = []
+    for slot in range(SLOTS):
+        value = probs[slot * entries : (slot + 1) * entries, :]
+        if slot > 0:
+            value = jnp.where(live_ref[:, slot - 1 : slot] > 0, value, -1e30)
+        scores.append(value)
+    top = scores[0]
+    for value in scores[1:]:
+        top = jnp.maximum(top, value)
+    scores = [jnp.exp(value - top) for value in scores]
+    whole = scores[0]
+    for value in scores[1:]:
+        whole = whole + value
+    for slot in range(SLOTS):
+        probs[slot * entries : (slot + 1) * entries, :] = scores[slot] / whole
+    for begin in range(0, wholes, tall):
+        rows = slice(begin, begin + tall)
+        grad_normed[rows, :] = two_part_dot(probs[rows, :], from_heads)
+    attended = jnp.zeros((entries, D), jnp.float32)
+    for slot in range(SLOTS):
+        rows = slice(slot * entries, (slot + 1) * entries)
+        attended = attended + grad_normed[rows, :] * keys[rows, D:]
+    proj_relay(3)
+    proj_finish(2)
+    attended_bf = attended.astype(jnp.bfloat16)
+    residual = first_row + dot_nt(attended_bf, weight_rows(out_at, 16))
+    hat_two, scale_two = normalize(residual)
+    normed_two = (hat_two * gain_two + shift_two).astype(jnp.bfloat16)
+    span = 512
+    second = residual + param_ref[19:20, :]
+    for begin in range(0, FF, span):
+        lanes = slice(begin, begin + span)
+        bias = param_ref[15 + begin // span : 16 + begin // span, :]
+        gate = dot_nt(normed_two, weight_rows(up_at, 64, begin // span)) + bias
+        square = gate * gate
+        bend = jnp.tanh(math.sqrt(2.0 / math.pi) * (gate + 0.044715 * square * gate))
+        part = (0.5 * gate * (1.0 + bend)).astype(jnp.bfloat16)
+        active[:, lanes] = part
+        slope[:, lanes] = 0.5 * (1.0 + bend) + 0.5 * gate * (1.0 - bend * bend) * (
+            math.sqrt(2.0 / math.pi) * (1.0 + 3.0 * 0.044715 * square)
+        )
+        second = second + plain_dot(part, weight_rows(down_at, 64, begin // span))
+    hat_end, scale_end = normalize(second)
+    z_ref[...] = (hat_end * gain_end + shift_end).astype(jnp.bfloat16)
+
+    proj_finish(3)
+    proj_settled()
+    for copy in table_copies:
+        copy.wait()
+    own_proj_ref[...] = packed[me // wide_count, lax.rem(me, wide_count), MAIN:, :]
+    grad_z = jnp.zeros((entries, D), jnp.float32)
+    for source in range(0, grad_ref.shape[0], 2):
+        pair = jnp.concatenate([grad_ref[source], grad_ref[source + 1]], axis=1)
+        at_plane, at_wide = divmod(source, wide_count)
+        grad_z = grad_z + plain_dot(
+            pair, packed[at_plane, at_wide : at_wide + 2, MAIN:, :].reshape(2 * features, D)
+        )
+    vec_ref[...] = jnp.zeros_like(vec_ref)
+    vec_ref[13:14, :] = over_rows(grad_z * hat_end)
+    vec_ref[14:15, :] = over_rows(grad_z)
+    grad_second = normalize_back(grad_z, gain_end, hat_end, scale_end)
+    branch_two = grad_second.astype(jnp.bfloat16)
+    vec_ref[19:20, :] = over_rows(branch_two.astype(jnp.float32))
+    tile_lanes = D // features
+    vec_ref[pl.ds(20 + me // tile_lanes, 1), :] = jnp.concatenate(
+        [jnp.where(lax.rem(me, tile_lanes) == k, bias_total, 0.0) for k in range(tile_lanes)],
+        axis=1,
+    )
+
+    def store(value, block, chunk, height, offset):
+        for chip_at in range(CHIPS):
+            for core_at in range(CORES):
+                top = (chip_at * CORES + core_at) * height
+                main_ref[core_at, chunk, chip_at, block, offset : offset + height, :] = value[
+                    top : top + height, :
+                ].astype(jnp.bfloat16)
+
+    grad_two = jnp.zeros((entries, D), jnp.float32)
+    for block in range(PLANES):
+        lanes = slice(block * span, (block + 1) * span)
+        store(dot_tn(active[:, lanes], branch_two), block, 0, 64, 0)
+        gate_grad = (dot_nt(branch_two, weight_rows(down_at, 64, block)) * slope[:, lanes]).astype(jnp.bfloat16)
+        vec_ref[15 + block : 16 + block, :] = over_rows(gate_grad.astype(jnp.float32))
+        store(dot_tn(gate_grad, normed_two), block, 1, 64, 0)
+        grad_two = grad_two + plain_dot(gate_grad, weight_rows(up_at, 64, block))
+    vec_ref[11:12, :] = over_rows(grad_two * hat_two)
+    vec_ref[12:13, :] = over_rows(grad_two)
+    grad_residual = grad_second + normalize_back(grad_two, gain_two, hat_two, scale_two)
+    branch_one = grad_residual.astype(jnp.bfloat16)
+    grad_out = dot_tn(branch_one, attended_bf)
+    for block in range(PLANES):
+        store(grad_out[block * 128 : (block + 1) * 128, :], block, 2, 16, 0)
+    grad_attended = plain_dot(branch_one, weight_rows(out_at, 16))
+
+    for slot in range(SLOTS):
+        rows = slice(slot * entries, (slot + 1) * entries)
+        grad_kv[rows, D:] = (grad_normed[rows, :] * grad_attended).astype(jnp.bfloat16)
+        grad_normed[rows, :] = grad_attended * keys[rows, D:]
+    for begin in range(0, wholes, tall):
+        rows = slice(begin, begin + tall)
+        slides[rows, :] = two_part_dot(grad_normed[rows, :], to_heads)
+    inner = jnp.zeros((entries, 128), jnp.float32)
+    for slot in range(SLOTS):
+        rows = slice(slot * entries, (slot + 1) * entries)
+        inner = inner + probs[rows, :] * slides[rows, :]
+    for slot in range(SLOTS):
+        rows = slice(slot * entries, (slot + 1) * entries)
+        slides[rows, :] = probs[rows, :] * (slides[rows, :] - inner)
+    for begin in range(0, wholes, tall):
+        rows = slice(begin, begin + tall)
+        grad_normed[rows, :] = two_part_dot(slides[rows, :], from_heads) * root
+    grad_query = jnp.zeros((entries, D), jnp.float32)
+    for slot in range(SLOTS):
+        rows = slice(slot * entries, (slot + 1) * entries)
+        push = grad_normed[rows, :]
+        grad_query = grad_query + push * keys[rows, 0:D]
+        grad_kv[rows, 0:D] = (push * query).astype(jnp.bfloat16)
+    query_bf = grad_query.astype(jnp.bfloat16)
+
+    grad_q = dot_tn(query_bf, normed[0:entries, :])
+    grad_k = dot_tn(grad_kv[:, 0:D], normed[...])
+    grad_v = dot_tn(grad_kv[:, D:], normed[...])
+    third = D * 3 // PLANES
+    every = jnp.concatenate([grad_q, grad_k, grad_v], axis=0)
+    for block in range(PLANES):
+        store(every[block * third : (block + 1) * third, :], block, 2, 48, 16)
+
+    for begin in range(0, wholes, tall):
+        rows = slice(begin, begin + tall)
+        grad_normed[rows, :] = plain_dot(grad_kv[rows, :], weight_rows(qkv_at, 48)[D:, :])
+
+    grad_normed[0:entries, :] += plain_dot(query_bf, weight_rows(qkv_at, 48)[0:D, :])
+
+    @pl.loop(0, SLOTS)
+    def _(slot):
+        rows = slot_rows(slot)
+        grad = grad_normed[rows, :]
+        hat = hats[rows, :]
+        sums[0:1, :] += over_rows(grad * hat)
+        sums[1:2, :] += over_rows(grad)
+        grad_x = normalize_back(grad, gain_one, hat, scales[rows, 0:1])
+        vec_ref[pl.ds(1 + slot, 1), :] = over_rows(grad_x)
+
+        @pl.when(slot > 0)
+        def _():
+            grad_pieces[pl.ds(pl.multiple_of((slot - 1) * entries, entries), entries), :] = (
+                grad_x.astype(jnp.bfloat16)
+            )
+
+    vec_ref[9:11, :] = sums[0:2, :]
+    vec_ref[1:2, :] += over_rows(grad_residual)
+    vec_ref[0:1, :] = vec_ref[1:2, :]
+    tile = 256
+    for begin in range(0, spot_count, tile):
+        outgoing_ref[begin : begin + tile, :] = plain_dot(
+            onehot[begin : begin + tile, :], grad_pieces[...]
+        ).astype(jnp.bfloat16)
+
+
+def layer(master, pieces, table, text_ids, text_mask, text_cot, slot_mask, params, cap):
+    f32, bf = jnp.float32, jnp.bfloat16
+    dma = pltpu.SemaphoreType.DMA
+    count = PLANES * CHIPS * CORES
+    entries = slot_mask.shape[0]
+    features = text_cot.shape[0]
+    rows = entries * SLOTS
+    hbm = pl.BlockSpec(memory_space=pl.ANY)
+    vmem = pl.BlockSpec(memory_space=pltpu.VMEM)
+    spread_count = 6 + 9 * PLANES
+    return pl.pallas_call(
+        layer_kernel,
+        out_shape=(
+            jax.ShapeDtypeStruct((entries, D), bf),
+            jax.ShapeDtypeStruct((CORES, CHUNKS, CHIPS, PLANES, CHUNK, D), bf),
+            jax.ShapeDtypeStruct((count * cap, D), bf),
+            jax.ShapeDtypeStruct((CORES * VROWS, D), f32),
+            jax.ShapeDtypeStruct((count, entries, features), bf),
+            jax.ShapeDtypeStruct((features, D), bf),
+            jax.ShapeDtypeStruct((count * cap, 1), jnp.int32),
+        ),
+        in_specs=[hbm] + [vmem] * 7,
+        out_specs=(vmem,) * 7,
+        scratch_shapes=[
+            pltpu.VMEM((PART, D), f32),
+            pltpu.VMEM((count,) + pieces.shape, jnp.int32),
+            pltpu.VMEM((SLOTS, entries), jnp.int32),
+            pltpu.VMEM((count, entries * PSLOTS), f32),
+            pltpu.VMEM((count, entries * PSLOTS), f32),
+            pltpu.VMEM((count * cap, D), bf),
+            pltpu.VMEM((count, entries, features), bf),
+            pltpu.VMEM((PLANES, CHIPS * CORES, PART, D), bf),
+            pltpu.VMEM((count * entries // BANDS, BANDS * features), f32),
+            pltpu.VMEM((count * cap, entries * PSLOTS), bf),
+            pltpu.VMEM((rows, D), f32),
+            pltpu.VMEM((rows, 128), f32),
+            pltpu.VMEM((rows, D), bf),
+            pltpu.VMEM((rows, 2 * D), f32),
+            pltpu.VMEM((rows, 128), f32),
+            pltpu.VMEM((rows, 2 * D), bf),
+            pltpu.VMEM((rows, D), f32),
+            pltpu.VMEM((entries * PSLOTS, D), bf),
+            pltpu.VMEM((entries, FF), bf),
+            pltpu.VMEM((entries, FF), f32),
+            pltpu.VMEM((rows, 128), f32),
+            pltpu.VMEM((8, D), f32),
+            dma((6,)),
+        ]
+        + [dma((count - 1,))] * 6
+        + [dma((spread_count,))] * 4,
+        compiler_params=pltpu.CompilerParams(
+            collective_id=5, has_side_effects=True, vmem_limit_bytes=63 * 2**20
+        ),
+        name="layer",
+    )(master, pieces, table, text_ids, text_mask, text_cot, slot_mask, params)
+
+
+def piece_grad_kernel(rows_ref, grads_ref, out_ref):
+    tile = out_ref.shape[0]
+    at = lax.broadcasted_iota(jnp.int32, (tile, rows_ref.shape[1]), 0) + pl.program_id(0) * tile
+    chosen = jnp.where(at == rows_ref[...], 1.0, 0.0).astype(jnp.bfloat16)
+    out_ref[...] = plain_dot(chosen, grads_ref[...])
+
+
+def add_piece_grads(rows, grads, group_rows):
+    tile = 256
+    return pl.pallas_call(
+        piece_grad_kernel,
+        grid=(group_rows // tile,),
+        out_shape=jax.ShapeDtypeStruct((group_rows, D), jnp.float32),
+        in_specs=[
+            pl.BlockSpec(rows.shape, lambda i: (0, 0)),
+            pl.BlockSpec(grads.shape, lambda i: (0, 0)),
+        ],
+        out_specs=pl.BlockSpec((tile, D), lambda i: (i, 0)),
+        compiler_params=pltpu.CompilerParams(vmem_limit_bytes=24 * 2**20),
+        name="add_piece_grads",
+    )(rows, grads)
+
+
+def on_device(
+    piece_table,
+    piece_ids,
+    slot_mask,
+    text_ids,
+    text_mask,
+    text_cot,
+    mat_master,
+    mat_momentum,
+    mat_ema,
+    vec_master,
+    vec_moment1,
+    vec_moment2,
+    vec_ema,
+):
+    device_count = PLANES * CHIPS * CORES
+    me = lax.axis_index("wide") * PLANES + lax.axis_index("narrow")
+    entries = piece_ids.shape[0]
+    group_rows = piece_table.shape[0]
+    cap = piece_cap(group_rows)
+    feature_rows = text_cot.shape[0]
+    params = vec_master.reshape(-1, D)
+    pieces = jnp.pad(piece_ids.T, ((0, SLOTS - PSLOTS), (0, 0)))
+    (
+        z_own,
+        main,
+        grad_outgoing,
+        vec_rows,
+        grad_own,
+        proj_own,
+        asked_rows,
+    ) = layer(
+        mat_master[0], pieces, piece_table, text_ids, text_mask, text_cot, slot_mask, params, cap
+    )
+    bias_out = vec_master[vec_master.shape[0] - OUTW :]
+    bias_own = lax.dynamic_slice_in_dim(bias_out, me * feature_rows, feature_rows, 0)
+    text_embeds, main_sum, proj_sum, vec_sum, gram, high, low = settle(
+        z_own,
+        main,
+        vec_rows.reshape(CORES, VROWS, D),
+        grad_own,
+        proj_own,
+        bias_own[:, None],
+        mat_momentum[0],
+        text_ids,
+        text_mask,
+    )
+    vec_grad = vec_sum.reshape(-1)[: vec_master.shape[0]]
+    grad_outgoing, _ = lax.optimization_barrier((grad_outgoing, gram))
+    grad_incoming = lax.all_to_all(
+        grad_outgoing.reshape(device_count, cap, D), BOTH, 0, 0, tiled=True
+    ).reshape(device_count * cap, D)
+    rows = muon_rows(gram, high, low)
+    grad_block, momentum_block, weight_block, ema_block = finish(
+        main_sum, proj_sum, rows, mat_momentum, mat_master, mat_ema
+    )
+    piece_grad = add_piece_grads(asked_rows.reshape(1, -1), grad_incoming, group_rows)
+    return (
+        text_embeds,
+        piece_grad,
+        grad_block,
+        momentum_block,
+        weight_block,
+        ema_block,
+    ) + adam(vec_grad, vec_master, vec_moment1, vec_moment2, vec_ema)
 
 
 def solution(mesh):
@@ -417,6 +2136,8 @@
         P(),
         P(),
     )
+    fits = mesh.shape["wide"] == CHIPS * CORES and mesh.shape["narrow"] == PLANES
+    step = on_device if fits else on_device_plain
     return jax.shard_map(
-        on_device, mesh=mesh, in_specs=in_specs, out_specs=out_specs, check_vma=False
-    )
+        step, mesh=mesh, in_specs=in_specs, out_specs=out_specs, check_vma=False
+    )

time: 921 us -> 330 us (0.36)
  Pallas kernels: 0 us -> 297 us
  waiting for transfers between devices: 293 us -> 0.01 us
  matrix products: 228 us -> 0 us
  blocking collectives: 146 us -> 0 us
  local copies, waits for them, and re-layouts: 129 us -> 19 us
  other arithmetic: 59.9 us -> 2.28 us
  starting transfers between devices: 32.6 us -> 6.15 us
  between operations: 19.6 us -> 1 us
    pallas_call x0 -> x5, Pallas kernels: none -> 297 us  [the longest x1 131 us: layer(): pl.pallas_call(layer_kernel, out_shape=(jax.ShapeDtypeStruct((entries, D)...]
    dot_general x134 -> x0, matrix products: 228 us -> none  [the longest x40 51.1 us: on_device(): gram = jnp.dot(jnp.dot(gram, poly, precision=HIGH), poly, precision=HIGH)]
    all_to_all x3 -> x0, waiting for transfers between devices: 145 us -> none  [the longest x1 103 us: on_device(): terms = lax.all_to_all(packed_term, BOTH, 0, 0, tiled=True)]
    all_gather x1 -> x0, blocking collectives: 101 us -> none  [on_device(): every_ids = lax.all_gather(slot_ids, BOTH, axis=0, tiled=False)]
    psum x1 -> x0, waiting for transfers between devices: 77.9 us -> none  [on_device(): lax.psum(jnp.stack([gram_of(segment) for segment in segments]), 'narrow')]
    all_gather x4 -> x0, waiting for transfers between devices: 70.1 us -> none  [the longest x1 47.7 us: on_device(): every_normed = lax.all_gather(normed_three_bf, BOTH, axis=0, tiled=True)]
    gather x6 -> x0, local copies, waits for them, and re-layouts: 64.7 us -> none  [the longest x5 36.8 us: on_device(): square = jnp.sum(jnp.diagonal(grams[position]))]
    psum x1 -> x0, blocking collectives: 44.6 us -> none  [on_device(): vec_grad = lax.psum(vec_local, BOTH)]
  transfers between devices with their start and end apart: 9 -> 1, of which waited for: 5 -> 0; matrix products, arithmetic and copies ran while one was open for 22% -> 1% of each run, Pallas kernels for 0% -> 16%
where the time goes in v4:
time: 330 us; the launch traced here: 325 us
  Pallas kernels  297 us (90%)
  local copies, waits for them, and re-layouts  19 us (6%)
  starting transfers between devices  6.15 us (2%)
    pallas_call x1, Pallas kernels, layer(): pl.pallas_call(layer_kernel, out_shape=(jax.ShapeDtypeStruct((entries, D)...  131 us
    pallas_call x1, Pallas kernels, settle(): pl.pallas_call(settle_kernel, out_shape=(jax.ShapeDtypeStruct((features,...  110 us
    pallas_call x1, Pallas kernels, muon_rows(): pl.pallas_call(muon_kernel, out_shape=jax.ShapeDtypeStruct((total, D), jn...  44 us
    unnamed x31, local copies, waits for them, and re-layouts  14.7 us
    pallas_call x1, Pallas kernels, finish(): pl.pallas_call(finish_kernel, grid=((MAIN_TILES + MOST_TILES) // tall,),...  7.58 us
  transfers between devices with their start and end apart: 1, of which 0 were waited for; matrix products, arithmetic and copies ran while one was open for 1% of the time, Pallas kernels for 16%

profile of v4, /device:TPU:31, one launch (start us, length us, event | category | flops | bytes accessed | tf_op | source)
XLA Modules:
  0.0 325.1 jit_solution(10568243891333601275)
XLA Ops:
  0.6 1.5 reshape.46.param_ref
  2.1 0.7 slice.6
  2.8 1.4 copy.26.live_ref
  4.2 1.3 pad.4.pieces_ref
  5.5 0.1 dynamic-slice_bitcast_fusion
  5.6 0.7 copy.27.bias_ref
  6.3 131.3 %layer.1 = (bf16[128,512]{1,0:T(8,128)(2,1)}, bf16[2,3,4,4,64,512]{5,4,3,2,1,0:T(8,128)(2,1)}, bf16[2048,512]{1,0:T(8,128)(2,1)}, f32[32,512]{1,0:T(8,128)}, bf1...) custom-call(f32[2560,512]{1,0:T(8,128)} %bitcast.14, s32[8,128]{1,0:T(8,128)} %pad.4.pieces_ref, ...), custom_call_target="tpu_custom_call" | custom-call | tf_op jit(solution)/shard_map/layer/pallas_call | solution.py:1973
  137.6 110.1 %settle.1 = (f32[128,8192]{1,0:T(8,128)}, bf16[1536,512]{1,0:T(8,128)(2,1)}, bf16[2,4,4,32,512]{4,3,2,1,0:T(8,128)(2,1)}, f32[2,16,512]{2,1,0:T(8,128)}, f32[512...) custom-call(bf16[128,512]{1,0:T(8,128)(2,1)} %get-tuple-element.30.z_ref, ...), custom_call_target="tpu_custom_call" | custom-call | tf_op jit(solution)/shard_map/settle/pallas_call | solution.py:1151
  247.7 6.1 %all-to-all-start = ((bf16[32,64,512]{2,1,0:T(8,128)(2,1)}), bf16[32,64,512]{2,1,0:T(8,128)(2,1)S(1)}, u32[]{:S(2)}, u32[]{:S(2)}) async-start(bf16[32,64,512]{2,1,0:T(8,128)(2,1)} %bitcast.19), calls=%async_computation | async-start | bytes 4194304 | tf_op jit(solution)/shard_map/all_to_all | solution.py:2092
  253.9 1.6 reduce
  255.5 1.3 copy-done.5
  256.8 1.2 copy-done.6
  258.0 1.2 copy-done.7
  259.3 44.0 %muon_rows.1.rows_ref = bf16[2560,512]{1,0:T(8,128)(2,1)S(1)} custom-call(f32[512,512]{1,0:T(8,128)S(1)} %copy-done.5, bf16[1024,512]{1,0:T(8,128)(2,1)S(1)} %copy-done.6, bf16[1024,512]{1,0:T(8,128)(2,1)S(1)} %copy-done.7), custom_call_target="tpu_custom_call" | custom-call | tf_op jit(solution)/shard_map/muon_rows/pallas_call | solution.py:1396
  303.3 0.0 copy-start
  303.4 2.5 copy-done
  305.8 2.5 copy-done.1
  308.3 2.5 copy-done.2
  310.8 7.6 %finish.1 = (f32[1,2560,512]{2,1,0:T(8,128)}, f32[1,2560,512]{2,1,0:T(8,128)}, f32[1,2560,512]{2,1,0:T(8,128)}, f32[1,2560,512]{2,1,0:T(8,128)}) custom-call(bf16[1536,512]{1,0:T(8,128)(2,1)S(1)} %copy-done.3, bf16[8,4,32,512]{3,2,1,0:T(8,128)(2,1)S(1)} %bitcast.16, bf16[2560,512]{1,0:T(8,128)(2,1)S(1)} %muon_rows.1.rows_ref, f32[1,2560,512]{2,1,0:T(8,128)S(1)} %copy-done, ...), custom_call_target="tpu_custom_call" | custom-call | flops 15728640 | bytes 41943040 | tf_op jit(solution)/shard_map/finish/pallas_call | solution.py:1448
  318.4 0.0 copy-done.11
  318.4 0.7 multiply_add_fusion
  319.1 0.0 all-to-all-done
  319.1 3.7 %add_piece_grads.1 = f32[1024,512]{1,0:T(8,128)} custom-call(s32[1,2048]{1,0:T(1,128)S(1)} %bitcast.17, bf16[2048,512]{1,0:T(8,128)(2,1)S(1)} %bitcast.15), custom_call_target="tpu_custom_call" | custom-call | tf_op jit(solution)/shard_map/add_piece_grads/pallas_call | solution.py:2029
  322.9 2.0 copy.30
  (21 shorter events, 0.1 us)
Async XLA Ops:
  247.7 7.8 %copy-start.10 = (f32[2,16,512]{2,1,0:T(8,128)S(1)}, f32[2,16,512]{2,1,0:T(8,128)}, u32[]{:S(2)}) copy-start(f32[2,16,512]{2,1,0:T(8,128)} %get-tuple-element.48) | copy-start | bytes 196612
  247.7 55.6 %copy-start.4 = (bf16[2,4,4,32,512]{4,3,2,1,0:T(8,128)(2,1)S(1)}, bf16[2,4,4,32,512]{4,3,2,1,0:T(8,128)(2,1)}, u32[]{:S(2)}) copy-start(bf16[2,4,4,32,512]{4,3,2,1,0:T(8,128)(2,1)} %get-tuple-element.41) | copy-start | bytes 3145732
  247.7 71.4 %all-to-all-start = ((bf16[32,64,512]{2,1,0:T(8,128)(2,1)}), bf16[32,64,512]{2,1,0:T(8,128)(2,1)S(1)}, u32[]{:S(2)}, u32[]{:S(2)}) async-start(bf16[32,64,512]{2,1,0:T(8,128)(2,1)} %bitcast.19), calls=%async_computation | async-start | bytes 4194304 | tf_op jit(solution)/shard_map/all_to_all | solution.py:2092
  255.4 47.9 %copy-start.3 = (bf16[1536,512]{1,0:T(8,128)(2,1)S(1)}, bf16[1536,512]{1,0:T(8,128)(2,1)}, u32[]{:S(2)}) copy-start(bf16[1536,512]{1,0:T(8,128)(2,1)} %get-tuple-element.40.main_ref) | copy-start | bytes 4718596
  255.5 1.3 copy-start.5
  256.8 1.2 copy-start.6
  258.0 1.2 copy-start.7
  303.3 2.5 copy-start
  305.8 2.5 copy-start.1
  308.3 2.5 copy-start.2
  310.8 7.6 %copy-start.9 = (f32[14336]{0:T(1024)S(1)}, f32[14336]{0:T(1024)}, u32[]{:S(2)}) copy-start(f32[14336]{0:T(1024)} %param.22) | copy-start | bytes 172036
  310.8 7.6 %copy-start.11 = (f32[14336]{0:T(1024)S(1)}, f32[14336]{0:T(1024)}, u32[]{:S(2)}) copy-start(f32[14336]{0:T(1024)} %param.25) | copy-start | bytes 172036
  310.8 7.6 %copy-start.12 = (f32[14336]{0:T(1024)S(1)}, f32[14336]{0:T(1024)}, u32[]{:S(2)}) copy-start(f32[14336]{0:T(1024)} %param.24) | copy-start | bytes 172036
  310.8 7.6 %copy-start.13 = (f32[14336]{0:T(1024)S(1)}, f32[14336]{0:T(1024)}, u32[]{:S(2)}) copy-start(f32[14336]{0:T(1024)} %param.23) | copy-start | bytes 172036
  319.1 3.7 %copy-start.8 = (f32[128,8192]{1,0:T(8,128)S(1)}, f32[128,8192]{1,0:T(8,128)}, u32[]{:S(2)}) copy-start(f32[128,8192]{1,0:T(8,128)} %get-tuple-element.65) | copy-start | bytes 12582916

commit v5 on v4

--- a/solution.py
+++ b/solution.py
@@ -1410,7 +1410,7 @@
             dma((len(SHARES) * 9,)),
         ],
         compiler_params=pltpu.CompilerParams(
-            collective_id=4, has_side_effects=True, vmem_limit_bytes=40 * 2**20
+            collective_id=4, has_side_effects=True, vmem_limit_bytes=60 * 2**20
         ),
         name="muon_rows",
     )(gram, high, low)
@@ -1492,6 +1492,105 @@
     return jnp.sum(values, axis=0, keepdims=True)
 
 
+def plane_sums(first, near_copies, near, buffers, far_sems, deep_sems):
+    x_first, y_first, x_second, y_second, second, deep = buffers
+    wide_at, plane, chip, core = place()
+    _, _, planes = neighbours(wide_at, plane, chip, core)
+    x_wide, y_wide = across(wide_at, plane, chip, core)
+    x_near, y_near = (x_wide, plane), (y_wide, plane)
+    x_at, y_at = lax.rem(chip, SIDE), chip // SIDE
+    lows, highs = pl.ds(0, 2), pl.ds(2, 2)
+    sent = []
+    waiting = {}
+
+    def start(src, dst, sems, index, target):
+        copy = remote(src, dst, sems, index, target)
+        copy.start()
+        sent.append(copy)
+        return copy
+
+    def add(left, right):
+        return (left.astype(jnp.float32) + right.astype(jnp.float32)).astype(jnp.bfloat16)
+
+    def first_step(chunk):
+        near_copies[chunk].wait_recv()
+
+        @pl.loop(0, CHIPS * PLANES)
+        def _(step):
+            y, x, m = step // (SIDE * PLANES), lax.rem(step // PLANES, SIDE), lax.rem(step, PLANES)
+            first[chunk, y, x, m] = add(first[chunk, y, x, m], near[chunk, y, x, m])
+
+        base = chunk * 4
+        waiting["x", chunk] = start(
+            first.at[chunk, :, 1 - x_at, lows], x_first.at[chunk], far_sems, base, x_near
+        )
+        waiting["y", chunk] = start(
+            first.at[chunk, 1 - y_at, :, highs], y_first.at[chunk], far_sems, base + 1, y_near
+        )
+
+    def second_step(chunk):
+        base = chunk * 4
+        waiting["x", chunk].wait_recv()
+        for y in range(SIDE):
+            for m in range(2):
+                first[chunk, y, x_at, m] = add(first[chunk, y, x_at, m], x_first[chunk, y, m])
+        waiting["yy", chunk] = start(
+            first.at[chunk, 1 - y_at, x_at, lows], y_second.at[chunk], far_sems, base + 2, y_near
+        )
+        waiting["y", chunk].wait_recv()
+        for x in range(SIDE):
+            for m in range(2):
+                first[chunk, y_at, x, 2 + m] = add(
+                    first[chunk, y_at, x, 2 + m], y_first[chunk, x, m]
+                )
+        waiting["xx", chunk] = start(
+            first.at[chunk, y_at, 1 - x_at, highs], x_second.at[chunk], far_sems, base + 3, x_near
+        )
+
+    def deep_step(chunk):
+        waiting["yy", chunk].wait_recv()
+        for m in range(2):
+            second[chunk, m] = add(first[chunk, y_at, x_at, m], y_second[chunk, m])
+        waiting["xx", chunk].wait_recv()
+        for m in range(2):
+            second[chunk, 2 + m] = add(first[chunk, y_at, x_at, 2 + m], x_second[chunk, m])
+        for k, target in enumerate(planes):
+            to_plane = lax.rem(plane + k + 1, PLANES)
+            waiting["z", chunk, k] = start(
+                second.at[chunk, to_plane], deep.at[chunk, k], deep_sems, chunk * 3 + k, target
+            )
+
+    def total(chunk):
+        value = second[chunk, plane].astype(jnp.float32)
+        for k in range(3):
+            waiting["z", chunk, k].wait_recv()
+            value = value + deep[chunk, k].astype(jnp.float32)
+        return value
+
+    def sums_settled():
+        for copy in sent:
+            copy.wait_send()
+
+    return first_step, second_step, deep_step, total, sums_settled
+
+
+def sum_scratch(chunks):
+    dma = pltpu.SemaphoreType.DMA
+    bf = jnp.bfloat16
+    return [
+        pltpu.VMEM((chunks, SIDE, 2, CHUNK, D), bf),
+        pltpu.VMEM((chunks, SIDE, 2, CHUNK, D), bf),
+        pltpu.VMEM((chunks, 2, CHUNK, D), bf),
+        pltpu.VMEM((chunks, 2, CHUNK, D), bf),
+        pltpu.VMEM((chunks, PLANES, CHUNK, D), bf),
+        pltpu.VMEM((chunks, 3, CHUNK, D), bf),
+        dma((chunks * 4,)),
+        dma((chunks * 4,)),
+        dma((chunks * 3,)),
+        dma((chunks * 3,)),
+    ]
+
+
 def layer_kernel(
     master_ref,
     pieces_ref,
@@ -1514,7 +1613,8 @@
     asked_ranks,
     asked_locals,
     incoming_ref,
-    grad_ref,
+    proj_rows,
+    proj_stage,
     packed,
     text_total,
     onehot,
@@ -1531,12 +1631,22 @@
     slides,
     sums,
     local_sem,
+    x_first,
+    y_first,
+    x_second,
+    y_second,
+    second_sum,
+    deep,
+    far_send,
+    far_recv,
+    deep_send,
+    deep_recv,
     tell_send,
     tell_recv,
     piece_send,
     piece_recv,
-    table_send,
-    table_recv,
+    near_send,
+    near_recv,
     body_send,
     body_recv,
     proj_send,
@@ -1554,20 +1664,31 @@
         for k in range(1, wide_count * PLANES)
     ]
 
-    def spread_of(own, held, sems):
-        return spread_steps(own, held, sems, 0, at)
-
-    body_held = packed.at[:, :, pl.ds(0, MAIN)]
-    proj_held = packed.at[:, :, pl.ds(MAIN, PART - MAIN)]
-    body_spread = spread_of(body_held.at[plane, wide_at], body_held, (body_send, body_recv))
-    proj_spread = spread_of(proj_held.at[plane, wide_at], proj_held, (proj_send, proj_recv))
-    body_begin, body_arrive, body_relay, body_finish, body_settled = body_spread
-    proj_begin, proj_arrive, proj_relay, proj_finish, proj_settled = proj_spread
+    sibling, _, planes = neighbours(*at)
+    body_begin, body_arrive, body_relay, body_finish, body_settled = spread_steps(
+        packed.at[plane, wide_at], packed, (body_send, body_recv), 0, at
+    )
+    holds_proj = plane == chip
+    proj_sems = (proj_send, proj_recv)
+    features = cot_ref.shape[0]
+
+    def proj_load():
+        begin = master_ref.shape[0] - OUTW // PLANES + core * PLANES * features
+        source = pl.ds(pl.multiple_of(begin, 16), PLANES * features)
+        return pltpu.make_async_copy(master_ref.at[source], proj_rows, local_sem.at[4])
+
+    def proj_copy(k):
+        to_plane = lax.rem(plane + k + 1, PLANES)
+        return remote(proj_stage.at[to_plane], own_proj_ref, proj_sems, k, planes[k])
+
+    @pl.when(holds_proj)
+    def _():
+        proj_load().start()
 
     loads = []
     begin = 0
     block = 0
-    for index, row_total in enumerate(matrix_rows()):
+    for index, row_total in enumerate(matrix_rows()[:4]):
         height = row_total // PLANES
         size = height // wide_count
         copy = pltpu.make_async_copy(
@@ -1589,8 +1710,17 @@
     for copy in loads:
         copy.wait()
     packed[plane, wide_at] = own_rows[...].astype(jnp.bfloat16)
+
+    def proj_begin():
+        @pl.when(holds_proj)
+        def _():
+            proj_load().wait()
+            proj_stage[...] = proj_rows[...].astype(jnp.bfloat16).reshape(proj_stage.shape)
+            for k in range(PLANES - 1):
+                proj_copy(k).start()
+            own_proj_ref[...] = proj_stage[plane]
+
     piece_copies = []
-    table_copies = []
 
     def piece_rows(device):
         return pl.ds(pl.multiple_of(device * cap, cap), cap)
@@ -1608,21 +1738,42 @@
             copy.start()
             piece_copies.append(copy)
 
-    def send_table(begin, end):
-        for index in range(begin, end):
-            wide_to, plane_to = peers[index]
+    near_copies = []
+    dz_first, dz_second, dz_deep, dz_total, dz_settled = plane_sums(
+        main_ref.at[core],
+        near_copies,
+        grad_kv,
+        (x_first, y_first, x_second, y_second, second_sum, deep),
+        (far_send, far_recv),
+        (deep_send, deep_recv),
+    )
+
+    def dz_begin():
+        @pl.when(jnp.logical_not(holds_proj))
+        def _():
+            k = lax.rem(plane - chip - 1 + PLANES, PLANES)
+            remote(proj_stage.at[0], own_proj_ref, proj_sems, k, sibling).wait_recv()
+
+        proj = own_proj_ref[...]
+        for wide in range(wide_count):
+            block = own_grad_ref[wide * PLANES : (wide + 1) * PLANES]
+            value = plain_dot(block.reshape(PLANES * entries, features), proj)
+            value = value.astype(jnp.bfloat16).reshape(PLANES, entries, D)
+            y, x = divmod(wide // CORES, SIDE)
+            for part in range(entries // CHUNK):
+                main_ref[wide % CORES, part, y, x] = value[:, part * CHUNK : (part + 1) * CHUNK, :]
+        for part in range(entries // CHUNK):
             copy = remote(
-                own_grad_ref.at[wide_to * PLANES + plane_to],
-                grad_ref.at[me],
-                (table_send, table_recv),
-                index,
-                (wide_to, plane_to),
+                main_ref.at[1 - core, part],
+                grad_kv.at[part],
+                (near_send, near_recv),
+                part,
+                sibling,
             )
             copy.start()
-            table_copies.append(copy)
+            near_copies.append(copy)
 
     text_rows = own_grad_ref.shape[0] * own_grad_ref.shape[1] // BANDS
-    features = cot_ref.shape[0]
     text_total[...] = jnp.zeros_like(text_total)
 
     row_tiles = ids_ref.shape[1] // TEXT_TILE
@@ -1696,24 +1847,20 @@
     body_arrive(1)
     build_pieces()
     send_pieces(0, 6)
-    text_steps(1, 3)
+    text_steps(1, 4)
     body_relay(0)
     body_arrive(2)
     send_pieces(6, 12)
-    text_steps(3, 5)
+    text_steps(4, 8)
     body_arrive(3)
     body_relay(1)
     body_finish(0)
-    send_pieces(12, 18)
-    text_steps(5, 8)
+    send_pieces(12, 16)
+    text_steps(8, 12)
     body_relay(2)
     body_finish(1)
-    send_pieces(18, 24)
-    text_steps(8, 11)
-    body_relay(3)
-    body_finish(2)
-    send_pieces(24, 31)
-    text_steps(11, 16)
+    send_pieces(16, 20)
+    text_steps(12, 16)
     bias_total = jnp.zeros((1, features), jnp.float32)
     blocks = own_grad_ref.shape[0] // BANDS
     for b in range(BANDS):
@@ -1722,17 +1869,19 @@
             (blocks,) + own_grad_ref.shape[1:]
         )
         bias_total = bias_total + over_rows(rounded.astype(jnp.float32))
-    grad_ref[me] = own_grad_ref[me]
+    dz_begin()
+    body_relay(3)
+    body_finish(2)
+    send_pieces(20, 24)
+    dz_first(0)
+    dz_first(1)
+    send_pieces(24, 28)
     body_finish(3)
-    proj_arrive(1)
-    send_table(0, 8)
-    proj_relay(0)
-    proj_arrive(2)
-    send_table(8, 16)
-    proj_relay(1)
-    proj_arrive(3)
-    send_table(16, 31)
-    proj_finish(0)
+    dz_second(0)
+    send_pieces(28, 31)
+    dz_second(1)
+    dz_deep(0)
+    dz_deep(1)
     body_settled()
     for copy in piece_copies:
         copy.wait()
@@ -1742,7 +1891,7 @@
             return packed[:, :, rows, :].reshape(PLANES * wide_count * size, D)
         return packed[plane_at, :, rows, :].reshape(wide_count * size, D)
 
-    qkv_at, out_at, up_at, down_at, proj_at = 0, 48, 64, 128, MAIN
+    qkv_at, out_at, up_at, down_at = 0, 48, 64, 128
     spot_count = incoming_ref.shape[0]
     gain_one, shift_one = param_ref[9:10, :], param_ref[10:11, :]
     gain_two, shift_two = param_ref[11:12, :], param_ref[12:13, :]
@@ -1783,8 +1932,6 @@
         rows = slice(begin, begin + tall)
         keys[rows, :] = dot_nt(normed[rows, :], weight_rows(qkv_at, 48)[D:, :])
 
-    proj_relay(2)
-    proj_finish(1)
     query = dot_nt(normed[0:entries, :], weight_rows(qkv_at, 48)[0:D, :])
     lane_head = lax.broadcasted_iota(jnp.int32, (D, 128), 0) // HDIM
     to_heads = jnp.where(
@@ -1823,8 +1970,6 @@
     for slot in range(SLOTS):
         rows = slice(slot * entries, (slot + 1) * entries)
         attended = attended + grad_normed[rows, :] * keys[rows, D:]
-    proj_relay(3)
-    proj_finish(2)
     attended_bf = attended.astype(jnp.bfloat16)
     residual = first_row + dot_nt(attended_bf, weight_rows(out_at, 16))
     hat_two, scale_two = normalize(residual)
@@ -1846,18 +1991,16 @@
     hat_end, scale_end = normalize(second)
     z_ref[...] = (hat_end * gain_end + shift_end).astype(jnp.bfloat16)
 
-    proj_finish(3)
-    proj_settled()
-    for copy in table_copies:
-        copy.wait()
-    own_proj_ref[...] = packed[me // wide_count, lax.rem(me, wide_count), MAIN:, :]
-    grad_z = jnp.zeros((entries, D), jnp.float32)
-    for source in range(0, grad_ref.shape[0], 2):
-        pair = jnp.concatenate([grad_ref[source], grad_ref[source + 1]], axis=1)
-        at_plane, at_wide = divmod(source, wide_count)
-        grad_z = grad_z + plain_dot(
-            pair, packed[at_plane, at_wide : at_wide + 2, MAIN:, :].reshape(2 * features, D)
-        )
+    grad_z = jnp.concatenate([dz_total(part) for part in range(entries // CHUNK)], axis=0)
+    for copy in near_copies:
+        copy.wait_send()
+    dz_settled()
+
+    @pl.when(holds_proj)
+    def _():
+        for k in range(PLANES - 1):
+            proj_copy(k).wait_send()
+
     vec_ref[...] = jnp.zeros_like(vec_ref)
     vec_ref[13:14, :] = over_rows(grad_z * hat_end)
     vec_ref[14:15, :] = over_rows(grad_z)
@@ -1874,7 +2017,8 @@
         for chip_at in range(CHIPS):
             for core_at in range(CORES):
                 top = (chip_at * CORES + core_at) * height
-                main_ref[core_at, chunk, chip_at, block, offset : offset + height, :] = value[
+                y, x = divmod(chip_at, SIDE)
+                main_ref[core_at, chunk, y, x, block, offset : offset + height, :] = value[
                     top : top + height, :
                 ].astype(jnp.bfloat16)
 
@@ -1894,10 +2038,19 @@
     for block in range(PLANES):
         store(grad_out[block * 128 : (block + 1) * 128, :], block, 2, 16, 0)
     grad_attended = plain_dot(branch_one, weight_rows(out_at, 16))
+    halves_of = entries // CHUNK
+
+    def store_kv(kind, slot, value):
+        y, x = divmod(slot // 2, SIDE)
+        begin = slot % 2 * halves_of
+        grad_kv[kind, y, x, begin : begin + halves_of] = value.astype(jnp.bfloat16).reshape(
+            halves_of, CHUNK, D
+        )
+
 
     for slot in range(SLOTS):
         rows = slice(slot * entries, (slot + 1) * entries)
-        grad_kv[rows, D:] = (grad_normed[rows, :] * grad_attended).astype(jnp.bfloat16)
+        store_kv(1, slot, grad_normed[rows, :] * grad_attended)
         grad_normed[rows, :] = grad_attended * keys[rows, D:]
     for begin in range(0, wholes, tall):
         rows = slice(begin, begin + tall)
@@ -1917,12 +2070,14 @@
         rows = slice(slot * entries, (slot + 1) * entries)
         push = grad_normed[rows, :]
         grad_query = grad_query + push * keys[rows, 0:D]
-        grad_kv[rows, 0:D] = (push * query).astype(jnp.bfloat16)
+        store_kv(0, slot, push * query)
     query_bf = grad_query.astype(jnp.bfloat16)
 
     grad_q = dot_tn(query_bf, normed[0:entries, :])
-    grad_k = dot_tn(grad_kv[:, 0:D], normed[...])
-    grad_v = dot_tn(grad_kv[:, D:], normed[...])
+    grad_keys = grad_kv[0].reshape(wholes, D)
+    grad_values = grad_kv[1].reshape(wholes, D)
+    grad_k = dot_tn(grad_keys, normed[...])
+    grad_v = dot_tn(grad_values, normed[...])
     third = D * 3 // PLANES
     every = jnp.concatenate([grad_q, grad_k, grad_v], axis=0)
     for block in range(PLANES):
@@ -1930,7 +2085,9 @@
 
     for begin in range(0, wholes, tall):
         rows = slice(begin, begin + tall)
-        grad_normed[rows, :] = plain_dot(grad_kv[rows, :], weight_rows(qkv_at, 48)[D:, :])
+        grad_normed[rows, :] = plain_dot(
+            grad_keys[rows, :], weight_rows(qkv_at, 48)[D : 2 * D, :]
+        ) + plain_dot(grad_values[rows, :], weight_rows(qkv_at, 48)[2 * D :, :])
 
     grad_normed[0:entries, :] += plain_dot(query_bf, weight_rows(qkv_at, 48)[0:D, :])
 
@@ -1974,7 +2131,7 @@
         layer_kernel,
         out_shape=(
             jax.ShapeDtypeStruct((entries, D), bf),
-            jax.ShapeDtypeStruct((CORES, CHUNKS, CHIPS, PLANES, CHUNK, D), bf),
+            jax.ShapeDtypeStruct((CORES, CHUNKS, SIDE, SIDE, PLANES, CHUNK, D), bf),
             jax.ShapeDtypeStruct((count * cap, D), bf),
             jax.ShapeDtypeStruct((CORES * VROWS, D), f32),
             jax.ShapeDtypeStruct((count, entries, features), bf),
@@ -1984,14 +2141,15 @@
         in_specs=[hbm] + [vmem] * 7,
         out_specs=(vmem,) * 7,
         scratch_shapes=[
-            pltpu.VMEM((PART, D), f32),
+            pltpu.VMEM((MAIN, D), f32),
             pltpu.VMEM((count,) + pieces.shape, jnp.int32),
             pltpu.VMEM((SLOTS, entries), jnp.int32),
             pltpu.VMEM((count, entries * PSLOTS), f32),
             pltpu.VMEM((count, entries * PSLOTS), f32),
             pltpu.VMEM((count * cap, D), bf),
-            pltpu.VMEM((count, entries, features), bf),
-            pltpu.VMEM((PLANES, CHIPS * CORES, PART, D), bf),
+            pltpu.VMEM((PLANES * features, D), f32),
+            pltpu.VMEM((PLANES, features, D), bf),
+            pltpu.VMEM((PLANES, CHIPS * CORES, MAIN, D), bf),
             pltpu.VMEM((count * entries // BANDS, BANDS * features), f32),
             pltpu.VMEM((count * cap, entries * PSLOTS), bf),
             pltpu.VMEM((rows, D), f32),
@@ -1999,17 +2157,20 @@
             pltpu.VMEM((rows, D), bf),
             pltpu.VMEM((rows, 2 * D), f32),
             pltpu.VMEM((rows, 128), f32),
-            pltpu.VMEM((rows, 2 * D), bf),
+            pltpu.VMEM((2, SIDE, SIDE, PLANES, CHUNK, D), bf),
             pltpu.VMEM((rows, D), f32),
             pltpu.VMEM((entries * PSLOTS, D), bf),
             pltpu.VMEM((entries, FF), bf),
             pltpu.VMEM((entries, FF), f32),
             pltpu.VMEM((rows, 128), f32),
             pltpu.VMEM((8, D), f32),
-            dma((6,)),
+            dma((5,)),
         ]
-        + [dma((count - 1,))] * 6
-        + [dma((spread_count,))] * 4,
+        + sum_scratch(entries // CHUNK)
+        + [dma((count - 1,))] * 4
+        + [dma((entries // CHUNK,))] * 2
+        + [dma((spread_count,))] * 2
+        + [dma((PLANES - 1,))] * 2,
         compiler_params=pltpu.CompilerParams(
             collective_id=5, has_side_effects=True, vmem_limit_bytes=63 * 2**20
         ),

time: 330 us -> 325 us (0.985)
  Pallas kernels: 297 us -> 291 us
    pallas_call x1, Pallas kernels: 131 us -> 111 us  [layer(): pl.pallas_call(layer_kernel, out_shape=(jax.ShapeDtypeStruct((entries, D)...]
    pallas_call x1, Pallas kernels: 110 us -> 121 us  [settle(): pl.pallas_call(settle_kernel, out_shape=(jax.ShapeDtypeStruct((features,...]
    unnamed x31 -> x27, local copies, waits for them, and re-layouts: 14.7 us -> 14.1 us
  transfers between devices with their start and end apart: 1 -> 1, of which waited for: 0 -> 0; matrix products, arithmetic and copies ran while one was open for 1% -> 1% of each run, Pallas kernels for 16% -> 17%
where the time goes in v5:
time: 325 us; the launch traced here: 319 us
  Pallas kernels  291 us (90%)
  local copies, waits for them, and re-layouts  18.4 us (6%)
  starting transfers between devices  6.5 us (2%)
    pallas_call x1, Pallas kernels, settle(): pl.pallas_call(settle_kernel, out_shape=(jax.ShapeDtypeStruct((features,...  121 us
    pallas_call x1, Pallas kernels, layer(): pl.pallas_call(layer_kernel, out_shape=(jax.ShapeDtypeStruct((entries, D)...  111 us
    pallas_call x1, Pallas kernels, muon_rows(): pl.pallas_call(muon_kernel, out_shape=jax.ShapeDtypeStruct((total, D), jn...  47.1 us
    unnamed x27, local copies, waits for them, and re-layouts  14.1 us
    pallas_call x1, Pallas kernels, finish(): pl.pallas_call(finish_kernel, grid=((MAIN_TILES + MOST_TILES) // tall,),...  7.58 us
    all_to_all x1, starting transfers between devices, on_device(): lax.all_to_all(grad_outgoing.reshape(device_count, cap, D), BOTH, 0, 0, t...  6.5 us
  transfers between devices with their start and end apart: 1, of which 0 were waited for; matrix products, arithmetic and copies ran while one was open for 1% of the time, Pallas kernels for 17%

profile of v5, /device:TPU:31, one launch (start us, length us, event | category | flops | bytes accessed | tf_op | source)
XLA Modules:
  0.0 318.9 jit_solution(8505501940080491239)
XLA Ops:
  0.6 1.5 reshape.43.param_ref
  2.1 0.7 slice.6
  2.8 1.4 copy.26.live_ref
  4.2 1.3 pad.4.pieces_ref
  5.5 0.1 dynamic-slice_bitcast_fusion
  5.6 0.7 copy.27.bias_ref
  6.3 111.2 %layer.1 = (bf16[128,512]{1,0:T(8,128)(2,1)}, bf16[2,3,2,2,4,64,512]{6,5,4,3,2,1,0:T(8,128)(2,1)}, bf16[2048,512]{1,0:T(8,128)(2,1)}, f32[32,512]{1,0:T(8,128)},...) custom-call(f32[2560,512]{1,0:T(8,128)} %bitcast.13, s32[8,128]{1,0:T(8,128)} %pad.4.pieces_ref, ...), custom_call_target="tpu_custom_call" | custom-call | tf_op jit(solution)/shard_map/layer/pallas_call | solution.py:2130
  117.6 121.2 %settle.1 = (f32[128,8192]{1,0:T(8,128)}, bf16[1536,512]{1,0:T(8,128)(2,1)}, bf16[2,4,4,32,512]{4,3,2,1,0:T(8,128)(2,1)}, f32[2,16,512]{2,1,0:T(8,128)}, f32[512...) custom-call(bf16[128,512]{1,0:T(8,128)(2,1)} %get-tuple-element.30.z_ref, ...), custom_call_target="tpu_custom_call" | custom-call | tf_op jit(solution)/shard_map/settle/pallas_call | solution.py:1151
  238.7 0.0 copy-start.8
  238.8 0.0 copy-start.5
  238.8 6.5 %all-to-all-start = ((bf16[32,64,512]{2,1,0:T(8,128)(2,1)}), bf16[32,64,512]{2,1,0:T(8,128)(2,1)S(1)}, u32[]{:S(2)}, u32[]{:S(2)}) async-start(bf16[32,64,512]{2,1,0:T(8,128)(2,1)} %bitcast.17), calls=%async_computation | async-start | bytes 4194304 | tf_op jit(solution)/shard_map/all_to_all | solution.py:2253
  245.3 1.6 reduce
  246.9 47.1 %muon_rows.1.rows_ref = bf16[2560,512]{1,0:T(8,128)(2,1)} custom-call(f32[512,512]{1,0:T(8,128)} %get-tuple-element.38.gram_ref, bf16[1024,512]{1,0:T(8,128)(2,1)} %get-tuple-element.42.high_ref, bf16[1024,512]{1,0:T(8,128)(2,1)} %get-tuple-element.43.low_ref), custom_call_target="tpu_custom_call" | custom-call | tf_op jit(solution)/shard_map/muon_rows/pallas_call | solution.py:1396
  294.0 0.0 copy-start
  294.0 2.5 copy-done
  296.5 2.5 copy-done.1
  299.0 1.7 copy-done.2
  300.7 2.5 copy-done.3
  303.2 1.4 copy-done.4
  304.6 7.6 %finish.1 = (f32[1,2560,512]{2,1,0:T(8,128)}, f32[1,2560,512]{2,1,0:T(8,128)}, f32[1,2560,512]{2,1,0:T(8,128)}, f32[1,2560,512]{2,1,0:T(8,128)}) custom-call(bf16[1536,512]{1,0:T(8,128)(2,1)S(1)} %copy-done.4, bf16[8,4,32,512]{3,2,1,0:T(8,128)(2,1)S(1)} %bitcast.15, bf16[2560,512]{1,0:T(8,128)(2,1)S(1)} %copy-done.2, f32[1,2560,512]{2,1,0:T(8,128)S(1)} %copy-done, ...), custom_call_target="tpu_custom_call" | custom-call | flops 15728640 | bytes 41943040 | tf_op jit(solution)/shard_map/finish/pallas_call | solution.py:1448
  312.2 0.7 multiply_add_fusion
  313.0 0.0 all-to-all-done
  313.0 3.7 %add_piece_grads.1 = f32[1024,512]{1,0:T(8,128)} custom-call(s32[1,2048]{1,0:T(1,128)S(1)} %bitcast.16, bf16[2048,512]{1,0:T(8,128)(2,1)S(1)} %bitcast.14), custom_call_target="tpu_custom_call" | custom-call | tf_op jit(solution)/shard_map/add_piece_grads/pallas_call | solution.py:2190
  316.7 2.0 copy.30
  (17 shorter events, 0.0 us)
Async XLA Ops:
  238.7 8.1 %copy-start.8 = (f32[2,16,512]{2,1,0:T(8,128)S(1)}, f32[2,16,512]{2,1,0:T(8,128)}, u32[]{:S(2)}) copy-start(f32[2,16,512]{2,1,0:T(8,128)} %get-tuple-element.48) | copy-start | bytes 196612
  238.8 55.3 %copy-start.5 = (bf16[2,4,4,32,512]{4,3,2,1,0:T(8,128)(2,1)S(1)}, bf16[2,4,4,32,512]{4,3,2,1,0:T(8,128)(2,1)}, u32[]{:S(2)}) copy-start(bf16[2,4,4,32,512]{4,3,2,1,0:T(8,128)(2,1)} %get-tuple-element.41) | copy-start | bytes 3145732
  238.8 74.2 %all-to-all-start = ((bf16[32,64,512]{2,1,0:T(8,128)(2,1)}), bf16[32,64,512]{2,1,0:T(8,128)(2,1)S(1)}, u32[]{:S(2)}, u32[]{:S(2)}) async-start(bf16[32,64,512]{2,1,0:T(8,128)(2,1)} %bitcast.17), calls=%async_computation | async-start | bytes 4194304 | tf_op jit(solution)/shard_map/all_to_all | solution.py:2253
  294.0 2.5 copy-start
  296.5 2.5 copy-start.1
  299.0 1.7 copy-start.2
  300.7 2.5 copy-start.3
  303.2 1.4 copy-start.4
  304.6 7.6 %copy-start.7 = (f32[14336]{0:T(1024)S(1)}, f32[14336]{0:T(1024)}, u32[]{:S(2)}) copy-start(f32[14336]{0:T(1024)} %param.22) | copy-start | bytes 172036
  304.6 7.6 %copy-start.9 = (f32[14336]{0:T(1024)S(1)}, f32[14336]{0:T(1024)}, u32[]{:S(2)}) copy-start(f32[14336]{0:T(1024)} %param.25) | copy-start | bytes 172036
  304.6 7.6 %copy-start.10 = (f32[14336]{0:T(1024)S(1)}, f32[14336]{0:T(1024)}, u32[]{:S(2)}) copy-start(f32[14336]{0:T(1024)} %param.24) | copy-start | bytes 172036
  304.6 7.6 %copy-start.11 = (f32[14336]{0:T(1024)S(1)}, f32[14336]{0:T(1024)}, u32[]{:S(2)}) copy-start(f32[14336]{0:T(1024)} %param.23) | copy-start | bytes 172036
  313.0 3.7 %copy-start.6 = (f32[128,8192]{1,0:T(8,128)S(1)}, f32[128,8192]{1,0:T(8,128)}, u32[]{:S(2)}) copy-start(f32[128,8192]{1,0:T(8,128)} %get-tuple-element.65) | copy-start | bytes 12582916

commit v6 on v5

--- a/solution.py
+++ b/solution.py
@@ -632,9 +632,15 @@
     return begin, arrive, relay, finish, settled
 
 
+SHARES = ((6, 0, 0, 384), (7, 0, 384, 128), (2, 0, 512, 512), (4, 0, 1024, 512)) + (
+    (0, 0, 1536, 512),
+    (0, 512, 2048, 512),
+)
+
+
 def settle_kernel(
-    z_ref,
-    main_ref,
+    every,
+    part,
     vec_ref,
     grad_ref,
     proj_ref,
@@ -642,27 +648,25 @@
     momentum_ref,
     ids_ref,
     mask_ref,
+    outgoing_ref,
     text_ref,
     sum_ref,
     proj_sum_ref,
     vec_out_ref,
+    rows_ref,
+    incoming_ref,
     gram_ref,
     high_ref,
     low_ref,
-    every,
+    poly,
+    chain,
+    chain_high,
+    chain_low,
+    rows_out,
     table_ref,
     text_tiles,
-    near,
-    first,
-    x_first,
-    y_first,
-    x_second,
-    y_second,
-    second,
-    deep,
     proj_own,
     proj_far,
-    part,
     proj_part,
     vec_near,
     vec_far,
@@ -676,14 +680,6 @@
     local_sem,
     tile_sem,
     text_sem,
-    z_send,
-    z_recv,
-    main_send,
-    main_recv,
-    far_send,
-    far_recv,
-    deep_send,
-    deep_recv,
     done_send,
     done_recv,
     pass_send,
@@ -694,6 +690,11 @@
     vec_recv,
     gram_send,
     gram_recv,
+    share_sem,
+    rows_send,
+    rows_recv,
+    piece_send,
+    piece_recv,
 ):
     wide_at, plane, chip, core = place()
     sibling, chips, planes = neighbours(wide_at, plane, chip, core)
@@ -705,9 +706,6 @@
     y_at = chip // SIDE
     tile_count, tile_first = owner_tiles(wide_at)
 
-    own_main = pltpu.make_async_copy(main_ref.at[core], first, local_sem.at[0])
-    own_main.start()
-
     def momentum_load(tile):
         source = pl.ds(pl.multiple_of((tile_first + tile) * TILE, TILE), TILE)
         return pltpu.make_async_copy(
@@ -718,23 +716,40 @@
     def _(tile):
         momentum_load(tile).start()
 
-    enter([sibling] + chips + planes)
+    wide_count = CHIPS * CORES
+    peers = [
+        (lax.rem(wide_at + k // PLANES, wide_count), lax.rem(plane + k % PLANES, PLANES))
+        for k in range(1, wide_count * PLANES)
+    ]
+    enter(peers)
+    me = wide_at * PLANES + plane
+    cap = outgoing_ref.shape[0] // (wide_count * PLANES)
+
+    def piece_rows(device):
+        return pl.ds(pl.multiple_of(device * cap, cap), cap)
+
+    def piece_copy(index):
+        wide_to, plane_to = peers[index]
+        return remote(
+            outgoing_ref.at[piece_rows(wide_to * PLANES + plane_to)],
+            incoming_ref.at[piece_rows(me)],
+            (piece_send, piece_recv),
+            index,
+            (wide_to, plane_to),
+        )
+
+    def send_pieces(begin, end):
+        for index in range(begin, end):
+            piece_copy(index).start()
+
+    own_pieces = pltpu.make_async_copy(
+        outgoing_ref.at[piece_rows(me)], incoming_ref.at[piece_rows(me)], local_sem.at[7]
+    )
+    own_pieces.start()
 
     vec_sems = (vec_send, vec_recv)
     vec_copies = [remote(vec_ref.at[other], vec_near, vec_sems, 0, sibling)]
     vec_copies[0].start()
-    z_begin, z_arrive, z_relay, z_finish, z_settled = spread_steps(
-        z_ref, every, (z_send, z_recv), 0, place()
-    )
-    own_z = pltpu.make_async_copy(z_ref, every.at[plane, wide_at], local_sem.at[1])
-    own_z.start()
-    main_sems = (main_send, main_recv)
-    near_copies = []
-    for chunk in range(CHUNKS):
-        copy = remote(main_ref.at[other, chunk], near.at[chunk], main_sems, chunk, sibling)
-        copy.start()
-        near_copies.append(copy)
-
     def vec_far_step():
         vec_copies[0].wait_recv()
         vec_far[chip] = vec_ref[core] + vec_near[...]
@@ -759,94 +774,6 @@
         copy = remote(vec_out_ref.at[core], vec_out_ref.at[core], vec_sems, 7, sibling)
         copy.start()
         vec_copies.append(copy)
-
-    far_sems = (far_send, far_recv)
-    lows, highs = pl.ds(0, 2), pl.ds(2, 2)
-    firsts = []
-
-    def first_step(chunk):
-        near_copies[chunk].wait_recv()
-
-        @pl.loop(0, CHIPS * PLANES)
-        def _(step):
-            y, x, m = step // (SIDE * PLANES), lax.rem(step // PLANES, SIDE), lax.rem(step, PLANES)
-            first[chunk, y, x, m] = (
-                first[chunk, y, x, m].astype(jnp.float32)
-                + near[chunk, y, x, m].astype(jnp.float32)
-            ).astype(jnp.bfloat16)
-
-        by_x = remote(
-            first.at[chunk, :, 1 - x_at, lows], x_first.at[chunk], far_sems, chunk * 4, x_near
-        )
-        by_y = remote(
-            first.at[chunk, 1 - y_at, :, highs], y_first.at[chunk], far_sems, chunk * 4 + 1, y_near
-        )
-        by_x.start()
-        by_y.start()
-        firsts.append((by_x, by_y))
-
-    seconds = []
-
-    def second_step(chunk):
-        by_x, by_y = firsts[chunk]
-        by_x.wait_recv()
-        for y in range(SIDE):
-            for m in range(2):
-                first[chunk, y, x_at, m] = (
-                    first[chunk, y, x_at, m].astype(jnp.float32)
-                    + x_first[chunk, y, m].astype(jnp.float32)
-                ).astype(jnp.bfloat16)
-        next_y = remote(
-            first.at[chunk, 1 - y_at, x_at, lows],
-            y_second.at[chunk],
-            far_sems,
-            chunk * 4 + 2,
-            y_near,
-        )
-        next_y.start()
-        by_y.wait_recv()
-        for x in range(SIDE):
-            for m in range(2):
-                first[chunk, y_at, x, 2 + m] = (
-                    first[chunk, y_at, x, 2 + m].astype(jnp.float32)
-                    + y_first[chunk, x, m].astype(jnp.float32)
-                ).astype(jnp.bfloat16)
-        next_x = remote(
-            first.at[chunk, y_at, 1 - x_at, highs],
-            x_second.at[chunk],
-            far_sems,
-            chunk * 4 + 3,
-            x_near,
-        )
-        next_x.start()
-        seconds.append((next_y, next_x))
-
-    deep_sems = (deep_send, deep_recv)
-    deep_copies = []
-
-    def deep_step(chunk):
-        next_y, next_x = seconds[chunk]
-        next_y.wait_recv()
-        for m in range(2):
-            second[chunk, m] = (
-                first[chunk, y_at, x_at, m].astype(jnp.float32)
-                + y_second[chunk, m].astype(jnp.float32)
-            ).astype(jnp.bfloat16)
-        next_x.wait_recv()
-        for m in range(2):
-            second[chunk, 2 + m] = (
-                first[chunk, y_at, x_at, 2 + m].astype(jnp.float32)
-                + x_second[chunk, m].astype(jnp.float32)
-            ).astype(jnp.bfloat16)
-        copies = []
-        for k, target in enumerate(planes):
-            to_plane = lax.rem(plane + k + 1, PLANES)
-            copy = remote(
-                second.at[chunk, to_plane], deep.at[chunk, k], deep_sems, chunk * 3 + k, target
-            )
-            copy.start()
-            copies.append(copy)
-        deep_copies.append(copies)
 
     count = every.shape[2]
     features = proj_ref.shape[0]
@@ -885,8 +812,8 @@
 
     done_sems = (done_send, done_recv)
     pass_sems = (pass_send, pass_recv)
-    done_copies = []
-    locals_done = []
+    done_copies = {}
+    locals_done = {}
 
     def natural(index, wide):
         _, size, base = PIECES[index]
@@ -901,25 +828,20 @@
             copy = remote(src, spot, done_sems, index * 4 + k, target)
             copy.start()
             copies.append(copy)
-        done_copies.append(copies)
+        done_copies[index] = copies
         copy = pltpu.make_async_copy(src, spot, local_sem.at[2 + index])
         copy.start()
-        locals_done.append(copy)
+        locals_done[index] = copy
 
     def publish_step(chunk):
-        for copy in deep_copies[chunk]:
-            copy.wait_recv()
-        value = second[chunk, plane].astype(jnp.float32)
-        for k in range(3):
-            value = value + deep[chunk, k].astype(jnp.float32)
-        part[chunk * CHUNK : (chunk + 1) * CHUNK, :] = value.astype(jnp.bfloat16)
         for index, (offset, size, _) in enumerate(PIECES):
             if offset // CHUNK == chunk:
                 publish(index, part.at[pl.ds(offset, size)], natural(index, wide_at))
 
-    pass_copies = []
+    pass_copies = {}
 
     def pass_step(index):
+        pass_copies[index] = []
         for k in range(3):
             done_copies[index][1 + k].wait_recv()
             from_chip = lax.rem(chip + CHIPS - 1 - k, CHIPS)
@@ -929,7 +851,7 @@
                 spot = proj_natural(from_chip, core)
             copy = remote(spot, spot, pass_sems, index * 3 + k, sibling)
             copy.start()
-            pass_copies.append(copy)
+            pass_copies[index].append(copy)
 
     def table_step():
         for block in range(PLANES * wide_count):
@@ -968,48 +890,11 @@
             text_tiles[lax.rem(step, 2)] = total
             text_copy(step).start()
 
-    own_main.wait()
-    z_begin()
-    first_step(0)
-    vec_far_step()
-    first_step(1)
-    z_arrive(1)
-    first_step(2)
-    z_relay(0)
-    z_arrive(2)
-    second_step(0)
-    z_relay(1)
-    z_arrive(3)
-    second_step(1)
-    z_finish(0)
-    z_relay(2)
-    second_step(2)
-    deep_step(0)
-    z_finish(1)
-    z_relay(3)
-    deep_step(1)
-    z_finish(2)
-    z_finish(3)
-    deep_step(2)
-    own_z.wait()
-    z_settled()
-    proj_near_step()
-    vec_deep_step()
-    publish_step(0)
-    publish_step(1)
-    proj_far_step()
-    publish_step(2)
-    table_step()
-    vec_last_step()
-    publish_proj()
-    for index in range(len(PIECES) + 1):
-        pass_step(index)
-    for copies in done_copies:
-        copies[0].wait_recv()
-    for copy in pass_copies:
-        copy.wait_recv()
-    for copy in locals_done:
-        copy.wait()
+    def settle_piece(index):
+        done_copies[index][0].wait_recv()
+        for copy in pass_copies[index]:
+            copy.wait_recv()
+        locals_done[index].wait()
 
     gram_sems = (gram_send, gram_recv)
 
@@ -1022,8 +907,10 @@
         high_ref[rows, :] = high
         low_ref[rows, :] = low
 
-    @pl.when(wide_at == OWNERS[4])
-    def _():
+    early = (wide_at == OWNERS[0]) | (wide_at == OWNERS[1])
+    late = (tile_count > 0) & jnp.logical_not(early)
+
+    def proj_tiles_step():
         loads = [
             pltpu.make_async_copy(
                 proj_sum_ref.at[tile // PLANES, tile % PLANES],
@@ -1041,8 +928,7 @@
         def _(tile):
             add_tile(tile, proj_tiles[tile].reshape(TILE, D))
 
-    @pl.when((tile_count > 0) & (wide_at != OWNERS[4]))
-    def _():
+    def main_tiles_step():
         def load(tile):
             source = pl.ds(pl.multiple_of((tile_first + tile) * TILE, TILE), TILE)
             return pltpu.make_async_copy(
@@ -1058,13 +944,10 @@
             load(tile).wait()
             add_tile(tile, main_tiles[tile])
 
-    for count_here in sorted(set(BLOCK_TILES)):
-
-        @pl.when(tile_count == count_here)
-        def _(count_here=count_here):
-            high = high_ref[0 : count_here * TILE, :]
-            cross = dot_tn(high, low_ref[0 : count_here * TILE, :])
-            gram_ref[...] = dot_tn(high, high) + (cross + cross.T)
+    def gram_product(count_here):
+        high = high_ref[0 : count_here * TILE, :]
+        cross = dot_tn(high, low_ref[0 : count_here * TILE, :])
+        gram_ref[...] = dot_tn(high, high) + (cross + cross.T)
 
     def gram_copies(first_index):
         copies = []
@@ -1077,10 +960,7 @@
             copies.append(remote(src, dst, gram_sems, first_index + k, target))
         return copies
 
-    owning = tile_count > 0
-
-    @pl.when(owning)
-    def _():
+    def gram_send_step():
         for t in range(PLANES):
             for strip, lane in ((t, 0), (STRIPS - 1 - t, 1)):
                 begin = strip // 2 * TILE
@@ -1092,178 +972,73 @@
             copy.start()
         pieces[plane] = packs[plane]
 
-    text_steps(0, text_count // 2)
-
-    @pl.when(owning)
-    def _():
-        for copy in gram_copies(0):
-            copy.wait()
-        totals[plane] = (pieces[0] + pieces[1]) + (pieces[2] + pieces[3])
-        for copy in gram_copies(3):
-            copy.start()
-
-    text_steps(text_count // 2, text_count)
-
-    @pl.when(owning)
-    def _():
-        for copy in gram_copies(3):
-            copy.wait()
-        for t in range(PLANES):
-            for strip, lane in ((t, 0), (STRIPS - 1 - t, 1)):
-                begin = strip // 2 * TILE
-                width = D - begin
-                at = 0 if lane == 0 else PACKED - width
-                gram_ref[strip * STRIP : (strip + 1) * STRIP, begin:] = totals[
-                    t, :, at : at + width
-                ]
-        row_block = lax.broadcasted_iota(jnp.int32, (D, D), 0) // TILE
-        lane_block = lax.broadcasted_iota(jnp.int32, (D, D), 1) // TILE
-        value = gram_ref[...]
-        gram_ref[...] = jnp.where(lane_block >= row_block, value, value.T)
-
-    for copies in done_copies:
-        for copy in copies:
-            copy.wait_send()
-    for copy in pass_copies:
-        copy.wait_send()
-    for copy in near_copies:
-        copy.wait_send()
-    for pair in firsts + seconds:
-        for copy in pair:
-            copy.wait_send()
-    for copies in deep_copies:
-        for copy in copies:
-            copy.wait_send()
-    vec_copies[0].wait_send()
-    vec_copies[7].wait()
-    text_copy(text_count - 2).wait()
-    text_copy(text_count - 1).wait()
-
-
-def settle(z_own, main, vec, grad_own, proj_own, bias_own, momentum, text_ids, text_mask):
-    dma = pltpu.SemaphoreType.DMA
-    f32, bf = jnp.float32, jnp.bfloat16
-    features, tokens = proj_own.shape[0], text_ids.size
-    rows = grad_own.shape[0] * grad_own.shape[1] // BANDS
-    hbm = pl.BlockSpec(memory_space=pl.ANY)
-    vmem = pl.BlockSpec(memory_space=pltpu.VMEM)
-    grid = (CHUNKS, SIDE, SIDE, PLANES, CHUNK, D)
-    return pl.pallas_call(
-        settle_kernel,
-        out_shape=(
-            jax.ShapeDtypeStruct((features, tokens), f32),
-            jax.ShapeDtypeStruct((MAIN_TILES * TILE, D), bf),
-            jax.ShapeDtypeStruct((CORES, PLANES, CHIPS, PROJ, D), bf),
-            jax.ShapeDtypeStruct((CORES, VROWS, D), f32),
-            jax.ShapeDtypeStruct((D, D), f32),
-            jax.ShapeDtypeStruct((MOST_TILES * TILE, D), bf),
-            jax.ShapeDtypeStruct((MOST_TILES * TILE, D), bf),
-        ),
-        in_specs=[vmem, hbm, vmem, vmem, vmem, vmem, hbm, vmem, vmem],
-        out_specs=(hbm, hbm, hbm, vmem, vmem, vmem, vmem),
-        scratch_shapes=[
-            pltpu.VMEM((PLANES, CHIPS * CORES) + z_own.shape, bf),
-            pltpu.VMEM((BANDS * features, rows), bf),
-            pltpu.VMEM((2, features, TEXT_TILE), f32),
-            pltpu.VMEM(grid, bf),
-            pltpu.VMEM(grid, bf),
-            pltpu.VMEM((CHUNKS, SIDE, 2, CHUNK, D), bf),
-            pltpu.VMEM((CHUNKS, SIDE, 2, CHUNK, D), bf),
-            pltpu.VMEM((CHUNKS, 2, CHUNK, D), bf),
-            pltpu.VMEM((CHUNKS, 2, CHUNK, D), bf),
-            pltpu.VMEM((CHUNKS, PLANES, CHUNK, D), bf),
-            pltpu.VMEM((CHUNKS, 3, CHUNK, D), bf),
-            pltpu.VMEM((CHIPS, PROJ, D), bf),
-            pltpu.VMEM((CHIPS, PROJ, D), bf),
-            pltpu.VMEM((MAIN, D), bf),
-            pltpu.VMEM((PLANES, PROJ, D), bf),
-            pltpu.VMEM((VROWS, D), f32),
-            pltpu.VMEM((CHIPS, VROWS, D), f32),
-            pltpu.VMEM((PLANES, VROWS, D), f32),
-            pltpu.VMEM((4, TILE, D), bf),
-            pltpu.VMEM((MOST_TILES, CHIPS, PROJ, D), bf),
-            pltpu.VMEM((MOST_TILES, TILE, D), f32),
-            pltpu.VMEM((PLANES, STRIP, PACKED), f32),
-            pltpu.VMEM((PLANES, STRIP, PACKED), f32),
-            pltpu.VMEM((PLANES, STRIP, PACKED), f32),
-            dma((8,)),
-            dma((2, MOST_TILES)),
-            dma((2,)),
-            dma((6 + 9 * PLANES,)),
-            dma((6 + 9 * PLANES,)),
-            dma((CHUNKS,)),
-            dma((CHUNKS,)),
-            dma((CHUNKS * 4,)),
-            dma((CHUNKS * 4,)),
-            dma((CHUNKS * 3,)),
-            dma((CHUNKS * 3,)),
-            dma((20,)),
-            dma((20,)),
-            dma((15,)),
-            dma((15,)),
-            dma((6,)),
-            dma((6,)),
-            dma((8,)),
-            dma((8,)),
-            dma((6,)),
-            dma((6,)),
-        ],
-        compiler_params=pltpu.CompilerParams(
-            collective_id=3, has_side_effects=True, vmem_limit_bytes=58 * 2**20
-        ),
-        name="settle",
-    )(
-        z_own,
-        main.reshape((CORES,) + grid),
-        vec,
-        grad_own,
-        proj_own,
-        bias_own,
-        momentum,
-        text_ids,
-        text_mask,
-    )
-
-
-SHARES = ((6, 0, 0, 384), (7, 0, 384, 128), (2, 0, 512, 512), (4, 0, 1024, 512)) + (
-    (0, 0, 1536, 512),
-    (0, 512, 2048, 512),
-)
-
-
-def muon_kernel(
-    gram_ref,
-    high_ref,
-    low_ref,
-    out_ref,
-    gram,
-    poly,
-    chain,
-    chain_high,
-    chain_low,
-    rows_out,
-    local_sem,
-    rows_send,
-    rows_recv,
-):
-    wide_at, plane, chip, core = place()
-    sibling, chips, planes = neighbours(wide_at, plane, chip, core)
-    x_wide, y_wide = across(wide_at, plane, chip, core)
-    x_near, y_near = (x_wide, plane), (y_wide, plane)
-    tile_count, _ = owner_tiles(wide_at)
-    enter([sibling, x_near, y_near])
-
-    @pl.when(tile_count > 0)
-    def _():
+    def gram_early_step():
+        @pl.when(early)
+        def _():
+            main_tiles_step()
+
+        for owner, count_here in zip(OWNERS[:2], BLOCK_TILES[:2]):
+
+            @pl.when(wide_at == owner)
+            def _(count_here=count_here):
+                gram_product(count_here)
+
+        @pl.when(early)
+        def _():
+            gram_send_step()
+
+    def gram_late_step():
+        @pl.when(wide_at == OWNERS[4])
+        def _():
+            proj_tiles_step()
+            gram_product(BLOCK_TILES[4])
+
+        @pl.when(late & (wide_at != OWNERS[4]))
+        def _():
+            main_tiles_step()
+            gram_product(BLOCK_TILES[3])
+
+        @pl.when(late)
+        def _():
+            gram_send_step()
+
+    def gram_total_step(here):
+        @pl.when(here)
+        def _():
+            for copy in gram_copies(0):
+                copy.wait()
+            totals[plane] = (pieces[0] + pieces[1]) + (pieces[2] + pieces[3])
+            for copy in gram_copies(3):
+                copy.start()
+
+    def gram_whole_step():
+        @pl.when(tile_count > 0)
+        def _():
+            for copy in gram_copies(3):
+                copy.wait()
+            for t in range(PLANES):
+                for strip, lane in ((t, 0), (STRIPS - 1 - t, 1)):
+                    begin = strip // 2 * TILE
+                    width = D - begin
+                    at = 0 if lane == 0 else PACKED - width
+                    gram_ref[strip * STRIP : (strip + 1) * STRIP, begin:] = totals[
+                        t, :, at : at + width
+                    ]
+            row_block = lax.broadcasted_iota(jnp.int32, (D, D), 0) // TILE
+            lane_block = lax.broadcasted_iota(jnp.int32, (D, D), 1) // TILE
+            value = gram_ref[...]
+            gram_ref[...] = jnp.where(lane_block >= row_block, value, value.T)
+
+    def chain_step():
         diagonal = lax.broadcasted_iota(jnp.int32, (D, D), 0) == lax.broadcasted_iota(
             jnp.int32, (D, D), 1
         )
         square = jnp.sum(jnp.where(diagonal, gram_ref[...], 0.0))
         inverse = 1.0 / (jnp.sqrt(jnp.full((1, 1), square)) + 1e-07)
-        gram[...] = gram_ref[...] * (inverse * inverse)
+        gram_ref[...] = gram_ref[...] * (inverse * inverse)
 
         def make_poly():
-            value = gram[...]
+            value = gram_ref[...]
             parts = halves(value)
             diagonal = lax.broadcasted_iota(jnp.int32, (D, D), 0) == lax.broadcasted_iota(
                 jnp.int32, (D, D), 1
@@ -1276,8 +1051,8 @@
 
         def next_gram():
             parts = halves(poly[...])
-            half_way = split_dot(halves(gram[...]), parts)
-            gram[...] = split_dot(halves(half_way), parts)
+            half_way = split_dot(halves(gram_ref[...]), parts)
+            gram_ref[...] = split_dot(halves(half_way), parts)
 
         def extend():
             chain[...] = split_dot(halves(chain[...]), halves(poly[...]))
@@ -1298,15 +1073,47 @@
         chain_high[...] = high
         chain_low[...] = low
 
-    sems = (rows_send, rows_recv)
+    proj_near_step()
+    publish_step(2)
+    publish_step(0)
+    publish_step(1)
+    vec_far_step()
+    pass_step(2)
+    pass_step(3)
+    proj_far_step()
+    pass_step(0)
+    pass_step(1)
+    vec_deep_step()
+    table_step()
+    settle_piece(2)
+    settle_piece(3)
+    publish_proj()
+    gram_early_step()
+    vec_last_step()
+    settle_piece(0)
+    settle_piece(1)
+    pass_step(4)
+    settle_piece(4)
+    gram_late_step()
+    text_steps(0, text_count // 2)
+    gram_total_step(tile_count > 0)
+    text_steps(text_count // 2, text_count)
+    gram_whole_step()
+    send_pieces(0, len(peers))
+    @pl.when(tile_count > 0)
+    def _():
+        chain_step()
+
+
+    share_sems = (rows_send, rows_recv)
 
     def share_copies(index):
         owner, source, begin, size = SHARES[index]
         owner_chip, owner_core = divmod(owner, CORES)
         mine = rows_out.at[pl.ds(source, size)]
-        spot = out_ref.at[pl.ds(begin, size)]
-        first = out_ref.at[pl.ds(begin, size // 2)]
-        last = out_ref.at[pl.ds(begin + size // 2, size // 2)]
+        spot = rows_ref.at[pl.ds(begin, size)]
+        first = rows_ref.at[pl.ds(begin, size // 2)]
+        last = rows_ref.at[pl.ds(begin + size // 2, size // 2)]
         base = index * 9
         roles = {
             "x": (owner_chip ^ 1) * CORES + owner_core,
@@ -1336,16 +1143,16 @@
         for role in ("o", "x", "y", "d"):
             at = roles[role]
             roles["s" + role] = at // CORES * CORES + 1 - at % CORES
-        local = (mine, spot, local_sem.at[index])
+        local = (mine, spot, share_sem.at[index])
         return roles, sends, gets, local
 
     def started(entry):
         src, dst, index, target = entry
-        return remote(src, dst, sems, index, target)
+        return remote(src, dst, share_sems, index, target)
 
     def arriving(entry):
         spot, index = entry
-        return remote(spot, spot, sems, index, sibling)
+        return remote(spot, spot, share_sems, index, sibling)
 
     plans = [share_copies(index) for index in range(len(SHARES))]
     for (roles, sends, gets, local), (_, source, _, size) in zip(plans, SHARES):
@@ -1389,31 +1196,95 @@
                     pltpu.make_async_copy(*local).wait()
 
 
-def muon_rows(gram, high, low):
+    for copies in list(done_copies.values()) + list(pass_copies.values()):
+        for copy in copies:
+            copy.wait_send()
+    vec_copies[0].wait_send()
+    vec_copies[7].wait()
+    text_copy(text_count - 2).wait()
+    text_copy(text_count - 1).wait()
+    own_pieces.wait()
+    for index in range(len(peers)):
+        piece_copy(index).wait()
+
+
+def settle(every, part, vec, grad_own, proj_own, bias_own, momentum, text_ids, text_mask, outgoing):
     dma = pltpu.SemaphoreType.DMA
+    f32, bf = jnp.float32, jnp.bfloat16
+    features, tokens = proj_own.shape[0], text_ids.size
+    rows = grad_own.shape[0] * grad_own.shape[1] // BANDS
+    hbm = pl.BlockSpec(memory_space=pl.ANY)
     vmem = pl.BlockSpec(memory_space=pltpu.VMEM)
-    total = (MAIN_TILES + MOST_TILES) * TILE
     return pl.pallas_call(
-        muon_kernel,
-        out_shape=jax.ShapeDtypeStruct((total, D), jnp.bfloat16),
-        in_specs=[vmem] * 3,
-        out_specs=pl.BlockSpec(memory_space=pl.ANY),
+        settle_kernel,
+        out_shape=(
+            jax.ShapeDtypeStruct((features, tokens), f32),
+            jax.ShapeDtypeStruct((MAIN_TILES * TILE, D), bf),
+            jax.ShapeDtypeStruct((CORES, PLANES, CHIPS, PROJ, D), bf),
+            jax.ShapeDtypeStruct((CORES, VROWS, D), f32),
+            jax.ShapeDtypeStruct(((MAIN_TILES + MOST_TILES) * TILE, D), bf),
+            jax.ShapeDtypeStruct(outgoing.shape, bf),
+        ),
+        in_specs=[vmem, vmem, vmem, vmem, vmem, vmem, hbm, vmem, vmem, hbm],
+        out_specs=(hbm, hbm, hbm, vmem, hbm, hbm),
         scratch_shapes=[
-            pltpu.VMEM((D, D), jnp.float32),
-            pltpu.VMEM((D, D), jnp.float32),
-            pltpu.VMEM((D, D), jnp.float32),
-            pltpu.VMEM((D, D), jnp.bfloat16),
-            pltpu.VMEM((D, D), jnp.bfloat16),
-            pltpu.VMEM((MOST_TILES * TILE, D), jnp.bfloat16),
+            pltpu.VMEM((D, D), f32),
+            pltpu.VMEM((MOST_TILES * TILE, D), bf),
+            pltpu.VMEM((MOST_TILES * TILE, D), bf),
+            pltpu.VMEM((D, D), f32),
+            pltpu.VMEM((D, D), f32),
+            pltpu.VMEM((D, D), bf),
+            pltpu.VMEM((D, D), bf),
+            pltpu.VMEM((MOST_TILES * TILE, D), bf),
+            pltpu.VMEM((BANDS * features, rows), bf),
+            pltpu.VMEM((2, features, TEXT_TILE), f32),
+            pltpu.VMEM((CHIPS, PROJ, D), bf),
+            pltpu.VMEM((CHIPS, PROJ, D), bf),
+            pltpu.VMEM((PLANES, PROJ, D), bf),
+            pltpu.VMEM((VROWS, D), f32),
+            pltpu.VMEM((CHIPS, VROWS, D), f32),
+            pltpu.VMEM((PLANES, VROWS, D), f32),
+            pltpu.VMEM((4, TILE, D), bf),
+            pltpu.VMEM((MOST_TILES, CHIPS, PROJ, D), bf),
+            pltpu.VMEM((MOST_TILES, TILE, D), f32),
+            pltpu.VMEM((PLANES, STRIP, PACKED), f32),
+            pltpu.VMEM((PLANES, STRIP, PACKED), f32),
+            pltpu.VMEM((PLANES, STRIP, PACKED), f32),
+            dma((8,)),
+            dma((2, MOST_TILES)),
+            dma((2,)),
+            dma((20,)),
+            dma((20,)),
+            dma((15,)),
+            dma((15,)),
+            dma((6,)),
+            dma((6,)),
+            dma((8,)),
+            dma((8,)),
+            dma((6,)),
+            dma((6,)),
             dma((len(SHARES),)),
             dma((len(SHARES) * 9,)),
             dma((len(SHARES) * 9,)),
+            dma((PLANES * CHIPS * CORES - 1,)),
+            dma((PLANES * CHIPS * CORES - 1,)),
         ],
         compiler_params=pltpu.CompilerParams(
-            collective_id=4, has_side_effects=True, vmem_limit_bytes=60 * 2**20
+            collective_id=3, has_side_effects=True, vmem_limit_bytes=58 * 2**20
         ),
-        name="muon_rows",
-    )(gram, high, low)
+        name="settle",
+    )(
+        every,
+        part,
+        vec,
+        grad_own,
+        proj_own,
+        bias_own,
+        momentum,
+        text_ids,
+        text_mask,
+        outgoing,
+    )
 
 
 def finish_kernel(main_ref, proj_ref, rows_ref, momentum_ref, master_ref, ema_ref, *outs):
@@ -1463,7 +1334,7 @@
         cost_estimate=pl.CostEstimate(
             flops=12 * master.size, bytes_accessed=32 * master.size, transcendentals=0
         ),
-        compiler_params=pltpu.CompilerParams(vmem_limit_bytes=32 * 2**20),
+        compiler_params=pltpu.CompilerParams(vmem_limit_bytes=62 * 2**20),
         name="finish",
     )(main_sum, proj, rows, momentum, master, ema)
 
@@ -1600,13 +1471,14 @@
     cot_ref,
     live_ref,
     param_ref,
-    z_ref,
-    main_ref,
+    every_ref,
+    part_ref,
     outgoing_ref,
     vec_ref,
     own_grad_ref,
     own_proj_ref,
     rows_ref,
+    main_ref,
     own_rows,
     every_ids,
     spots_ref,
@@ -1615,6 +1487,7 @@
     incoming_ref,
     proj_rows,
     proj_stage,
+    z_ref,
     packed,
     text_total,
     onehot,
@@ -1647,10 +1520,25 @@
     piece_recv,
     near_send,
     near_recv,
+    main_near,
+    main_x_first,
+    main_y_first,
+    main_x_second,
+    main_y_second,
+    main_second,
+    main_deep,
+    main_far_send,
+    main_far_recv,
+    main_deep_send,
+    main_deep_recv,
+    main_send,
+    main_recv,
     body_send,
     body_recv,
     proj_send,
     proj_recv,
+    z_send,
+    z_recv,
 ):
     at = place()
     wide_at, plane, chip, core = at
@@ -1667,6 +1555,9 @@
     sibling, _, planes = neighbours(*at)
     body_begin, body_arrive, body_relay, body_finish, body_settled = spread_steps(
         packed.at[plane, wide_at], packed, (body_send, body_recv), 0, at
+    )
+    z_begin, z_arrive, z_relay, z_finish, z_settled = spread_steps(
+        z_ref, every_ref, (z_send, z_recv), 0, at
     )
     holds_proj = plane == chip
     proj_sems = (proj_send, proj_recv)
@@ -1701,12 +1592,14 @@
         begin = begin + size
         block = block + height
     enter(peers)
+    every_ids[me] = jnp.concatenate(
+        [pieces_ref[...], jnp.zeros((SLOTS - PSLOTS, entries), jnp.int32)], axis=0
+    )
     tell_copies = []
     for index, target in enumerate(peers):
-        copy = remote(pieces_ref, every_ids.at[me], (tell_send, tell_recv), index, target)
+        copy = remote(every_ids.at[me], every_ids.at[me], (tell_send, tell_recv), index, target)
         copy.start()
         tell_copies.append(copy)
-    every_ids[me] = pieces_ref[...]
     for copy in loads:
         copy.wait()
     packed[plane, wide_at] = own_rows[...].astype(jnp.bfloat16)
@@ -1747,6 +1640,27 @@
         (far_send, far_recv),
         (deep_send, deep_recv),
     )
+
+    main_copies = {}
+    main_first, main_then, main_last, main_total, main_settled = plane_sums(
+        main_ref.at[core],
+        main_copies,
+        main_near,
+        (main_x_first, main_y_first, main_x_second, main_y_second, main_second, main_deep),
+        (main_far_send, main_far_recv),
+        (main_deep_send, main_deep_recv),
+    )
+
+    def main_begin(chunk):
+        copy = remote(
+            main_ref.at[1 - core, chunk],
+            main_near.at[chunk],
+            (main_send, main_recv),
+            chunk,
+            sibling,
+        )
+        copy.start()
+        main_copies[chunk] = copy
 
     def dz_begin():
         @pl.when(jnp.logical_not(holds_proj))
@@ -1948,11 +1862,14 @@
     for begin in range(0, wholes, tall):
         rows = slice(begin, begin + tall)
         probs[rows, :] = two_part_dot(grad_normed[rows, :], to_heads) * root
+    live = jnp.concatenate(
+        [live_ref[...].astype(jnp.float32), jnp.zeros((1, entries), jnp.float32)], axis=0
+    ).T
     scores = []
     for slot in range(SLOTS):
         value = probs[slot * entries : (slot + 1) * entries, :]
         if slot > 0:
-            value = jnp.where(live_ref[:, slot - 1 : slot] > 0, value, -1e30)
+            value = jnp.where(live[:, slot - 1 : slot] > 0, value, -1e30)
         scores.append(value)
     top = scores[0]
     for value in scores[1:]:
@@ -1991,6 +1908,10 @@
     hat_end, scale_end = normalize(second)
     z_ref[...] = (hat_end * gain_end + shift_end).astype(jnp.bfloat16)
 
+    z_begin()
+    own_z = pltpu.make_async_copy(z_ref, every_ref.at[plane, wide_at], local_sem.at[5])
+    own_z.start()
+    z_arrive(1)
     grad_z = jnp.concatenate([dz_total(part) for part in range(entries // CHUNK)], axis=0)
     for copy in near_copies:
         copy.wait_send()
@@ -2022,6 +1943,8 @@
                     top : top + height, :
                 ].astype(jnp.bfloat16)
 
+    z_relay(0)
+    z_arrive(2)
     grad_two = jnp.zeros((entries, D), jnp.float32)
     for block in range(PLANES):
         lanes = slice(block * span, (block + 1) * span)
@@ -2030,6 +1953,10 @@
         vec_ref[15 + block : 16 + block, :] = over_rows(gate_grad.astype(jnp.float32))
         store(dot_tn(gate_grad, normed_two), block, 1, 64, 0)
         grad_two = grad_two + plain_dot(gate_grad, weight_rows(up_at, 64, block))
+    main_begin(0)
+    main_begin(1)
+    z_relay(1)
+    z_arrive(3)
     vec_ref[11:12, :] = over_rows(grad_two * hat_two)
     vec_ref[12:13, :] = over_rows(grad_two)
     grad_residual = grad_second + normalize_back(grad_two, gain_two, hat_two, scale_two)
@@ -2038,6 +1965,10 @@
     for block in range(PLANES):
         store(grad_out[block * 128 : (block + 1) * 128, :], block, 2, 16, 0)
     grad_attended = plain_dot(branch_one, weight_rows(out_at, 16))
+    main_first(0)
+    main_first(1)
+    z_finish(0)
+    z_relay(2)
     halves_of = entries // CHUNK
 
     def store_kv(kind, slot, value):
@@ -2071,6 +2002,8 @@
         push = grad_normed[rows, :]
         grad_query = grad_query + push * keys[rows, 0:D]
         store_kv(0, slot, push * query)
+    z_finish(1)
+    z_relay(3)
     query_bf = grad_query.astype(jnp.bfloat16)
 
     grad_q = dot_tn(query_bf, normed[0:entries, :])
@@ -2083,6 +2016,8 @@
     for block in range(PLANES):
         store(every[block * third : (block + 1) * third, :], block, 2, 48, 16)
 
+    main_begin(2)
+    main_then(0)
     for begin in range(0, wholes, tall):
         rows = slice(begin, begin + tall)
         grad_normed[rows, :] = plain_dot(
@@ -2107,6 +2042,10 @@
                 grad_x.astype(jnp.bfloat16)
             )
 
+    main_first(2)
+    z_finish(2)
+    z_finish(3)
+    main_then(1)
     vec_ref[9:11, :] = sums[0:2, :]
     vec_ref[1:2, :] += over_rows(grad_residual)
     vec_ref[0:1, :] = vec_ref[1:2, :]
@@ -2115,13 +2054,24 @@
         outgoing_ref[begin : begin + tile, :] = plain_dot(
             onehot[begin : begin + tile, :], grad_pieces[...]
         ).astype(jnp.bfloat16)
+    main_last(0)
+    main_then(2)
+    main_last(1)
+    main_last(2)
+    for chunk in range(CHUNKS):
+        part_ref[chunk * CHUNK : (chunk + 1) * CHUNK, :] = main_total(chunk).astype(jnp.bfloat16)
+    own_z.wait()
+    z_settled()
+    main_settled()
+    for chunk in range(CHUNKS):
+        main_copies[chunk].wait_send()
 
 
 def layer(master, pieces, table, text_ids, text_mask, text_cot, slot_mask, params, cap):
     f32, bf = jnp.float32, jnp.bfloat16
     dma = pltpu.SemaphoreType.DMA
     count = PLANES * CHIPS * CORES
-    entries = slot_mask.shape[0]
+    entries = slot_mask.shape[1]
     features = text_cot.shape[0]
     rows = entries * SLOTS
     hbm = pl.BlockSpec(memory_space=pl.ANY)
@@ -2130,8 +2080,8 @@
     return pl.pallas_call(
         layer_kernel,
         out_shape=(
-            jax.ShapeDtypeStruct((entries, D), bf),
-            jax.ShapeDtypeStruct((CORES, CHUNKS, SIDE, SIDE, PLANES, CHUNK, D), bf),
+            jax.ShapeDtypeStruct((PLANES, CHIPS * CORES, entries, D), bf),
+            jax.ShapeDtypeStruct((MAIN, D), bf),
             jax.ShapeDtypeStruct((count * cap, D), bf),
             jax.ShapeDtypeStruct((CORES * VROWS, D), f32),
             jax.ShapeDtypeStruct((count, entries, features), bf),
@@ -2139,16 +2089,18 @@
             jax.ShapeDtypeStruct((count * cap, 1), jnp.int32),
         ),
         in_specs=[hbm] + [vmem] * 7,
-        out_specs=(vmem,) * 7,
+        out_specs=(hbm,) + (vmem,) * 6,
         scratch_shapes=[
+            pltpu.VMEM((CORES, CHUNKS, SIDE, SIDE, PLANES, CHUNK, D), bf),
             pltpu.VMEM((MAIN, D), f32),
-            pltpu.VMEM((count,) + pieces.shape, jnp.int32),
+            pltpu.VMEM((count, SLOTS, entries), jnp.int32),
             pltpu.VMEM((SLOTS, entries), jnp.int32),
             pltpu.VMEM((count, entries * PSLOTS), f32),
             pltpu.VMEM((count, entries * PSLOTS), f32),
             pltpu.VMEM((count * cap, D), bf),
             pltpu.VMEM((PLANES * features, D), f32),
             pltpu.VMEM((PLANES, features, D), bf),
+            pltpu.VMEM((entries, D), bf),
             pltpu.VMEM((PLANES, CHIPS * CORES, MAIN, D), bf),
             pltpu.VMEM((count * entries // BANDS, BANDS * features), f32),
             pltpu.VMEM((count * cap, entries * PSLOTS), bf),
@@ -2164,13 +2116,17 @@
             pltpu.VMEM((entries, FF), f32),
             pltpu.VMEM((rows, 128), f32),
             pltpu.VMEM((8, D), f32),
-            dma((5,)),
+            dma((6,)),
         ]
         + sum_scratch(entries // CHUNK)
         + [dma((count - 1,))] * 4
         + [dma((entries // CHUNK,))] * 2
+        + [pltpu.VMEM((CHUNKS, SIDE, SIDE, PLANES, CHUNK, D), bf)]
+        + sum_scratch(CHUNKS)
+        + [dma((CHUNKS,))] * 2
         + [dma((spread_count,))] * 2
-        + [dma((PLANES - 1,))] * 2,
+        + [dma((PLANES - 1,))] * 2
+        + [dma((spread_count,))] * 2,
         compiler_params=pltpu.CompilerParams(
             collective_id=5, has_side_effects=True, vmem_limit_bytes=63 * 2**20
         ),
@@ -2216,30 +2172,29 @@
     vec_moment2,
     vec_ema,
 ):
-    device_count = PLANES * CHIPS * CORES
     me = lax.axis_index("wide") * PLANES + lax.axis_index("narrow")
     entries = piece_ids.shape[0]
     group_rows = piece_table.shape[0]
     cap = piece_cap(group_rows)
     feature_rows = text_cot.shape[0]
     params = vec_master.reshape(-1, D)
-    pieces = jnp.pad(piece_ids.T, ((0, SLOTS - PSLOTS), (0, 0)))
+    pieces = piece_ids.T
     (
-        z_own,
-        main,
+        every,
+        part,
         grad_outgoing,
         vec_rows,
         grad_own,
         proj_own,
         asked_rows,
     ) = layer(
-        mat_master[0], pieces, piece_table, text_ids, text_mask, text_cot, slot_mask, params, cap
+        mat_master[0], pieces, piece_table, text_ids, text_mask, text_cot, slot_mask.T, params, cap
     )
     bias_out = vec_master[vec_master.shape[0] - OUTW :]
     bias_own = lax.dynamic_slice_in_dim(bias_out, me * feature_rows, feature_rows, 0)
-    text_embeds, main_sum, proj_sum, vec_sum, gram, high, low = settle(
-        z_own,
-        main,
+    text_embeds, main_sum, proj_sum, vec_sum, rows, grad_incoming = settle(
+        every,
+        part,
         vec_rows.reshape(CORES, VROWS, D),
         grad_own,
         proj_own,
@@ -2247,13 +2202,9 @@
         mat_momentum[0],
         text_ids,
         text_mask,
+        grad_outgoing,
     )
     vec_grad = vec_sum.reshape(-1)[: vec_master.shape[0]]
-    grad_outgoing, _ = lax.optimization_barrier((grad_outgoing, gram))
-    grad_incoming = lax.all_to_all(
-        grad_outgoing.reshape(device_count, cap, D), BOTH, 0, 0, tiled=True
-    ).reshape(device_count * cap, D)
-    rows = muon_rows(gram, high, low)
     grad_block, momentum_block, weight_block, ema_block = finish(
         main_sum, proj_sum, rows, mat_momentum, mat_master, mat_ema
     )

time: 325 us -> 311 us (0.957)
  local copies, waits for them, and re-layouts: 18.4 us -> 8.52 us
  starting transfers between devices: 6.5 us -> 0 us
  Pallas kernels: 291 us -> 296 us
    pallas_call x1, Pallas kernels: 7.58 us -> 16.4 us  [finish(): pl.pallas_call(finish_kernel, grid=((MAIN_TILES + MOST_TILES) // tall,),...]
    pallas_call x1, Pallas kernels: 121 us -> 113 us  [settle(): pl.pallas_call(settle_kernel, out_shape=(jax.ShapeDtypeStruct((features,...]
    unnamed x27 -> x16, local copies, waits for them, and re-layouts: 14.1 us -> 6.24 us
    all_to_all x1 -> x0, starting transfers between devices: 6.5 us -> none  [on_device(): lax.all_to_all(grad_outgoing.reshape(device_count, cap, D), BOTH, 0, 0, t...]
    pallas_call x2 -> x1, Pallas kernels: 158 us -> 163 us  [layer(): pl.pallas_call(layer_kernel, out_shape=(jax.ShapeDtypeStruct((PLANES, CHI...]
  transfers between devices with their start and end apart: 1 -> 0, of which waited for: 0 -> 0; matrix products, arithmetic and copies ran while one was open for 1% -> 0% of each run, Pallas kernels for 17% -> 0%
where the time goes in v6:
time: 311 us; the launch traced here: 307 us
  Pallas kernels  296 us (95%)
  local copies, waits for them, and re-layouts  8.52 us (3%)
    pallas_call x1, Pallas kernels, layer(): pl.pallas_call(layer_kernel, out_shape=(jax.ShapeDtypeStruct((PLANES, CHI...  163 us
    pallas_call x1, Pallas kernels, settle(): pl.pallas_call(settle_kernel, out_shape=(jax.ShapeDtypeStruct((features,...  113 us
    pallas_call x1, Pallas kernels, finish(): pl.pallas_call(finish_kernel, grid=((MAIN_TILES + MOST_TILES) // tall,),...  16.4 us
    unnamed x16, local copies, waits for them, and re-layouts  6.24 us

profile of v6, /device:TPU:31, one launch (start us, length us, event | category | flops | bytes accessed | tf_op | source)
XLA Modules:
  0.0 306.7 jit_solution(14626039125173047168)
XLA Ops:
  0.6 1.5 reshape.37.param_ref
  2.1 0.0 slice-start
  2.1 163.1 %layer.1 = (bf16[4,8,128,512]{3,2,1,0:T(8,128)(2,1)}, bf16[192,512]{1,0:T(8,128)(2,1)}, bf16[2048,512]{1,0:T(8,128)(2,1)}, f32[32,512]{1,0:T(8,128)}, bf16[32,12...) custom-call(f32[2560,512]{1,0:T(8,128)} %bitcast.13, s32[7,128]{1,0:T(8,128)} %bitcast.18, ...), custom_call_target="tpu_custom_call" | custom-call | tf_op jit(solution)/shard_map/layer/pallas_call | solution.py:2080
  165.2 0.0 slice-done
  165.2 0.1 dynamic-slice_bitcast_fusion
  165.3 0.7 copy.25.bias_ref
  166.1 0.0 copy-start.1
  166.1 112.9 %settle.1 = (f32[128,8192]{1,0:T(8,128)}, bf16[1536,512]{1,0:T(8,128)(2,1)}, bf16[2,4,4,32,512]{4,3,2,1,0:T(8,128)(2,1)}, f32[2,16,512]{2,1,0:T(8,128)}, bf16[25...) custom-call(bf16[4,8,128,512]{3,2,1,0:T(8,128)(2,1)} %get-tuple-element.28.every, bf16[192,512]{1,0:T(8,128)(2,1)} %get-tuple-element.29.part, ...), custom_call_target="tpu_custom_call" | custom-call | tf_op jit(solution)/shard_map/settle/pallas_call | solution.py:1218
  279.0 0.0 copy-done.1
  279.0 0.3 reduce
  279.3 0.0 copy-start
  279.3 1.6 copy-done
  280.9 3.7 %add_piece_grads.1 = f32[1024,512]{1,0:T(8,128)} custom-call(s32[1,2048]{1,0:T(1,128)S(1)} %bitcast.11, bf16[2048,512]{1,0:T(8,128)(2,1)S(1)} %copy-done), custom_call_target="tpu_custom_call" | custom-call | tf_op jit(solution)/shard_map/add_piece_grads/pallas_call | solution.py:2146
  284.6 0.0 copy-start.3
  284.6 0.0 copy-start.2
  284.6 0.0 copy-start.6
  284.7 16.4 %finish.1 = (f32[1,2560,512]{2,1,0:T(8,128)}, f32[1,2560,512]{2,1,0:T(8,128)}, f32[1,2560,512]{2,1,0:T(8,128)}, f32[1,2560,512]{2,1,0:T(8,128)}) custom-call(bf16[1536,512]{1,0:T(8,128)(2,1)} %get-tuple-element.37.main_ref, bf16[8,4,32,512]{3,2,1,0:T(8,128)(2,1)} %bitcast.14, bf16[2560,512]{1,0:T(8,128)(2,1)} %get-tuple-element.39.rows_ref, ...), custom_call_target="tpu_custom_call" | custom-call | flops 15728640 | bytes 41943040 | tf_op jit(solution)/shard_map/finish/pallas_call | solution.py:1319
  301.1 0.0 copy-done.3
  301.1 0.0 copy-done.2
  301.1 0.0 copy-done.4
  301.1 0.0 copy-done.5
  301.1 0.0 copy-done.6
  301.1 0.7 multiply_add_fusion
  301.8 4.6 %copy.28 = f32[128,8192]{1,0:T(8,128)} copy(f32[128,8192]{1,0:T(8,128)} %get-tuple-element.61) | data formatting | bytes 8388608
  (3 shorter events, 0.0 us)
Async XLA Ops:
  2.1 163.1 %slice-start = ((f32[14336]{0:T(1024)}), f32[4096]{0:T(1024)S(1)}, s32[]{:S(2)}) async-start(f32[14336]{0:T(1024)} %param.22), calls=%async_computation | async-start | bytes 32768 | tf_op jit(solution)/shard_map/slice | solution.py:2193
  166.1 112.9 %copy-start.1 = (s32[2048,1]{1,0:T(8,128)S(1)}, s32[2048,1]{1,0:T(8,128)}, u32[]{:S(2)}) copy-start(s32[2048,1]{1,0:T(8,128)} %get-tuple-element.35) | copy-start | bytes 24580
  279.3 1.6 copy-start
  284.6 16.4 %copy-start.3 = (f32[2,16,512]{2,1,0:T(8,128)S(1)}, f32[2,16,512]{2,1,0:T(8,128)}, u32[]{:S(2)}) copy-start(f32[2,16,512]{2,1,0:T(8,128)} %get-tuple-element.44) | copy-start | bytes 196612
  284.6 16.5 %copy-start.2 = (f32[14336]{0:T(1024)S(1)}, f32[14336]{0:T(1024)}, u32[]{:S(2)}) copy-start(f32[14336]{0:T(1024)} %param.22) | copy-start | bytes 172036
  284.6 16.5 %copy-start.4 = (f32[14336]{0:T(1024)S(1)}, f32[14336]{0:T(1024)}, u32[]{:S(2)}) copy-start(f32[14336]{0:T(1024)} %param.25) | copy-start | bytes 172036
  284.6 16.5 %copy-start.5 = (f32[14336]{0:T(1024)S(1)}, f32[14336]{0:T(1024)}, u32[]{:S(2)}) copy-start(f32[14336]{0:T(1024)} %param.24) | copy-start | bytes 172036
  284.6 16.5 %copy-start.6 = (f32[14336]{0:T(1024)S(1)}, f32[14336]{0:T(1024)}, u32[]{:S(2)}) copy-start(f32[14336]{0:T(1024)} %param.23) | copy-start | bytes 172036

commit v7 on v6

--- a/solution.py
+++ b/solution.py
@@ -1078,26 +1078,26 @@
     publish_step(0)
     publish_step(1)
     vec_far_step()
+    proj_far_step()
     pass_step(2)
     pass_step(3)
-    proj_far_step()
+    publish_proj()
     pass_step(0)
     pass_step(1)
+    settle_piece(2)
+    settle_piece(3)
+    gram_early_step()
+    pass_step(4)
+    settle_piece(0)
+    settle_piece(1)
+    settle_piece(4)
+    gram_late_step()
     vec_deep_step()
     table_step()
-    settle_piece(2)
-    settle_piece(3)
-    publish_proj()
-    gram_early_step()
+    text_steps(0, 5)
+    gram_total_step(tile_count > 0)
     vec_last_step()
-    settle_piece(0)
-    settle_piece(1)
-    pass_step(4)
-    settle_piece(4)
-    gram_late_step()
-    text_steps(0, text_count // 2)
-    gram_total_step(tile_count > 0)
-    text_steps(text_count // 2, text_count)
+    text_steps(5, text_count)
     gram_whole_step()
     send_pieces(0, len(peers))
     @pl.when(tile_count > 0)
@@ -1311,7 +1311,7 @@
 
 
 def finish(main_sum, proj_sum, rows, momentum, master, ema):
-    height = 2 * TILE
+    height = 4 * TILE
     tall = height // TILE
     main_steps = MAIN_TILES // tall
     block = pl.BlockSpec((1, height, D), lambda i: (0, i, 0))

time: 311 us -> 309 us (level)
  no operation moved by 1% of the time
where the time goes in v7:
time: 309 us; the launch traced here: 304 us
  Pallas kernels  294 us (95%)
  local copies, waits for them, and re-layouts  8.52 us (3%)
    pallas_call x1, Pallas kernels, layer(): pl.pallas_call(layer_kernel, out_shape=(jax.ShapeDtypeStruct((PLANES, CHI...  163 us
    pallas_call x1, Pallas kernels, settle(): pl.pallas_call(settle_kernel, out_shape=(jax.ShapeDtypeStruct((features,...  112 us
    pallas_call x1, Pallas kernels, finish(): pl.pallas_call(finish_kernel, grid=((MAIN_TILES + MOST_TILES) // tall,),...  15.4 us
    unnamed x16, local copies, waits for them, and re-layouts  6.24 us

profile of v7, /device:TPU:31, one launch (start us, length us, event | category | flops | bytes accessed | tf_op | source)
XLA Modules:
  0.0 304.5 jit_solution(13157727928869859604)
XLA Ops:
  0.6 1.5 reshape.37.param_ref
  2.1 0.0 slice-start
  2.1 163.1 %layer.1 = (bf16[4,8,128,512]{3,2,1,0:T(8,128)(2,1)}, bf16[192,512]{1,0:T(8,128)(2,1)}, bf16[2048,512]{1,0:T(8,128)(2,1)}, f32[32,512]{1,0:T(8,128)}, bf16[32,12...) custom-call(f32[2560,512]{1,0:T(8,128)} %bitcast.13, s32[7,128]{1,0:T(8,128)} %bitcast.18, ...), custom_call_target="tpu_custom_call" | custom-call | tf_op jit(solution)/shard_map/layer/pallas_call | solution.py:2080
  165.2 0.0 slice-done
  165.2 0.1 dynamic-slice_bitcast_fusion
  165.3 0.7 copy.25.bias_ref
  166.0 0.0 copy-start.1
  166.1 111.7 %settle.1 = (f32[128,8192]{1,0:T(8,128)}, bf16[1536,512]{1,0:T(8,128)(2,1)}, bf16[2,4,4,32,512]{4,3,2,1,0:T(8,128)(2,1)}, f32[2,16,512]{2,1,0:T(8,128)}, bf16[25...) custom-call(bf16[4,8,128,512]{3,2,1,0:T(8,128)(2,1)} %get-tuple-element.28.every, bf16[192,512]{1,0:T(8,128)(2,1)} %get-tuple-element.29.part, ...), custom_call_target="tpu_custom_call" | custom-call | tf_op jit(solution)/shard_map/settle/pallas_call | solution.py:1218
  277.7 0.0 copy-done.1
  277.7 0.3 reduce
  278.1 0.0 copy-start
  278.1 1.6 copy-done
  279.7 3.7 %add_piece_grads.1 = f32[1024,512]{1,0:T(8,128)} custom-call(s32[1,2048]{1,0:T(1,128)S(1)} %bitcast.11, bf16[2048,512]{1,0:T(8,128)(2,1)S(1)} %copy-done), custom_call_target="tpu_custom_call" | custom-call | tf_op jit(solution)/shard_map/add_piece_grads/pallas_call | solution.py:2146
  283.4 0.0 copy-start.3
  283.4 0.0 copy-start.2
  283.4 0.0 copy-start.6
  283.4 15.4 %finish.1 = (f32[1,2560,512]{2,1,0:T(8,128)}, f32[1,2560,512]{2,1,0:T(8,128)}, f32[1,2560,512]{2,1,0:T(8,128)}, f32[1,2560,512]{2,1,0:T(8,128)}) custom-call(bf16[1536,512]{1,0:T(8,128)(2,1)} %get-tuple-element.37.main_ref, bf16[8,4,32,512]{3,2,1,0:T(8,128)(2,1)} %bitcast.14, bf16[2560,512]{1,0:T(8,128)(2,1)} %get-tuple-element.39.rows_ref, ...), custom_call_target="tpu_custom_call" | custom-call | flops 15728640 | bytes 41943040 | tf_op jit(solution)/shard_map/finish/pallas_call | solution.py:1319
  298.8 0.0 copy-done.3
  298.9 0.0 copy-done.2
  298.9 0.0 copy-done.4
  298.9 0.0 copy-done.5
  298.9 0.0 copy-done.6
  298.9 0.7 multiply_add_fusion
  299.6 4.6 %copy.28 = f32[128,8192]{1,0:T(8,128)} copy(f32[128,8192]{1,0:T(8,128)} %get-tuple-element.61) | data formatting | bytes 8388608
  (3 shorter events, 0.0 us)
Async XLA Ops:
  2.1 163.1 %slice-start = ((f32[14336]{0:T(1024)}), f32[4096]{0:T(1024)S(1)}, s32[]{:S(2)}) async-start(f32[14336]{0:T(1024)} %param.22), calls=%async_computation | async-start | bytes 32768 | tf_op jit(solution)/shard_map/slice | solution.py:2193
  166.0 111.7 %copy-start.1 = (s32[2048,1]{1,0:T(8,128)S(1)}, s32[2048,1]{1,0:T(8,128)}, u32[]{:S(2)}) copy-start(s32[2048,1]{1,0:T(8,128)} %get-tuple-element.35) | copy-start | bytes 24580
  278.1 1.6 copy-start
  283.4 15.5 %copy-start.3 = (f32[2,16,512]{2,1,0:T(8,128)S(1)}, f32[2,16,512]{2,1,0:T(8,128)}, u32[]{:S(2)}) copy-start(f32[2,16,512]{2,1,0:T(8,128)} %get-tuple-element.44) | copy-start | bytes 196612
  283.4 15.5 %copy-start.2 = (f32[14336]{0:T(1024)S(1)}, f32[14336]{0:T(1024)}, u32[]{:S(2)}) copy-start(f32[14336]{0:T(1024)} %param.22) | copy-start | bytes 172036
  283.4 15.5 %copy-start.4 = (f32[14336]{0:T(1024)S(1)}, f32[14336]{0:T(1024)}, u32[]{:S(2)}) copy-start(f32[14336]{0:T(1024)} %param.25) | copy-start | bytes 172036
  283.4 15.5 %copy-start.5 = (f32[14336]{0:T(1024)S(1)}, f32[14336]{0:T(1024)}, u32[]{:S(2)}) copy-start(f32[14336]{0:T(1024)} %param.24) | copy-start | bytes 172036
  283.4 15.5 %copy-start.6 = (f32[14336]{0:T(1024)S(1)}, f32[14336]{0:T(1024)}, u32[]{:S(2)}) copy-start(f32[14336]{0:T(1024)} %param.23) | copy-start | bytes 172036
